TPU v7x, 128 devices: a whole 4x4x4 slice. The times are simulated.
128 devices in a mesh: ctx: 16 (over z, y), ep: 8 (over x, core).
Axes of the slice: x: 4, y: 4, z: 4, core: 2. Of those that a mesh axis runs over, the one named last changes fastest.
Arguments:
- queries: bfloat16 [256, 2, 128, 576], P('ep'), may hold values from -440 to 440
- prompt_latent: bfloat16 [32768, 576], P('ctx'), may hold values from -6.1 to 6.1
- new_latent: bfloat16 [256, 2, 576], P('ep'), may hold values from -6 to 6
- blocks: int32 [256, 32], P('ep'), may hold values from 0 to 511, as said below
- value_up: bfloat16 [128, 512, 128], P(('ctx', 'ep')), may hold values from -0.75 to 0.75
- w_out: bfloat16 [16384, 7168], P(('ctx', 'ep')), may hold values from -0.1875 to 0.1875
- residual: bfloat16 [512, 7168], P(('ctx', 'ep')), may hold values from -1.5 to 1.5
- norm_gain: float32 [7168], replicated, may hold values from 0.1 to 1.9
- router: bfloat16 [7168, 16], replicated, may hold values from -0.0625 to 0.0625
- routes: int32 [512, 8], P(('ctx', 'ep')), may hold values from 0 to 15, as said below
- bucket_slots: int32 [512, 8], P(('ctx', 'ep')), may hold values from 0 to 3, as said below
- w_gate: bfloat16 [16, 7168, 2048], P('ctx', None, 'ep'), may hold values from -0.0625 to 0.0625
- w_up: bfloat16 [16, 7168, 2048], P('ctx', None, 'ep'), may hold values from -0.0625 to 0.0625
- w_down: bfloat16 [16, 2048, 7168], P('ctx', 'ep'), may hold values from -0.25 to 0.25
Outputs:
- layer_out: bfloat16 [512, 7168], P(('ctx', 'ep'))
Inputs may be any that keep to these rules, and one draw needn't show every extreme that they name: A sample's 32 blocks are distinct. Counting blocks by shard (the 32 consecutive blocks of one index of ctx), each sample has exactly 8 in one shard drawn from the seed, and its other 24 blocks are spread over the other shards as evenly as possible. `routes`: each row names 8 distinct experts; in each aligned block of 4 rows (the rows of one device) some expert is named by every row. `bucket_slots`: within the 4 rows of one device, the rows naming one expert hold the slots 0, 1, 2 and so on for that expert, in an order of the rows drawn from the seed and common to all experts of that device.
All inputs are finite; a program needn't handle non-finite values.
Results may differ from a plain program's by a relative error of at most 0.023.
Values may be sent and summed in bfloat16 or wider, within the bound.
No kernel may reach another device: no remote copies, remote signals or barrier semaphores. Data moves between devices by JAX's collectives and lax.ppermute only.
A program may use at most 192 MiB of HBM per device.

v0:
```python
import jax
import jax.numpy as jnp
from jax import lax
from jax.sharding import PartitionSpec as P

BLOCK = 64
CAPB = 8
CAP = 2


score_scale = 192.0 ** (-0.5)
masked_score = -1e30


def merge_partials(weighted, row_max, row_total, groups):
    weighted = weighted.reshape((groups, -1) + weighted.shape[1:])
    row_max = row_max.reshape((groups, -1) + row_max.shape[1:])
    row_total = row_total.reshape((groups, -1) + row_total.shape[1:])
    overall = jnp.max(row_max, axis=0)
    factor = jnp.exp(row_max - overall[None])
    summed = jnp.sum(factor[..., None] * weighted, axis=0)
    denominator = jnp.sum(factor * row_total, axis=0)
    return (summed / denominator[..., None]).astype(jnp.bfloat16)


def expert_work(arrived, w_gate, w_up, w_down):
    sources, experts_here, slot_count, model_width = arrived.shape
    flat_rows = arrived[:, 0].reshape(sources * slot_count, model_width)
    gate_act = jnp.dot(flat_rows, w_gate[0], preferred_element_type=jnp.float32)
    up_act = jnp.dot(flat_rows, w_up[0], preferred_element_type=jnp.float32)
    inner_act = (jax.nn.silu(gate_act) * up_act).astype(jnp.bfloat16)
    partial_out = jnp.dot(inner_act, w_down[0], preferred_element_type=jnp.float32)
    results = [partial_out.reshape(sources, slot_count, model_width)]
    return jnp.stack(results, axis=1)


def per_device(
    queries,
    prompt_latent,
    new_latent,
    blocks,
    value_up,
    w_out,
    residual,
    norm_gain,
    router,
    routes,
    bucket_slots,
    w_gate,
    w_up,
    w_down,
):
    n_ctx = lax.axis_size("ctx")
    n_ep = lax.axis_size("ep")
    devices = n_ctx * n_ep
    ctx_place = lax.axis_index("ctx")
    samples, step_count, head_count, latent = queries.shape
    rank_width = value_up.shape[1]
    blk_local = prompt_latent.shape[0] // BLOCK
    shard_of = blocks // blk_local
    offset = blocks % blk_local
    is_local = (shard_of == ctx_place).astype(jnp.int32)
    position = jnp.cumsum(is_local, axis=1) - 1
    chosen = (is_local[:, :, None] == 1) & (position[:, :, None] == jnp.arange(CAPB)[None, None, :])
    block_table = jnp.sum(jnp.where(chosen, offset[:, :, None], 0), axis=1)
    filled = jnp.any(chosen, axis=1)
    key_rows = (block_table[:, :, None] * BLOCK + jnp.arange(BLOCK)[None, None, :]).reshape(-1)
    gathered = jnp.take(prompt_latent, key_rows, axis=0).reshape(samples, CAPB * BLOCK, latent)
    key_live = jnp.repeat(filled, BLOCK, axis=1)
    flat_query = queries.reshape(samples, step_count * head_count, latent)
    scores = (
        jnp.einsum("sqd,skd->sqk", flat_query, gathered, preferred_element_type=jnp.float32)
        * score_scale
    )
    scores = jnp.where(key_live[:, None, :], scores, masked_score)
    own_scores = (
        jnp.einsum("sqd,skd->sqk", flat_query, new_latent, preferred_element_type=jnp.float32)
        * score_scale
    )
    query_step = jnp.arange(step_count * head_count) // head_count
    own_live = (jnp.arange(step_count)[None, :] <= query_step[:, None]) & (ctx_place == n_ctx - 1)
    own_scores = jnp.where(own_live[None], own_scores, masked_score)
    row_max = jnp.maximum(jnp.max(scores, axis=2), jnp.max(own_scores, axis=2))
    key_weight = jnp.where(key_live[:, None, :], jnp.exp(scores - row_max[..., None]), 0.0)
    own_weight = jnp.where(own_live[None], jnp.exp(own_scores - row_max[..., None]), 0.0)
    row_total = jnp.sum(key_weight, axis=2) + jnp.sum(own_weight, axis=2)
    weighted = jnp.einsum(
        "sqk,skr->sqr",
        key_weight.astype(jnp.bfloat16),
        gathered[:, :, :rank_width],
        preferred_element_type=jnp.float32,
    )
    weighted = weighted + jnp.einsum(
        "sqk,skr->sqr",
        own_weight.astype(jnp.bfloat16),
        new_latent[:, :, :rank_width],
        preferred_element_type=jnp.float32,
    )
    weighted = weighted.reshape(samples, step_count, head_count, rank_width)
    row_max = row_max.reshape(samples, step_count, head_count)
    row_total = row_total.reshape(samples, step_count, head_count)
    part_acc, part_max, part_total = (
        lax.all_to_all(weighted, ("ctx", "ep"), split_axis=2, concat_axis=0, tiled=True),
        lax.all_to_all(row_max, ("ctx", "ep"), split_axis=2, concat_axis=0, tiled=True),
        lax.all_to_all(row_total, ("ctx", "ep"), split_axis=2, concat_axis=0, tiled=True),
    )
    latent_out = merge_partials(part_acc, part_max, part_total, n_ctx)
    head_values = jnp.einsum(
        "sthr,hrv->sthv", latent_out, value_up, preferred_element_type=jnp.float32
    ).astype(jnp.bfloat16)
    total_samples = head_values.shape[0]
    head_flat = head_values.reshape(total_samples * step_count, -1)
    attention = lax.psum_scatter(
        jnp.dot(head_flat, w_out, preferred_element_type=jnp.float32),
        ("ctx", "ep"),
        scatter_dimension=0,
        tiled=True,
    )
    hidden_state = (residual.astype(jnp.float32) + attention).astype(jnp.bfloat16)
    hidden_wide = hidden_state.astype(jnp.float32)
    mean_square = jnp.mean(hidden_wide * hidden_wide, axis=1, keepdims=True)
    normed = (hidden_wide * lax.rsqrt(mean_square + 1e-06) * norm_gain).astype(jnp.bfloat16)
    affinity = jax.nn.sigmoid(jnp.dot(normed, router, preferred_element_type=jnp.float32))
    picked_aff = jnp.take_along_axis(affinity, routes, axis=1)
    combine_w = 2.5 * picked_aff / jnp.sum(picked_aff, axis=1, keepdims=True)
    kept_route = bucket_slots < CAP
    target = routes * CAP + jnp.minimum(bucket_slots, CAP - 1)
    experts_all = router.shape[1]
    slot_hit = jnp.any(
        (target[:, :, None] == jnp.arange(experts_all * CAP)[None, None, :])
        & kept_route[:, :, None],
        axis=1,
    )
    outgoing = jnp.einsum(
        "te,td->ed", slot_hit.astype(jnp.bfloat16), normed, preferred_element_type=jnp.float32
    ).astype(jnp.bfloat16)
    exp_local = w_gate.shape[0]
    model_width = normed.shape[1]
    outgoing = outgoing.reshape(n_ctx, exp_local, CAP, model_width)
    copies = jnp.broadcast_to(
        outgoing[:, None], (n_ctx, n_ep, exp_local, CAP, model_width)
    ).reshape(devices, exp_local, CAP, model_width)
    partial_out = expert_work(
        lax.all_to_all(copies, ("ctx", "ep"), split_axis=0, concat_axis=0, tiled=True),
        w_gate,
        w_up,
        w_down,
    ).astype(jnp.bfloat16)
    returned = lax.all_to_all(partial_out, ("ctx", "ep"), split_axis=0, concat_axis=0, tiled=True)
    expert_out = jnp.sum(
        returned.reshape(n_ctx, n_ep, exp_local, CAP, model_width).astype(jnp.float32), axis=1
    )
    expert_rows = expert_out.reshape(experts_all * CAP, model_width)
    fetched = jnp.take(expert_rows, target, axis=0)
    route_weight = jnp.where(kept_route, combine_w, 0.0)
    moe_sum = jnp.sum(route_weight[:, :, None] * fetched, axis=1)
    return (hidden_wide + moe_sum).astype(jnp.bfloat16)


def solution(mesh):
    placed = (
        P("ep", None, None, None),
        P("ctx", None),
        P("ep", None, None),
        P("ep", None),
        P(("ctx", "ep"), None, None),
        P(("ctx", "ep"), None),
        P(("ctx", "ep"), None),
        P(),
        P(),
        P(("ctx", "ep"), None),
        P(("ctx", "ep"), None),
        P("ctx", None, "ep"),
        P("ctx", None, "ep"),
        P("ctx", "ep", None),
    )
    return jax.shard_map(
        per_device, mesh=mesh, in_specs=placed, out_specs=P(("ctx", "ep"), None), check_vma=False
    )
```

profile of v0, /device:TPU:1, one launch (start us, length us, event | category | flops | bytes accessed | tf_op | source)
XLA Modules:
  0.0 798.6 jit_solution(14939651665633660800)
XLA Ops:
  9.9 4.3 copy.75
  14.6 70.9 %gather_fusion = bf16[16384,576]{1,0:T(8,128)(2,1)} fusion(bf16[2048,576]{1,0:T(8,128)(2,1)} %copy.75, s32[16384]{0:T(1024)S(1)} %broadcast_clamp_fusion), kind=kCustom, calls=%fused_computation | custom fusion | bytes 37814272 | tf_op jit(solution)/shard_map/jit(_take)/gather | solution.py:68
  85.5 18.9 %broadcast_select_fusion = bf16[32,512,576]{2,1,0:T(8,128)(2,1)} fusion(bf16[32,512,576]{2,1,0:T(8,128)(2,1)} %bitcast.108, pred[32,512]{1,0:T(8,128)(4,1)S(1)} %compare_and_fusion), kind=kLoop, calls=%fused_computation.3 | loop fusion | flops 9437184 | bytes 37765120 | tf_op jit(solution)/shard_map/jit(_take)/select_n | solution.py:68
  104.4 15.9 %bitcast_reduce_fusion = (f32[32,256]{1,0:T(8,128)S(1)}, f32[32,512,256]{2,1,0:T(8,128)}) fusion(pred[32,512]{1,0:T(8,128)(4,1)S(1)} %broadcast_in_dim.117, bf16[32,512,576]{2,1,0:T(8,128)(2,1)} %broadcast_select_fusion, bf16[32,2,128,576]{2,3,1,0:T(8,128)(2,1)S(1)} %copy-done.8), kind=kOutput, calls=%fused_computation.7 | convolution fusion | flops 4844412928 | bytes 45137920 | tf_op jit(solution)/shard_map/sqd,skd->sqk/dot_general | solution.py:72
  120.3 1.4 fusion.70
  122.5 11.5 %all-to-all-start = ((f32[32,2,128]{0,1,2:T(2,128)}), f32[32,2,128]{0,1,2:T(2,128)S(1)}, u32[]{:S(2)}, u32[]{:S(2)}) async-start(f32[32,2,128]{0,1,2:T(2,128)} %copy.78), calls=%async_computation | async-start | bytes 262144 | tf_op jit(solution)/shard_map/all_to_all | solution.py:104
  134.0 22.8 %fusion = f32[32,256,512]{2,1,0:T(8,128)} fusion(bf16[32,512,576]{2,1,0:T(8,128)(2,1)} %broadcast_select_fusion, f32[32,512,256]{2,1,0:T(8,128)} %get-tuple-element.14, f32[32,256]{1,0:T(8,128)S(1)} %max.11, pred[32,512]{1,0:T(8,128)(4,1)S(1)} %broadcast_in_dim.117), kind=kOutput, calls=%fused_computation.4 | convolution fusion | flops 4315938816 | bytes 50397184 | tf_op jit(solution)/shard_map/sqk,skr->sqr/dot_general | solution.py:87
  156.8 6.0 fusion.4
  163.7 10.2 %all-to-all-start.2 = ((f32[32,2,128]{0,1,2:T(2,128)}), f32[32,2,128]{0,1,2:T(2,128)S(1)}, u32[]{:S(2)}, u32[]{:S(2)}) async-start(f32[32,2,128]{0,1,2:T(2,128)} %copy.84), calls=%async_computation.2 | async-start | bytes 262144 | tf_op jit(solution)/shard_map/all_to_all | solution.py:105
  173.9 8.2 %convolution_add_fusion = f32[32,256,512]{2,1,0:T(8,128)S(1)} fusion(f32[32,256,512]{2,1,0:T(8,128)} %fusion, bf16[32,2,576]{2,1,0:T(2,128)(2,1)S(1)} %copy-done.4, f32[32,256,2]{1,2,0:T(2,128)S(1)} %get-tuple-element.16, pred[256,2]{0,1:T(4,128)(4,1)S(1)} %compare_and_fusion.1, f32[32,256]{1,0:T(8,128)S(1)} %max.11), kind=kOutput, calls=%fused_computation.14 | convolution fusion | flops 21020672 | bytes 33719296 | tf_op jit(solution)/shard_map/sqk,skr->sqr/dot_general | solution.py:93
  182.1 19.6 %copy.81 = f32[32,2,128,512]{3,0,1,2:T(8,128)} copy(f32[32,2,128,512]{3,2,1,0:T(8,128)S(1)} %bitcast.109) | data formatting | bytes 33554432 | tf_op jit(solution)/shard_map/reshape | solution.py:99
  201.6 10.2 %all-to-all-start.1 = ((f32[32,2,128,512]{3,0,1,2:T(8,128)}), f32[32,2,128,512]{3,0,1,2:T(8,128)}, u32[]{:S(2)}, u32[]{:S(2)}) async-start(f32[32,2,128,512]{3,0,1,2:T(8,128)} %copy.81), calls=%async_computation.1 | async-start | bytes 33554432 | tf_op jit(solution)/shard_map/all_to_all | solution.py:103
  212.8 210.8 %all-to-all-done.1 = f32[32,2,128,512]{3,0,1,2:T(8,128)} async-done(((f32[32,2,128,512]{3,0,1,2:T(8,128)}), f32[32,2,128,512]{3,0,1,2:T(8,128)}, u32[]{:S(2)}, u32[]{:S(2)}) %all-to-all-start.1) | async-done | bytes 16777248 | tf_op jit(solution)/shard_map/all_to_all | solution.py:103
  423.7 7.0 copy.82
  430.7 1.5 multiply_reduce_fusion
  432.8 7.3 fusion.71
  440.2 203.5 %all-reduce.3.cloned.1.call-done = f32[512,7168]{1,0:T(8,128)} async-done(((f32[512,7168]{1,0:T(8,128)}), f32[512,7168]{1,0:T(8,128)}) %all-reduce.3.cloned.1.call-update) | async-done | bytes 14680080
  643.7 1.1 fusion.47
  646.8 1.9 broadcast_in_dim.133
  648.7 53.8 %all_to_all.55 = bf16[128,1,2,7168]{3,2,1,0:T(2,128)(2,1)} all-to-all(bf16[128,1,2,7168]{3,2,1,0:T(2,128)(2,1)S(1)} %bitcast.111), channel_id=1, replica_groups=mesh['ctx'=16,'ep'=8] {'ctx','ep'}, dimensions={0} | all-to-all | bytes 7340032 | tf_op jit(solution)/shard_map/all_to_all | solution.py:144
  702.5 8.4 %reshape_squeeze.3 = bf16[256,7168]{1,0:T(8,128)(2,1)} reshape(bf16[128,1,2,7168]{3,2,1,0:T(2,128)(2,1)} %all_to_all.55) | data formatting | bytes 7340032 | tf_op jit(solution)/shard_map/reshape;squeeze | solution.py:28
  711.0 4.4 fusion.23
  715.4 0.9 copy-done.9
  716.3 1.1 fusion.28
  717.4 3.2 fusion.10
  720.6 5.6 copy.88
  726.2 5.7 all-to-all-start.4
  732.1 47.0 %all-to-all-done.4 = bf16[128,1,2,7168]{3,2,1,0:T(2,128)(2,1)} async-done(((bf16[128,1,2,7168]{3,2,1,0:T(2,128)(2,1)}), bf16[128,1,2,7168]{3,2,1,0:T(2,128)(2,1)}, u32[]{:S(2)}, u32[]{:S(2)}) %all-to-all-start.4) | async-done | bytes 3670048 | tf_op jit(solution)/shard_map/all_to_all | solution.py:149
  779.1 6.7 convert_reduce_fusion
  785.7 1.8 reshape.278
  787.5 1.7 gather_fusion.1
  789.3 1.5 fusion.42
  (77 shorter events, 9.7 us)
Async XLA Ops:
  6.5 426.2 %copy-start = (bf16[128,7168]{1,0:T(8,128)(2,1)S(1)}, bf16[128,7168]{1,0:T(8,128)(2,1)}, u32[]{:S(2)}) copy-start(bf16[128,7168]{1,0:T(8,128)(2,1)} %param.19) | copy-start | bytes 5505028
  85.5 18.9 %copy-start.8 = (bf16[32,2,128,576]{2,3,1,0:T(8,128)(2,1)S(1)}, bf16[32,2,128,576]{2,3,1,0:T(8,128)(2,1)}, u32[]{:S(2)}) copy-start(bf16[32,2,128,576]{2,3,1,0:T(8,128)(2,1)} %param.14) | copy-start | bytes 28311556
  104.4 15.9 %copy-start.4 = (bf16[32,2,576]{2,1,0:T(2,128)(2,1)S(1)}, bf16[32,2,576]{2,1,0:T(2,128)(2,1)}, u32[]{:S(2)}) copy-start(bf16[32,2,576]{2,1,0:T(2,128)(2,1)} %param.16) | copy-start | bytes 221188
  122.5 41.2 %all-to-all-start = ((f32[32,2,128]{0,1,2:T(2,128)}), f32[32,2,128]{0,1,2:T(2,128)S(1)}, u32[]{:S(2)}, u32[]{:S(2)}) async-start(f32[32,2,128]{0,1,2:T(2,128)} %copy.78), calls=%async_computation | async-start | bytes 262144 | tf_op jit(solution)/shard_map/all_to_all | solution.py:104
  134.0 22.8 %copy-start.1 = (f32[32,512,256]{2,1,0:T(8,128)S(1)}, f32[32,512,256]{2,1,0:T(8,128)}, u32[]{:S(2)}) copy-start(f32[32,512,256]{2,1,0:T(8,128)} %get-tuple-element.14) | copy-start | bytes 50331652
  163.7 37.9 %all-to-all-start.2 = ((f32[32,2,128]{0,1,2:T(2,128)}), f32[32,2,128]{0,1,2:T(2,128)S(1)}, u32[]{:S(2)}, u32[]{:S(2)}) async-start(f32[32,2,128]{0,1,2:T(2,128)} %copy.84), calls=%async_computation.2 | async-start | bytes 262144 | tf_op jit(solution)/shard_map/all_to_all | solution.py:105
  201.6 222.0 %all-to-all-start.1 = ((f32[32,2,128,512]{3,0,1,2:T(8,128)}), f32[32,2,128,512]{3,0,1,2:T(8,128)}, u32[]{:S(2)}, u32[]{:S(2)}) async-start(f32[32,2,128,512]{3,0,1,2:T(8,128)} %copy.81), calls=%async_computation.1 | async-start | bytes 33554432 | tf_op jit(solution)/shard_map/all_to_all | solution.py:103
  211.9 431.9 %all-reduce.3.cloned.1.call-start = ((), (), s32[]{:S(2)}) async-start(), calls=%async_computation.5 | async-start | bytes 29360128
  430.6 1.6 copy-start.11
  432.7 7.3 copy-start.5
  432.7 7.4 copy-start.7
  432.8 211.0 %copy-start.3 = (bf16[4,7168]{1,0:T(4,128)(2,1)S(1)}, bf16[4,7168]{1,0:T(4,128)(2,1)}, u32[]{:S(2)}) copy-start(bf16[4,7168]{1,0:T(4,128)(2,1)} %param.20) | copy-start | bytes 172036
  432.8 212.1 %copy-start.6 = (f32[7168]{0:T(1024)S(1)}, f32[7168]{0:T(1024)}, u32[]{:S(2)}) copy-start(f32[7168]{0:T(1024)} %param.21) | copy-start | bytes 86020
  432.8 212.1 %copy-start.10 = (bf16[7168,16]{0,1:T(8,128)(2,1)S(1)}, bf16[7168,16]{0,1:T(8,128)(2,1)}, u32[]{:S(2)}) copy-start(bf16[7168,16]{0,1:T(8,128)(2,1)} %param.22) | copy-start | bytes 688132
  710.9 4.4 copy-start.2
  711.0 5.3 copy-start.9
  726.2 52.9 %all-to-all-start.4 = ((bf16[128,1,2,7168]{3,2,1,0:T(2,128)(2,1)}), bf16[128,1,2,7168]{3,2,1,0:T(2,128)(2,1)}, u32[]{:S(2)}, u32[]{:S(2)}) async-start(bf16[128,1,2,7168]{3,2,1,0:T(2,128)(2,1)} %copy.88), calls=%async_computation.4 | async-start | bytes 7340032 | tf_op jit(solution)/shard_map/all_to_all | solution.py:149
Sparse Core Ops, SparseCore 0:
  440.2 203.4 all-reduce.2
where the time goes:
time: 806 us; the launch traced here: 799 us
  waiting for transfers between devices  461 us (57%)
  local copies, waits for them, and re-layouts  126 us (16%)
  matrix products  65.1 us (8%)
  blocking collectives  53.8 us (7%)
  other arithmetic  40.2 us (5%)
  starting transfers between devices  38.2 us (5%)
  between operations  14.1 us (2%)
    all_to_all x1, waiting for transfers between devices, per_device(): lax.all_to_all(weighted, ('ctx', 'ep'), split_axis=2, concat_axis=0, tile...  211 us
    unnamed x2, waiting for transfers between devices  204 us
    gather x1, local copies, waits for them, and re-layouts, per_device(): jnp.take(prompt_latent, key_rows, axis=0)  70.9 us
    all_to_all x1, blocking collectives, per_device(): lax.all_to_all(copies, ('ctx', 'ep'), split_axis=0, concat_axis=0, tiled=...  53.8 us
    all_to_all x1, waiting for transfers between devices, per_device(): lax.all_to_all(partial_out, ('ctx', 'ep'), split_axis=0, concat_axis=0, t...  47 us
    dot_general x1, matrix products, per_device(): jnp.einsum('sqk,skr->sqr', key_weight.astype(jnp.bfloat16), gathered[:, :...  22.8 us
    reshape x1, local copies, waits for them, and re-layouts, per_device(): weighted = weighted.reshape(samples, step_count, head_count, rank_width)  19.6 us
    select_n x2, other arithmetic, per_device(): jnp.take(prompt_latent, key_rows, axis=0)  19 us
  transfers between devices with their start and end apart: 5, of which 3 were waited for; matrix products, arithmetic and copies ran while one was open for 7% of the time, Pallas kernels for 0%

commit v1 on v0

v1 whole, which is shorter than its diff:
```python
import jax
import jax.numpy as jnp
from jax import lax
from jax.experimental import pallas as pl
from jax.experimental.pallas import tpu as pltpu
from jax.sharding import PartitionSpec as P

BLOCK = 64
CAPB = 8
CAP = 2
PAIR = 2 * BLOCK
OWN_ROWS = 16

score_scale = 192.0 ** (-0.5)
masked_score = -1e30
BF = jnp.bfloat16
F32 = jnp.float32


def attend_kernel(
    count_ref, table_ref, own_ref, q_ref, prompt_ref, new_ref, acc_ref, stat_ref, keys, acc, top, tot
):
    sample = pl.program_id(0)
    rows = q_ref.shape[1]
    rank = acc_ref.shape[2]
    count = count_ref[sample]
    own = own_ref[0]
    chunks = (count + own + 1) // 2

    @pl.when(sample == 0)
    def _():
        keys[...] = jnp.zeros_like(keys)

    top[...] = jnp.full(top.shape, masked_score, F32)
    tot[...] = jnp.zeros_like(tot)
    acc[...] = jnp.zeros_like(acc)
    column = lax.broadcasted_iota(jnp.int32, (rows, PAIR), 1)
    step = lax.broadcasted_iota(jnp.int32, (rows, PAIR), 0) // (rows // 2)

    def body(chunk, carry):
        for half in range(2):
            place = 2 * chunk + half

            @pl.when(place < count)
            def _():
                start = pl.multiple_of(table_ref[sample, jnp.minimum(place, CAPB - 1)] * BLOCK, BLOCK)
                keys[half * BLOCK : (half + 1) * BLOCK, :] = prompt_ref[pl.ds(start, BLOCK), :]

            @pl.when((place == count) & (own == 1))
            def _():
                keys[half * BLOCK : half * BLOCK + OWN_ROWS, :] = new_ref[0]

        place = 2 * chunk + column // BLOCK
        within = column % BLOCK
        live = (place < count) | ((place == count) & (own == 1) & (within <= step))
        scores = (
            lax.dot_general(
                q_ref[0], keys[...], (((1,), (1,)), ((), ())), preferred_element_type=F32
            )
            * score_scale
        )
        scores = jnp.where(live, scores, masked_score)
        old_top = top[...]
        new_top = jnp.maximum(old_top, jnp.max(scores, axis=1, keepdims=True))
        factor = jnp.exp(old_top - new_top)
        weight = jnp.where(live, jnp.exp(scores - new_top[:, :1]), 0.0)
        top[...] = new_top
        tot[...] = tot[...] * factor + jnp.sum(weight, axis=1, keepdims=True)
        acc[...] = acc[...] * factor[:, :1] + jnp.dot(
            weight.astype(BF), keys[:, :rank], preferred_element_type=F32
        )
        return carry

    lax.fori_loop(0, chunks, body, 0)
    acc_ref[0] = acc[...].astype(BF)
    lane = lax.broadcasted_iota(jnp.int32, (rows, stat_ref.shape[2]), 1)
    stat_ref[0] = jnp.where(lane == 0, top[:, :1], tot[:, :1])


def attend(flat_query, prompt_latent, own_rows, count, table, own, rank):
    samples, rows, latent = flat_query.shape
    prompt = prompt_latent.shape[0]
    return pl.pallas_call(
        attend_kernel,
        grid_spec=pltpu.PrefetchScalarGridSpec(
            num_scalar_prefetch=3,
            grid=(samples,),
            in_specs=[
                pl.BlockSpec((1, rows, latent), lambda s, *_: (s, 0, 0)),
                pl.BlockSpec((prompt, latent), lambda s, *_: (0, 0)),
                pl.BlockSpec((1, OWN_ROWS, latent), lambda s, *_: (s, 0, 0)),
            ],
            out_specs=[
                pl.BlockSpec((1, rows, rank), lambda s, *_: (s, 0, 0)),
                pl.BlockSpec((1, rows, 2), lambda s, *_: (s, 0, 0)),
            ],
            scratch_shapes=[
                pltpu.VMEM((PAIR, latent), BF),
                pltpu.VMEM((rows, rank), F32),
                pltpu.VMEM((rows, 128), F32),
                pltpu.VMEM((rows, 128), F32),
            ],
        ),
        out_shape=[
            jax.ShapeDtypeStruct((samples, rows, rank), BF),
            jax.ShapeDtypeStruct((samples, rows, 2), F32),
        ],
        compiler_params=pltpu.CompilerParams(vmem_limit_bytes=40 * 1024 * 1024),
        cost_estimate=pl.CostEstimate(
            flops=2 * samples * rows * PAIR * (latent + rank),
            bytes_accessed=2 * samples * rows * (latent + rank),
            transcendentals=samples * rows * PAIR,
        ),
    )(count, table, own, flat_query, prompt_latent, own_rows)


def per_device(
    queries,
    prompt_latent,
    new_latent,
    blocks,
    value_up,
    w_out,
    residual,
    norm_gain,
    router,
    routes,
    bucket_slots,
    w_gate,
    w_up,
    w_down,
):
    n_ctx = lax.axis_size("ctx")
    n_ep = lax.axis_size("ep")
    devices = n_ctx * n_ep
    ctx_place = lax.axis_index("ctx")
    ep_place = lax.axis_index("ep")
    core = ep_place % 2
    swap = [(i, i ^ 1) for i in range(n_ep)]
    samples, step_count, head_count, latent = queries.shape
    rank = value_up.shape[1]
    value_width = value_up.shape[2]
    own_heads = head_count // n_ctx
    tokens_here = samples * step_count
    model_width = w_out.shape[1]
    part = model_width // n_ep

    all_up = lax.all_gather(value_up, ("ctx", "ep"), axis=0, tiled=True)

    blk_local = prompt_latent.shape[0] // BLOCK
    shard_of = blocks // blk_local
    offset = blocks % blk_local
    is_local = (shard_of == ctx_place).astype(jnp.int32)
    position = jnp.cumsum(is_local, axis=1) - 1
    chosen = (is_local[:, :, None] == 1) & (
        position[:, :, None] == jnp.arange(CAPB)[None, None, :]
    )
    table = jnp.sum(jnp.where(chosen, offset[:, :, None], 0), axis=1)
    count = jnp.minimum(jnp.sum(is_local, axis=1), CAPB)
    own = (ctx_place == n_ctx - 1).astype(jnp.int32).reshape(1)
    own_rows = jnp.pad(new_latent, ((0, 0), (0, OWN_ROWS - step_count), (0, 0)))

    flat_query = queries.reshape(samples, step_count * head_count, latent)
    acc, stat = attend(flat_query, prompt_latent, own_rows, count, table, own, rank)

    stat = stat.reshape(samples, step_count, n_ctx, own_heads, 2).transpose(2, 4, 3, 0, 1)
    stat = stat.reshape(n_ctx, 2 * own_heads, tokens_here)
    stat = lax.all_to_all(stat, "ctx", split_axis=0, concat_axis=0, tiled=True)
    row_max, row_total = stat[:, :own_heads], stat[:, own_heads:]
    factor = jnp.exp(row_max - jnp.max(row_max, axis=0, keepdims=True))
    factor = factor / jnp.sum(factor * row_total, axis=0, keepdims=True)

    w_cols = w_out.reshape(w_out.shape[0], n_ep, part).transpose(1, 0, 2)
    w_cols = lax.all_to_all(w_cols, "ep", split_axis=0, concat_axis=0, tiled=True)
    w_cols = w_cols.reshape(own_heads * value_width, part)

    acc = acc.reshape(samples, step_count, head_count, rank)
    part_values = jnp.einsum("sthr,hrv->hstv", acc, all_up, preferred_element_type=F32).astype(BF)
    part_values = part_values.reshape(n_ctx, own_heads * tokens_here, value_width)
    part_values = lax.all_to_all(part_values, "ctx", split_axis=0, concat_axis=0, tiled=True)
    part_values = part_values.reshape(n_ctx, own_heads, tokens_here, value_width)
    head_values = jnp.sum(part_values.astype(F32) * factor[..., None], axis=0).astype(BF)
    head_values = head_values.transpose(1, 0, 2).reshape(tokens_here, own_heads * value_width)

    head_flat = lax.all_gather(head_values, "ep", axis=0, tiled=True)
    projected = jnp.dot(head_flat, w_cols, preferred_element_type=F32).astype(BF)
    tok_dev = residual.shape[0]
    projected = lax.all_to_all(
        projected.reshape(devices, tok_dev, part),
        ("ctx", "ep"),
        split_axis=0,
        concat_axis=0,
        tiled=True,
    )
    attention = jnp.sum(projected.reshape(n_ctx, n_ep, tok_dev, part).astype(F32), axis=0)
    attention = attention.transpose(1, 0, 2).reshape(tok_dev, model_width)

    hidden_state = (residual.astype(F32) + attention).astype(BF)
    hidden_wide = hidden_state.astype(F32)
    mean_square = jnp.mean(hidden_wide * hidden_wide, axis=1, keepdims=True)
    normed = (hidden_wide * lax.rsqrt(mean_square + 1e-06) * norm_gain).astype(BF)
    affinity = jax.nn.sigmoid(jnp.dot(normed, router, preferred_element_type=F32))
    experts_all = router.shape[1]
    experts = jnp.arange(experts_all)
    picked = (routes[:, :, None] == experts[None, None, :]).astype(F32)
    picked_aff = jnp.sum(picked * affinity[:, None, :], axis=2)
    combine_w = 2.5 * picked_aff / jnp.sum(picked_aff, axis=1, keepdims=True)
    kept_route = bucket_slots < CAP
    hits = picked[:, :, :, None] * (
        (bucket_slots[:, :, None] == jnp.arange(CAP)[None, None, :]) & kept_route[:, :, None]
    ).astype(F32)[:, :, None, :]
    slot_hit = jnp.sum(hits, axis=1).reshape(tok_dev, experts_all * CAP)
    slot_weight = jnp.sum(hits * combine_w[:, :, None, None], axis=1)

    outgoing = jnp.einsum(
        "te,td->ed", slot_hit.astype(BF), normed, preferred_element_type=F32
    ).astype(BF)
    chips = n_ep // CAP
    copies = jnp.broadcast_to(
        outgoing.reshape(n_ctx, 1, CAP, n_ep, part), (n_ctx, chips, CAP, n_ep, part)
    ).reshape(devices, n_ep, part)
    arrived = lax.all_to_all(copies, ("ctx", "ep"), split_axis=0, concat_axis=0, tiled=True)
    arrived = arrived.reshape(devices, model_width)
    sibling = lax.ppermute(arrived, "ep", swap)
    rows = jnp.concatenate([arrived, sibling], axis=0)
    gate_act = jnp.dot(rows, w_gate[0], preferred_element_type=F32)
    up_act = jnp.dot(rows, w_up[0], preferred_element_type=F32)
    inner_act = (jax.nn.silu(gate_act) * up_act).astype(BF)
    theirs = jnp.dot(inner_act[devices:], w_down[0], preferred_element_type=F32).astype(BF)
    theirs = lax.ppermute(theirs, "ep", swap)
    ours = jnp.dot(inner_act[:devices], w_down[0], preferred_element_type=F32)
    pair_out = (ours + theirs.astype(F32)).astype(BF).reshape(devices, n_ep, part)
    returned = lax.all_to_all(pair_out, ("ctx", "ep"), split_axis=0, concat_axis=0, tiled=True)
    expert_rows = jnp.sum(
        returned.reshape(n_ctx, chips, CAP, n_ep, part).astype(F32), axis=1
    ).reshape(1, experts_all, CAP, n_ep, part)
    moe_sum = jnp.sum(slot_weight[:, :, :, None, None] * expert_rows, axis=(1, 2))
    return (hidden_wide + moe_sum.reshape(tok_dev, model_width)).astype(BF)


def solution(mesh):
    placed = (
        P("ep", None, None, None),
        P("ctx", None),
        P("ep", None, None),
        P("ep", None),
        P(("ctx", "ep"), None, None),
        P(("ctx", "ep"), None),
        P(("ctx", "ep"), None),
        P(),
        P(),
        P(("ctx", "ep"), None),
        P(("ctx", "ep"), None),
        P("ctx", None, "ep"),
        P("ctx", None, "ep"),
        P("ctx", "ep", None),
    )
    return jax.shard_map(
        per_device, mesh=mesh, in_specs=placed, out_specs=P(("ctx", "ep"), None), check_vma=False
    )
```

time: 806 us -> 318 us (0.39)
  waiting for transfers between devices: 461 us -> 74.2 us
  local copies, waits for them, and re-layouts: 126 us -> 43 us
  Pallas kernels: 0 us -> 43 us
  matrix products: 65.1 us -> 25.1 us
  other arithmetic: 40.2 us -> 6.04 us
  blocking collectives: 53.8 us -> 72.9 us
    unnamed x2, waiting for transfers between devices: 204 us -> 0.73 us
    all_to_all x4, waiting for transfers between devices: 258 us -> 66.7 us  [the longest x1 27.8 us: per_device(): lax.all_to_all(pair_out, ('ctx', 'ep'), split_axis=0, concat_axis=0, tile...]
    gather x5 -> x0, local copies, waits for them, and re-layouts: 73.5 us -> none  [the longest x1 70.9 us: per_device(): jnp.take(prompt_latent, key_rows, axis=0)]
    pallas_call x0 -> x1, Pallas kernels: none -> 43 us  [attend(): pl.pallas_call(attend_kernel, grid_spec=pltpu.PrefetchScalarGridSpec(num_...]
    all_to_all x0 -> x1, blocking collectives: none -> 41 us  [per_device(): lax.all_to_all(w_cols, 'ep', split_axis=0, concat_axis=0, tiled=True)]
    dot_general x11 -> x8, matrix products: 65.1 us -> 25.1 us  [the longest x1 17.9 us: per_device(): jnp.einsum('sthr,hrv->hstv', acc, all_up, preferred_element_type=F32)]
    unnamed x25 -> x32, local copies, waits for them, and re-layouts: 5.28 us -> 28.3 us
    all_to_all x1, blocking collectives: 53.8 us -> 32 us  [per_device(): lax.all_to_all(copies, ('ctx', 'ep'), split_axis=0, concat_axis=0, tiled=...]
  transfers between devices with their start and end apart: 5 -> 8, of which waited for: 3 -> 5; matrix products, arithmetic and copies ran while one was open for 7% -> 18% of each run, Pallas kernels for 0% -> 14%
where the time goes in v1:
time: 318 us; the launch traced here: 314 us
  waiting for transfers between devices  74.2 us (23%)
  blocking collectives  72.9 us (23%)
  local copies, waits for them, and re-layouts  43 us (14%)
  Pallas kernels  43 us (14%)
  starting transfers between devices  35.8 us (11%)
  matrix products  25.1 us (8%)
  between operations  13.8 us (4%)
  other arithmetic  6.04 us (2%)
    pallas_call x1, Pallas kernels, attend(): pl.pallas_call(attend_kernel, grid_spec=pltpu.PrefetchScalarGridSpec(num_...  43 us
    all_to_all x1, blocking collectives, per_device(): lax.all_to_all(w_cols, 'ep', split_axis=0, concat_axis=0, tiled=True)  41 us
    all_to_all x1, blocking collectives, per_device(): lax.all_to_all(copies, ('ctx', 'ep'), split_axis=0, concat_axis=0, tiled=...  32 us
    unnamed x32, local copies, waits for them, and re-layouts  28.3 us
    all_to_all x1, waiting for transfers between devices, per_device(): lax.all_to_all(pair_out, ('ctx', 'ep'), split_axis=0, concat_axis=0, tile...  27.8 us
    all_to_all x1, waiting for transfers between devices, per_device(): lax.all_to_all(part_values, 'ctx', split_axis=0, concat_axis=0, tiled=True)  21.1 us
    all_to_all x1, starting transfers between devices, per_device(): stat = lax.all_to_all(stat, 'ctx', split_axis=0, concat_axis=0, tiled=True)  19.9 us
    dot_general x1, matrix products, per_device(): jnp.einsum('sthr,hrv->hstv', acc, all_up, preferred_element_type=F32)  17.9 us
  transfers between devices with their start and end apart: 8, of which 5 were waited for; matrix products, arithmetic and copies ran while one was open for 18% of the time, Pallas kernels for 14%

profile of v1, /device:TPU:1, one launch (start us, length us, event | category | flops | bytes accessed | tf_op | source)
XLA Modules:
  0.0 313.9 jit_solution(8339831268365875404)
XLA Ops:
  7.3 0.7 broadcast_compare_fusion
  8.3 14.5 %copy.41 = bf16[32,2,128,576]{3,2,1,0:T(8,128)(2,1)} copy(bf16[32,2,128,576]{2,3,1,0:T(8,128)(2,1)} %param.14) | data formatting | bytes 18874368 | tf_op args[0]
  22.8 3.1 %copy.42.prompt_ref = bf16[2048,576]{1,0:T(8,128)(2,1)S(1)} copy(bf16[2048,576]{0,1:T(8,128)(2,1)} %param.15) | data formatting | bytes 4718592 | tf_op args[1]
  26.7 43.0 %shard_map.136 = (bf16[32,256,512]{2,1,0:T(8,128)(2,1)}, f32[32,256,2]{2,1,0:T(8,128)S(1)}) custom-call(s32[32]{0:T(128)S(1)} %broadcast_minimum_fusion.count_ref, s32[32,8]{1,0:T(8,128)S(1)} %select_reduce_fusion.table_ref, s32[1]{0:T(128)} %bitcast.own_ref, bf16[32,256,576]{2,1,0:T(8,128)(2,1)} %bitcast.66, bf16[2048,576]{1,0:T(8,128)(2,1)S(1)} %copy.42.prompt_ref, ...), custom_call_target="tpu_custom_call" | custom-call | flops 2281701376 | bytes 17825792 | tf_op jit(solution)/shard_map/pallas_call | solution.py:83
  69.7 1.9 copy-done.1
  71.6 5.0 %copy.45 = f32[32,2,16,8,2]{2,3,4,1,0:T(8,128)S(1)} copy(f32[32,2,16,8,2]{4,3,2,1,0:T(8,128)} %bitcast.65) | data formatting | bytes 131072 | tf_op jit(solution)/shard_map/reshape | solution.py:166
  77.0 0.7 reshape.140
  77.7 19.9 %all-to-all-start.1 = ((f32[16,1,1024]{2,1,0:T(1,128)}), f32[16,1,1024]{2,1,0:T(1,128)S(1)}, u32[]{:S(2)}, u32[]{:S(2)}) async-start(f32[16,1,1024]{2,1,0:T(1,128)} %reshape.140), calls=%async_computation.1 | async-start | bytes 131072 | tf_op jit(solution)/shard_map/all_to_all | solution.py:168
  97.6 17.9 %fusion.10 = bf16[128,32,2,128]{3,1,2,0:T(8,128)(2,1)S(1)} fusion(bf16[128,512,128]{2,1,0:T(8,128)(2,1)} %all-gather.3.cloned.1.call-done, bf16[32,2,128,512]{3,2,1,0:T(8,128)(2,1)} %bitcast.67), kind=kOutput, calls=%fused_computation.16 | convolution fusion | flops 1074790400 | bytes 27262976 | tf_op jit(solution)/shard_map/sthr,hrv->hstv/dot_general | solution.py:178
  115.6 3.8 %copy.44 = bf16[128,32,2,128]{3,2,1,0:T(2,128)(2,1)} copy(bf16[128,32,2,128]{3,1,2,0:T(8,128)(2,1)S(1)} %fusion.10) | data formatting | bytes 4194304 | tf_op jit(solution)/shard_map/convert_element_type | solution.py:178
  119.3 6.5 %all-to-all-start = ((bf16[16,512,128]{2,1,0:T(8,128)(2,1)}), bf16[16,512,128]{2,1,0:T(8,128)(2,1)S(1)}, u32[]{:S(2)}, u32[]{:S(2)}) async-start(bf16[16,512,128]{2,1,0:T(8,128)(2,1)} %bitcast.68), calls=%async_computation | async-start | bytes 4194304 | tf_op jit(solution)/shard_map/all_to_all | solution.py:180
  126.4 0.8 reduce.2
  127.4 21.1 %all-to-all-done = bf16[16,512,128]{2,1,0:T(8,128)(2,1)S(1)} async-done(((bf16[16,512,128]{2,1,0:T(8,128)(2,1)}), bf16[16,512,128]{2,1,0:T(8,128)(2,1)S(1)}, u32[]{:S(2)}, u32[]{:S(2)}) %all-to-all-start) | async-done | bytes 2097184 | tf_op jit(solution)/shard_map/all_to_all | solution.py:180
  148.5 1.3 multiply_reduce_fusion
  150.5 3.9 %copy.48 = bf16[128,7168]{0,1:T(8,128)(2,1)} copy(bf16[128,7168]{1,0:T(8,128)(2,1)} %param.19) | data formatting | bytes 3670016 | tf_op args[5]
  154.4 41.0 %all_to_all.30 = bf16[8,128,896]{1,2,0:T(8,128)(2,1)S(1)} all-to-all(bf16[8,128,896]{1,2,0:T(8,128)(2,1)} %bitcast.73), channel_id=1, replica_groups=mesh['ctx'=16,'ep'=8] {'ep'}, dimensions={0} | all-to-all | bytes 3670016 | tf_op jit(solution)/shard_map/all_to_all | solution.py:174
  195.4 2.7 copy.49
  198.1 3.1 convolution_convert_fusion.2
  201.2 1.1 reshape.129
  202.3 4.2 %all-to-all-start.3 = ((bf16[128,4,896]{2,1,0:T(4,128)(2,1)}), bf16[128,4,896]{2,1,0:T(4,128)(2,1)S(1)}, u32[]{:S(2)}, u32[]{:S(2)}) async-start(bf16[128,4,896]{2,1,0:T(4,128)(2,1)} %reshape.129), calls=%async_computation.3 | async-start | bytes 1835008 | tf_op jit(solution)/shard_map/all_to_all | solution.py:188
  206.7 17.8 %all-to-all-done.3 = bf16[128,4,896]{2,1,0:T(4,128)(2,1)S(1)} async-done(((bf16[128,4,896]{2,1,0:T(4,128)(2,1)}), bf16[128,4,896]{2,1,0:T(4,128)(2,1)S(1)}, u32[]{:S(2)}, u32[]{:S(2)}) %all-to-all-start.3) | async-done | bytes 917536 | tf_op jit(solution)/shard_map/all_to_all | solution.py:188
  226.4 32.0 %all_to_all.31 = bf16[128,8,896]{2,1,0:T(8,128)(2,1)S(1)} all-to-all(bf16[128,8,896]{2,1,0:T(8,128)(2,1)S(1)} %bitcast.75), channel_id=1, replica_groups=mesh['ctx'=16,'ep'=8] {'ctx','ep'}, dimensions={0} | all-to-all | bytes 3670016 | tf_op jit(solution)/shard_map/all_to_all | solution.py:222
  258.7 1.0 collective-permute-start
  259.7 3.3 %collective-permute-done = bf16[128,7168]{1,0:T(8,128)(2,1)S(1)} collective-permute-done((bf16[128,7168]{1,0:T(8,128)(2,1)S(1)}, bf16[128,7168]{1,0:T(8,128)(2,1)S(1)}, u32[]{:S(2)}, u32[]{:S(2)}) %collective-permute-start) | collective-permute-done | bytes 1835040 | tf_op jit(solution)/shard_map/ppermute | solution.py:224
  263.2 1.1 fusion.8
  264.3 0.9 copy-done.10
  265.2 1.1 multiply_convert_fusion
  266.3 0.9 copy-done.2
  268.3 3.4 %collective-permute-done.1 = bf16[128,7168]{1,0:T(8,128)(2,1)S(1)} collective-permute-done((bf16[128,7168]{1,0:T(8,128)(2,1)S(1)}, bf16[128,7168]{1,0:T(8,128)(2,1)S(1)}, u32[]{:S(2)}, u32[]{:S(2)}) %collective-permute-start.1) | collective-permute-done | bytes 1835040 | tf_op jit(solution)/shard_map/ppermute | solution.py:230
  272.4 1.6 copy.56
  274.0 3.8 %all-to-all-start.5 = ((bf16[128,8,896]{2,1,0:T(8,128)(2,1)}), bf16[128,8,896]{2,1,0:T(8,128)(2,1)S(1)}, u32[]{:S(2)}, u32[]{:S(2)}) async-start(bf16[128,8,896]{2,1,0:T(8,128)(2,1)} %bitcast.38), calls=%async_computation.5 | async-start | bytes 3670016 | tf_op jit(solution)/shard_map/all_to_all | solution.py:233
  277.9 27.8 %all-to-all-done.5 = bf16[128,8,896]{2,1,0:T(8,128)(2,1)S(1)} async-done(((bf16[128,8,896]{2,1,0:T(8,128)(2,1)}), bf16[128,8,896]{2,1,0:T(8,128)(2,1)S(1)}, u32[]{:S(2)}, u32[]{:S(2)}) %all-to-all-start.5) | async-done | bytes 1835040 | tf_op jit(solution)/shard_map/all_to_all | solution.py:233
  (65 shorter events, 9.1 us)
Async XLA Ops:
  6.5 218.5 %copy-start = (bf16[7168,16]{0,1:T(8,128)(2,1)S(1)}, bf16[7168,16]{0,1:T(8,128)(2,1)}, u32[]{:S(2)}) copy-start(bf16[7168,16]{0,1:T(8,128)(2,1)} %param.22) | copy-start | bytes 688132
  6.5 91.1 %all-gather.3.cloned.1.call-start = ((), (), s32[]{:S(2)}) async-start(), calls=%async_computation.6 | async-start | bytes 16908288 | tf_op jit(solution)/shard_map/all_gather | solution.py:148
  22.8 3.2 %copy-start.3 = (bf16[32,2,576]{2,1,0:T(2,128)(2,1)S(1)}, bf16[32,2,576]{2,1,0:T(2,128)(2,1)}, u32[]{:S(2)}) copy-start(bf16[32,2,576]{2,1,0:T(2,128)(2,1)} %param.16) | copy-start | bytes 221188
  22.8 3.2 %copy-start.4 = (s32[32,32]{1,0:T(8,128)S(1)}, s32[32,32]{1,0:T(8,128)}, u32[]{:S(2)}) copy-start(s32[32,32]{1,0:T(8,128)} %param.17) | copy-start | bytes 12292
  69.7 1.9 copy-start.1
  77.7 41.6 %all-to-all-start.1 = ((f32[16,1,1024]{2,1,0:T(1,128)}), f32[16,1,1024]{2,1,0:T(1,128)S(1)}, u32[]{:S(2)}, u32[]{:S(2)}) async-start(f32[16,1,1024]{2,1,0:T(1,128)} %reshape.140), calls=%async_computation.1 | async-start | bytes 131072 | tf_op jit(solution)/shard_map/all_to_all | solution.py:168
  119.3 29.2 %all-to-all-start = ((bf16[16,512,128]{2,1,0:T(8,128)(2,1)}), bf16[16,512,128]{2,1,0:T(8,128)(2,1)S(1)}, u32[]{:S(2)}, u32[]{:S(2)}) async-start(bf16[16,512,128]{2,1,0:T(8,128)(2,1)} %bitcast.68), calls=%async_computation | async-start | bytes 4194304 | tf_op jit(solution)/shard_map/all_to_all | solution.py:180
  125.8 72.3 %all-gather.5.cloned.1.call-start = ((), (), s32[]{:S(2)}) async-start(), calls=%async_computation.7 | async-start | bytes 1179648 | tf_op jit(solution)/shard_map/all_gather | solution.py:185
  201.1 5.4 %copy-start.8 = (s32[4,8]{1,0:T(4,128)S(1)}, s32[4,8]{1,0:T(4,128)}, u32[]{:S(2)}) copy-start(s32[4,8]{1,0:T(4,128)} %param.24) | copy-start | bytes 388
  201.2 5.4 %copy-start.7 = (s32[4,8]{1,0:T(4,128)S(1)}, s32[4,8]{1,0:T(4,128)}, u32[]{:S(2)}) copy-start(s32[4,8]{1,0:T(4,128)} %param.23) | copy-start | bytes 388
  201.2 23.7 %copy-start.5 = (bf16[4,7168]{1,0:T(4,128)(2,1)S(1)}, bf16[4,7168]{1,0:T(4,128)(2,1)}, u32[]{:S(2)}) copy-start(bf16[4,7168]{1,0:T(4,128)(2,1)} %param.20) | copy-start | bytes 172036
  201.2 23.9 %copy-start.6 = (f32[7168]{0:T(1024)S(1)}, f32[7168]{0:T(1024)}, u32[]{:S(2)}) copy-start(f32[7168]{0:T(1024)} %param.21) | copy-start | bytes 86020
  202.3 22.2 %all-to-all-start.3 = ((bf16[128,4,896]{2,1,0:T(4,128)(2,1)}), bf16[128,4,896]{2,1,0:T(4,128)(2,1)S(1)}, u32[]{:S(2)}, u32[]{:S(2)}) async-start(bf16[128,4,896]{2,1,0:T(4,128)(2,1)} %reshape.129), calls=%async_computation.3 | async-start | bytes 1835008 | tf_op jit(solution)/shard_map/all_to_all | solution.py:188
  258.6 4.5 %copy-start.9 = (bf16[1,7168,256]{2,1,0:T(8,128)(2,1)S(1)}, bf16[1,7168,256]{2,1,0:T(8,128)(2,1)}, u32[]{:S(2)}) copy-start(bf16[1,7168,256]{2,1,0:T(8,128)(2,1)} %param.25) | copy-start | bytes 11010052
  258.7 4.4 %collective-permute-start = (bf16[128,7168]{1,0:T(8,128)(2,1)S(1)}, bf16[128,7168]{1,0:T(8,128)(2,1)S(1)}, u32[]{:S(2)}, u32[]{:S(2)}) collective-permute-start(bf16[128,7168]{1,0:T(8,128)(2,1)S(1)} %bitcast.70), channel_id=1, source_target_pairs={{0,1},{1,0},{2,3},{3,2},{4,5},{5,4},{6,7},{7,6},{8,9},{9,8},{10,11... | collective-permute-start | bytes 5505032 | tf_op jit(solution)/shard_map/ppermute | solution.py:224
  263.2 2.0 copy-start.10
  265.2 2.0 copy-start.2
  267.9 3.9 %collective-permute-start.1 = (bf16[128,7168]{1,0:T(8,128)(2,1)S(1)}, bf16[128,7168]{1,0:T(8,128)(2,1)S(1)}, u32[]{:S(2)}, u32[]{:S(2)}) collective-permute-start(bf16[128,7168]{1,0:T(8,128)(2,1)S(1)} %convolution_convert_fusion), channel_id=1, source_target_pairs={{0,1},{1,0},{2,3},{3,2},{4,5},{5,4},{6,7},{7,6},{8,9},{9,8},{10,11... | collective-permute-start | bytes 5505032 | tf_op jit(solution)/shard_map/ppermute | solution.py:230
  274.0 31.7 %all-to-all-start.5 = ((bf16[128,8,896]{2,1,0:T(8,128)(2,1)}), bf16[128,8,896]{2,1,0:T(8,128)(2,1)S(1)}, u32[]{:S(2)}, u32[]{:S(2)}) async-start(bf16[128,8,896]{2,1,0:T(8,128)(2,1)} %bitcast.38), calls=%async_computation.5 | async-start | bytes 3670016 | tf_op jit(solution)/shard_map/all_to_all | solution.py:233
Sparse Core Ops, SparseCore 0:
  10.5 83.9 all-gather.2
  150.6 33.3 all-gather.4

commit v2 on v1

v2 whole, which is shorter than its diff:
```python
import functools

import jax
import jax.numpy as jnp
from jax import lax
from jax.experimental import pallas as pl
from jax.experimental.pallas import tpu as pltpu
from jax.sharding import PartitionSpec as P

BLOCK = 64
CAPB = 8
CAP = 2
FEW = 2
GROUP = 4
RING = 4
STAT_ROWS = 16
VMEM_LIMIT = 40 * 1024 * 1024
OWN_ROWS = 16

score_scale = 192.0 ** (-0.5)
masked_score = -1e30
BF = jnp.bfloat16
F32 = jnp.float32


def cut(ref, place, spans, lead=()):
    pieces = [
        ref[(*lead, pl.ds(pl.multiple_of(base + place * width, 8), width), slice(None))]
        for base, width in spans
    ]
    return jnp.concatenate(pieces, axis=0)


def split(value):
    high = value.astype(BF)
    rest = value - high.astype(F32)
    middle = rest.astype(BF)
    return high, middle, (rest - middle.astype(F32)).astype(BF)


def attend_kernel(
    count_ref, table_ref, info_ref, q_ref, prompt_ref, new_ref, *refs, spans, offset
):
    *out_refs, few, many, acc, stat = refs
    group, steps, latent, heads = q_ref.shape
    rank = out_refs[0].shape[2]
    rows = steps * heads
    first = offset + pl.program_id(0) * group
    own = info_ref[0]
    place = info_ref[1]

    def one(g, keys, n_blocks):
        sample = first + g
        count = count_ref[sample]
        for j in range(n_blocks):
            start = pl.multiple_of(table_ref[sample, j] * BLOCK, BLOCK)
            keys[j * BLOCK : (j + 1) * BLOCK, :] = prompt_ref[pl.ds(start, BLOCK), :]
        n_prompt = n_blocks * BLOCK
        keys[n_prompt : n_prompt + OWN_ROWS, :] = new_ref[g]
        n_keys = n_prompt + OWN_ROWS
        query = jnp.concatenate([q_ref[g, t] for t in range(steps)], axis=1)
        scores = jnp.dot(keys[...], query, preferred_element_type=F32) * score_scale
        key = lax.broadcasted_iota(jnp.int32, (n_keys, rows), 0)
        step = (lax.broadcasted_iota(jnp.int32, (n_keys, rows), 1) >= heads).astype(jnp.int32)
        own_last = jnp.where(own == 1, n_prompt + step, -1)
        live = (key < count * BLOCK) | ((key >= n_prompt) & (key <= own_last))
        scores = jnp.where(live, scores, masked_score)
        top = jnp.max(scores, axis=0, keepdims=True)
        weight = jnp.exp(scores - top)
        stat[g : g + 1, :rows] = top
        stat[g : g + 1, rows:] = jnp.sum(weight, axis=0, keepdims=True)
        acc[g] = lax.dot_general(
            weight.astype(BF),
            keys[:, :rank],
            (((0,), (0,)), ((), ())),
            preferred_element_type=F32,
        )
        part_rows = rows // RING
        late = (pl.program_id(0) >= pl.num_programs(0) // 2).astype(jnp.int32)
        for k, out_ref in zip((0, 2 - late, 3 - late, 1 + 2 * late), out_refs):
            part = cut(acc, lax.rem(place + k, RING), spans, (g,))
            out_ref[0, g * part_rows : (g + 1) * part_rows, :] = part.astype(BF)

    for g in range(group):
        one(g, few.at[g], FEW)
    for g in range(group):

        @pl.when(count_ref[first + g] > FEW)
        def _():
            one(g, many, CAPB)

    for i, addend in enumerate(split(stat[0:group, :])):
        stat[(i + 1) * group : (i + 2) * group, :] = addend.astype(F32)
    stat[4 * group :, :] = jnp.zeros((STAT_ROWS - 3 * group, 2 * rows), F32)
    tail = stat[group : group + STAT_ROWS, :].astype(BF)
    for out_ref in out_refs:
        out_ref[0, group * rows // RING :, :] = tail


def attend(query_t, prompt_latent, own_rows, count, table, info, rank, half, spans):
    samples, steps, latent, heads = query_t.shape
    samples = samples // 2
    rows = steps * heads
    prompt = prompt_latent.shape[0]
    groups = samples // GROUP
    skip = half * groups
    part_rows = GROUP * rows // RING + STAT_ROWS
    return pl.pallas_call(
        functools.partial(attend_kernel, spans=spans, offset=half * samples),
        grid_spec=pltpu.PrefetchScalarGridSpec(
            num_scalar_prefetch=3,
            grid=(groups,),
            in_specs=[
                pl.BlockSpec((GROUP, steps, latent, heads), lambda s, *_: (s + skip, 0, 0, 0)),
                pl.BlockSpec((prompt, latent), lambda s, *_: (0, 0)),
                pl.BlockSpec((GROUP, OWN_ROWS, latent), lambda s, *_: (s + skip, 0, 0)),
            ],
            out_specs=[pl.BlockSpec((1, part_rows, rank), lambda s, *_: (s, 0, 0))] * RING,
            scratch_shapes=[
                pltpu.VMEM((GROUP, FEW * BLOCK + OWN_ROWS, latent), BF),
                pltpu.VMEM((CAPB * BLOCK + OWN_ROWS, latent), BF),
                pltpu.VMEM((GROUP, rows, rank), F32),
                pltpu.VMEM((GROUP + STAT_ROWS, 2 * rows), F32),
            ],
        ),
        out_shape=[jax.ShapeDtypeStruct((groups, part_rows, rank), BF)] * RING,
        compiler_params=pltpu.CompilerParams(vmem_limit_bytes=VMEM_LIMIT),
        cost_estimate=pl.CostEstimate(
            flops=4 * samples * rows * FEW * BLOCK * (latent + rank),
            bytes_accessed=4 * samples * rows * (latent + rank),
            transcendentals=samples * rows * FEW * BLOCK,
        ),
    )(count, table, info, query_t, prompt_latent, own_rows)


def columns_of(stats, scratch, place, spans, total_base):
    lanes = scratch.shape[1]
    row = lax.broadcasted_iota(jnp.int32, (STAT_ROWS, lanes), 0)
    lane = lax.broadcasted_iota(jnp.int32, (STAT_ROWS, lanes), 1)
    pick = ((row % GROUP == lane) & (row < 3 * GROUP)).astype(BF)
    scratch[...] = lax.dot_general(
        stats, pick, (((0,), (0,)), ((), ())), preferred_element_type=F32
    )
    totals = [(base + total_base, width) for base, width in spans]
    return cut(scratch, place, spans), cut(scratch, place, totals)


def combined(parts, scratch, place, spans, total_base):
    body = parts[0].shape[0] - STAT_ROWS
    stats = [
        columns_of(part[body:, :], scratch.at[k], place, spans, total_base)
        for k, part in enumerate(parts)
    ]
    top = functools.reduce(jnp.maximum, [one for one, _ in stats])
    factors = [jnp.exp(one - top) for one, _ in stats]
    return top, sum(f * one for f, (_, one) in zip(factors, stats)), factors


def weighted(parts, factors, j):
    rows = factors[0].shape[0]
    return sum(
        part[j * rows : (j + 1) * rows, :].astype(F32) * factor[:, j : j + 1]
        for part, factor in zip(parts, factors)
    )


def stat_tail(scratch, addends):
    for i, addend in enumerate(addends):
        scratch[i * GROUP : (i + 1) * GROUP, :] = addend.astype(F32)
    scratch[3 * GROUP :, :] = jnp.zeros((STAT_ROWS - 3 * GROUP, scratch.shape[1]), F32)
    return scratch[...].astype(BF)


def relay_kernel(place_ref, held, ahead, behind, forward, backward, columns, lines, *, spans):
    body = held.shape[2] - STAT_ROWS
    half_width = lines.shape[2] // 2
    for side, (passed, out, k) in enumerate(((ahead, forward, 1), (behind, backward, 3))):
        parts = [held.at[side, 0], passed.at[side, 0]]
        target = lax.rem(place_ref[0] + k, RING)
        _, _, factors = combined(parts, columns, target, spans, half_width)
        for j in range(GROUP):
            rows = body // GROUP
            out[0, j * rows : (j + 1) * rows, :] = weighted(parts, factors, j).astype(BF)
        both = []
        for k, part in enumerate(parts):
            lines[k] = part[body:, :].astype(F32)
            both.append(sum(lines[k, i * GROUP : (i + 1) * GROUP, :] for i in range(3)))
        tops = [one[:, :half_width] for one in both]
        top = jnp.maximum(*tops)
        total = sum(jnp.exp(t - top) * one[:, half_width:] for t, one in zip(tops, both))
        addends = split(jnp.concatenate([top, total], axis=1))
        out[0, body:, :] = stat_tail(lines.at[0], addends)


def relay(held, ahead, behind, place, spans):
    groups, part_rows, rank = held.shape
    paired = (2, groups // 2, part_rows, rank)
    both = pl.BlockSpec((2, 1, part_rows, rank), lambda s, *_: (0, s, 0, 0))
    return pl.pallas_call(
        functools.partial(relay_kernel, spans=spans),
        grid_spec=pltpu.PrefetchScalarGridSpec(
            num_scalar_prefetch=1,
            grid=(groups // 2,),
            in_specs=[both] * 3,
            out_specs=[pl.BlockSpec((1, part_rows, rank), lambda s, *_: (s, 0, 0))] * 2,
            scratch_shapes=[
                pltpu.VMEM((2, rank, 128), F32),
                pltpu.VMEM((2, STAT_ROWS, rank), F32),
            ],
        ),
        out_shape=[jax.ShapeDtypeStruct((groups // 2, part_rows, rank), BF)] * 2,
        compiler_params=pltpu.CompilerParams(vmem_limit_bytes=VMEM_LIMIT),
        cost_estimate=pl.CostEstimate(
            flops=4 * groups * part_rows * rank,
            bytes_accessed=6 * groups * part_rows * rank,
            transcendentals=0,
        ),
    )(place, held.reshape(paired), ahead.reshape(paired), behind.reshape(paired))


def first_kernel(
    place_ref, own, ahead, behind, passed_f, passed_b, *refs, spans, next_spans
):
    *outs, columns, total, stat = refs
    rows = sum(width for _, width in spans)
    width = stat.shape[1]
    for side, parts in enumerate(
        (
            [own.at[0, 0], passed_f.at[0], behind.at[0, 0]],
            [own.at[1, 0], passed_b.at[0], ahead.at[1, 0]],
        )
    ):
        top, tot, factors = combined(parts, columns, place_ref[0], spans, width // 2)
        for j in range(GROUP):
            total[j * rows : (j + 1) * rows, :] = weighted(parts, factors, j)
        row = lax.broadcasted_iota(jnp.int32, (rows, width), 0)
        lane = lax.broadcasted_iota(jnp.int32, (rows, width), 1)
        addends = [
            sum(
                lax.dot_general(
                    value,
                    (lane == row + base).astype(BF),
                    (((0,), (0,)), ((), ())),
                    preferred_element_type=F32,
                )
                for value, base in ((one, 0), (other, rows))
            )[:GROUP, :]
            for one, other in zip(split(top), split(tot))
        ]
        tail = stat_tail(stat, addends)
        small = GROUP * rows // RING
        for k, out in enumerate(outs):
            target = lax.rem(place_ref[1] + k, RING)
            every = [(j * rows + base, w) for j in range(GROUP) for base, w in next_spans]
            out[side, 0, :small, :] = cut(total, target, every).astype(BF)
            out[side, 0, small:, :] = tail


def first_merge(own, ahead, behind, passed_f, passed_b, places, spans, next_spans):
    groups, part_rows, rank = own.shape
    rows = sum(width for _, width in spans)
    paired = (2, groups // 2, part_rows, rank)
    out_rows = GROUP * rows // RING + STAT_ROWS
    both = pl.BlockSpec((2, 1, part_rows, rank), lambda s, *_: (0, s, 0, 0))
    single = pl.BlockSpec((1, part_rows, rank), lambda s, *_: (s, 0, 0))
    outs = pl.pallas_call(
        functools.partial(first_kernel, spans=spans, next_spans=next_spans),
        grid_spec=pltpu.PrefetchScalarGridSpec(
            num_scalar_prefetch=1,
            grid=(groups // 2,),
            in_specs=[both] * 3 + [single] * 2,
            out_specs=[pl.BlockSpec((2, 1, out_rows, rank), lambda s, *_: (0, s, 0, 0))] * RING,
            scratch_shapes=[
                pltpu.VMEM((3, rank, 128), F32),
                pltpu.VMEM((GROUP * rows, rank), F32),
                pltpu.VMEM((STAT_ROWS, rank), F32),
            ],
        ),
        out_shape=[jax.ShapeDtypeStruct((2, groups // 2, out_rows, rank), BF)] * RING,
        compiler_params=pltpu.CompilerParams(vmem_limit_bytes=VMEM_LIMIT),
        cost_estimate=pl.CostEstimate(
            flops=6 * groups * part_rows * rank,
            bytes_accessed=8 * groups * part_rows * rank,
            transcendentals=0,
        ),
    )(
        places,
        own.reshape(paired),
        ahead.reshape(paired),
        behind.reshape(paired),
        passed_f,
        passed_b,
    )
    return [out.reshape(groups, out_rows, rank) for out in outs]


def last_kernel(place_ref, *refs, spans, total_base):
    *parts, out, columns = refs
    parts = [part.at[0] for part in parts]
    _, total, factors = combined(parts, columns, place_ref[0], spans, total_base)
    factors = [factor / total for factor in factors]
    rows = factors[0].shape[0]
    for j in range(GROUP):
        out[0, j * rows : (j + 1) * rows, :] = weighted(parts, factors, j).astype(BF)


def last_merge(parts, place, spans, total_base):
    groups, part_rows, rank = parts[0].shape
    out_rows = part_rows - STAT_ROWS
    return pl.pallas_call(
        functools.partial(last_kernel, spans=spans, total_base=total_base),
        grid_spec=pltpu.PrefetchScalarGridSpec(
            num_scalar_prefetch=1,
            grid=(groups,),
            in_specs=[pl.BlockSpec((1, part_rows, rank), lambda s, *_: (s, 0, 0))] * RING,
            out_specs=pl.BlockSpec((1, out_rows, rank), lambda s, *_: (s, 0, 0)),
            scratch_shapes=[pltpu.VMEM((RING, rank, 128), F32)],
        ),
        out_shape=jax.ShapeDtypeStruct((groups, out_rows, rank), BF),
        compiler_params=pltpu.CompilerParams(vmem_limit_bytes=VMEM_LIMIT),
        cost_estimate=pl.CostEstimate(
            flops=8 * groups * part_rows * rank,
            bytes_accessed=10 * groups * part_rows * rank,
            transcendentals=0,
        ),
    )(place, *parts)


def per_device(
    queries,
    prompt_latent,
    new_latent,
    blocks,
    value_up,
    w_out,
    residual,
    norm_gain,
    router,
    routes,
    bucket_slots,
    w_gate,
    w_up,
    w_down,
):
    n_ctx = lax.axis_size("ctx")
    n_ep = lax.axis_size("ep")
    devices = n_ctx * n_ep
    ctx_place = lax.axis_index("ctx")
    ep_place = lax.axis_index("ep")
    core = ep_place % 2
    swap = [(i, i ^ 1) for i in range(n_ep)]
    samples, step_count, head_count, latent = queries.shape
    rank = value_up.shape[1]
    value_width = value_up.shape[2]
    own_heads = head_count // n_ctx
    tokens_here = samples * step_count
    model_width = w_out.shape[1]
    part = model_width // n_ep

    w_rows = lax.all_gather(
        w_out,
        "ep",
        axis=0,
        axis_index_groups=[list(range(k, n_ep, 2)) for k in range(2)],
        tiled=True,
    )
    z_place, y_place = ctx_place // RING, ctx_place % RING
    ctx_axes = jnp.stack([z_place, y_place])

    inward = [(e * n_ctx + c, c * n_ep + e) for e in range(n_ep) for c in range(n_ctx)]
    outward = [(there, here) for here, there in inward]
    everywhere = ("ctx", "ep")
    residual, routes, bucket_slots = (
        lax.ppermute(value, everywhere, inward) for value in (residual, routes, bucket_slots)
    )

    def along_z(k):
        return [(i, (i + k * RING) % n_ctx) for i in range(n_ctx)]

    def along_y(k):
        return [(i, i // RING * RING + (i + k) % RING) for i in range(n_ctx)]

    blk_local = prompt_latent.shape[0] // BLOCK
    shard_of = blocks // blk_local
    offset = blocks % blk_local
    is_local = (shard_of == ctx_place).astype(jnp.int32)
    position = jnp.cumsum(is_local, axis=1) - 1
    chosen = (is_local[:, :, None] == 1) & (
        position[:, :, None] == jnp.arange(CAPB)[None, None, :]
    )
    table = jnp.sum(jnp.where(chosen, offset[:, :, None], 0), axis=1)
    count = jnp.minimum(jnp.sum(is_local, axis=1), CAPB)
    own = (ctx_place == n_ctx - 1).astype(jnp.int32)
    own_rows = jnp.pad(new_latent, ((0, 0), (0, OWN_ROWS - step_count), (0, 0)))

    query_t = jnp.swapaxes(queries, 2, 3)
    per_step = head_count // RING
    by_z = [(t * head_count, per_step) for t in range(step_count)]
    by_y = [
        (t * head_count + z * per_step, own_heads) for t in range(step_count) for z in range(RING)
    ]
    second = [(t * per_step, own_heads) for t in range(step_count)]
    part_rows = step_count * per_step

    def send(forward, backward, along):
        return lax.ppermute(forward, "ctx", along(1)), lax.ppermute(backward, "ctx", along(3))

    z_first, y_first = ctx_axes, ctx_axes[::-1]
    own_a, forward_a, backward_a, held_a = attend(
        query_t, prompt_latent, own_rows, count, table, jnp.stack([own, z_place]), rank, 0, by_z
    )
    ahead_a, behind_a = send(forward_a, backward_a, along_z)
    own_b, forward_b, backward_b, held_b = attend(
        query_t, prompt_latent, own_rows, count, table, jnp.stack([own, y_place]), rank, 1, by_y
    )
    ahead_b, behind_b = send(forward_b, backward_b, along_y)
    passed_a = relay(held_a, ahead_a, behind_a, z_first, by_z)
    passed_fa, passed_ba = send(*passed_a, along_z)
    passed_b = relay(held_b, ahead_b, behind_b, y_first, by_y)
    passed_fb, passed_bb = send(*passed_b, along_y)

    value_up, _ = lax.optimization_barrier((value_up, passed_b[0]))
    own_up = lax.all_to_all(
        jnp.broadcast_to(value_up, (n_ep,) + value_up.shape[1:]),
        "ep",
        split_axis=0,
        concat_axis=0,
        tiled=True,
    )
    own_a, own_up = lax.optimization_barrier((own_a, own_up))

    next_a = first_merge(
        own_a, ahead_a, behind_a, passed_fa, passed_ba, z_first, by_z, second
    )
    next_b = first_merge(
        own_b, ahead_b, behind_b, passed_fb, passed_bb, y_first, by_y, second
    )
    got_a = [next_a[0]] + [lax.ppermute(next_a[k], "ctx", along_y(k)) for k in (1, 2, 3)]
    got_b = [next_b[0]] + [lax.ppermute(next_b[k], "ctx", along_z(k)) for k in (1, 2, 3)]
    latent_a = last_merge(got_a, y_first, second, part_rows)
    latent_b = last_merge(got_b, z_first, second, part_rows)
    latent_out = jnp.concatenate([latent_a, latent_b], axis=0)
    latent_out = latent_out.reshape(samples, step_count, own_heads, rank)
    head_values = jnp.einsum(
        "sthr,hrv->sthv", latent_out, own_up, preferred_element_type=F32
    ).astype(BF)
    head_values = head_values.reshape(tokens_here, own_heads // 2, 2, value_width)

    def pick(value, index, axis):
        return lax.dynamic_index_in_dim(value, index, axis, keepdims=False)

    kept = pick(head_values, core, 2)
    given = lax.ppermute(pick(head_values, 1 - core, 2), "ep", swap)
    head_flat = jnp.where(core == 0, jnp.stack([kept, given]), jnp.stack([given, kept]))
    theirs = jnp.dot(
        pick(head_flat, 1 - core, 0).reshape(tokens_here, -1), w_rows, preferred_element_type=F32
    ).astype(BF)
    theirs = lax.ppermute(theirs, "ep", swap)
    ours = jnp.dot(
        pick(head_flat, core, 0).reshape(tokens_here, -1), w_rows, preferred_element_type=F32
    )
    projected = (ours + theirs.astype(F32)).astype(BF)
    tok_dev = residual.shape[0]
    projected = lax.all_to_all(
        projected.reshape(n_ctx, tok_dev, model_width),
        "ctx",
        split_axis=0,
        concat_axis=0,
        tiled=True,
    )
    attention = jnp.sum(projected.astype(F32), axis=0)

    hidden_state = (residual.astype(F32) + attention).astype(BF)
    hidden_wide = hidden_state.astype(F32)
    mean_square = jnp.mean(hidden_wide * hidden_wide, axis=1, keepdims=True)
    normed = (hidden_wide * lax.rsqrt(mean_square + 1e-06) * norm_gain).astype(BF)
    affinity = jax.nn.sigmoid(jnp.dot(normed, router, preferred_element_type=F32))
    experts_all = router.shape[1]
    experts = jnp.arange(experts_all)
    picked = (routes[:, :, None] == experts[None, None, :]).astype(F32)
    picked_aff = jnp.sum(picked * affinity[:, None, :], axis=2)
    combine_w = 2.5 * picked_aff / jnp.sum(picked_aff, axis=1, keepdims=True)
    kept_route = bucket_slots < CAP
    hits = picked[:, :, :, None] * (
        (bucket_slots[:, :, None] == jnp.arange(CAP)[None, None, :]) & kept_route[:, :, None]
    ).astype(F32)[:, :, None, :]
    slot_hit = jnp.sum(hits, axis=1).reshape(tok_dev, experts_all * CAP)
    slot_weight = jnp.sum(hits * combine_w[:, :, None, None], axis=1)
    slot_weight = lax.ppermute(
        slot_weight.reshape(tok_dev, experts_all * CAP), everywhere, outward
    ).reshape(tok_dev, experts_all, CAP)
    hidden_wide = lax.ppermute(hidden_state, everywhere, outward).astype(F32)

    outgoing = jnp.einsum(
        "te,td->ed", slot_hit.astype(BF), normed, preferred_element_type=F32
    ).astype(BF)
    chips = n_ep // CAP
    copies = jnp.broadcast_to(
        outgoing.reshape(n_ctx, 1, CAP, n_ep, part), (n_ctx, chips, CAP, n_ep, part)
    ).reshape(devices, n_ep, part)
    arrived = lax.all_to_all(copies, ("ctx", "ep"), split_axis=0, concat_axis=0, tiled=True)
    arrived = arrived.reshape(devices, model_width)
    sibling = lax.ppermute(arrived, "ep", swap)
    rows = jnp.concatenate([arrived, sibling], axis=0)
    gate_act = jnp.dot(rows, w_gate[0], preferred_element_type=F32)
    up_act = jnp.dot(rows, w_up[0], preferred_element_type=F32)
    inner_act = (jax.nn.silu(gate_act) * up_act).astype(BF)
    theirs = jnp.dot(inner_act[devices:], w_down[0], preferred_element_type=F32).astype(BF)
    theirs = lax.ppermute(theirs, "ep", swap)
    ours = jnp.dot(inner_act[:devices], w_down[0], preferred_element_type=F32)
    pair_out = (ours + theirs.astype(F32)).astype(BF).reshape(n_ctx, n_ep, n_ep, part)
    pair_out = pair_out.swapaxes(0, 1).reshape(devices, n_ep, part)
    returned = lax.all_to_all(pair_out, ("ctx", "ep"), split_axis=0, concat_axis=0, tiled=True)
    expert_rows = jnp.sum(
        returned.reshape(n_ctx, chips, CAP, n_ep, part).astype(F32), axis=1
    ).reshape(1, experts_all, CAP, n_ep, part)
    moe_sum = jnp.sum(slot_weight[:, :, :, None, None] * expert_rows, axis=(1, 2))
    return (hidden_wide + moe_sum.reshape(tok_dev, model_width)).astype(BF)


def solution(mesh):
    placed = (
        P("ep", None, None, None),
        P("ctx", None),
        P("ep", None, None),
        P("ep", None),
        P(("ctx", "ep"), None, None),
        P(("ctx", "ep"), None),
        P(("ctx", "ep"), None),
        P(),
        P(),
        P(("ctx", "ep"), None),
        P(("ctx", "ep"), None),
        P("ctx", None, "ep"),
        P("ctx", None, "ep"),
        P("ctx", "ep", None),
    )
    return jax.shard_map(
        per_device, mesh=mesh, in_specs=placed, out_specs=P(("ctx", "ep"), None), check_vma=False
    )
```

time: 318 us -> 256 us (0.81)
  blocking collectives: 72.9 us -> 37.4 us
  starting transfers between devices: 35.8 us -> 65.1 us
  local copies, waits for them, and re-layouts: 43 us -> 19.4 us
  waiting for transfers between devices: 74.2 us -> 58.9 us
  matrix products: 25.1 us -> 12 us
    ppermute x0 -> x20, starting transfers between devices: none -> 47.1 us  [the longest x4 11.4 us: send(): lax.ppermute(backward, 'ctx', along(3))]
    all_to_all x1 -> x0, blocking collectives: 41 us -> none  [per_device(): lax.all_to_all(w_cols, 'ep', split_axis=0, concat_axis=0, tiled=True)]
    all_to_all x3 -> x2, waiting for transfers between devices: 38.9 us -> 0.01 us  [the longest x1 0.01 us: per_device(): lax.all_to_all(jnp.broadcast_to(value_up, (n_ep,) + value_up.shape[1:]),...]
    ppermute x0 -> x20, waiting for transfers between devices: none -> 38.5 us  [the longest x4 8.36 us: send(): lax.ppermute(forward, 'ctx', along(1))]
    all_to_all x3 -> x2, starting transfers between devices: 30.6 us -> 12.3 us  [the longest x1 7.5 us: per_device(): lax.all_to_all(projected.reshape(n_ctx, tok_dev, model_width), 'ctx', spl...]
    all_to_all x1, waiting for transfers between devices: 27.8 us -> 10.9 us  [per_device(): lax.all_to_all(pair_out, ('ctx', 'ep'), split_axis=0, concat_axis=0, tile...]
    unnamed x32 -> x49, local copies, waits for them, and re-layouts: 28.3 us -> 14.1 us
    dot_general x2 -> x3, matrix products: 21 us -> 7.94 us  [the longest x1 4.62 us: per_device(): jnp.dot(pick(head_flat, 1 - core, 0).reshape(tokens_here, -1), w_rows, pr...]
  transfers between devices with their start and end apart: 8 -> 27, of which waited for: 5 -> 15; matrix products, arithmetic and copies ran while one was open for 18% -> 4% of each run, Pallas kernels for 14% -> 17%
where the time goes in v2:
time: 256 us; the launch traced here: 255 us
  starting transfers between devices  65.1 us (25%)
  waiting for transfers between devices  58.9 us (23%)
  Pallas kernels  44 us (17%)
  blocking collectives  37.4 us (15%)
  local copies, waits for them, and re-layouts  19.4 us (8%)
  between operations  13.9 us (5%)
  matrix products  12 us (5%)
  other arithmetic  4.13 us (2%)
    all_to_all x1, blocking collectives, per_device(): lax.all_to_all(copies, ('ctx', 'ep'), split_axis=0, concat_axis=0, tiled=...  37.4 us
    pallas_call x2, Pallas kernels, attend(): pl.pallas_call(functools.partial(attend_kernel, spans=spans, offset=half...  20.3 us
    unnamed x49, local copies, waits for them, and re-layouts  14.1 us
    ppermute x4, starting transfers between devices, send(): lax.ppermute(backward, 'ctx', along(3))  11.4 us
    all_to_all x1, waiting for transfers between devices, per_device(): lax.all_to_all(pair_out, ('ctx', 'ep'), split_axis=0, concat_axis=0, tile...  10.9 us
    ppermute x3, starting transfers between devices, per_device(): lax.ppermute(value, everywhere, inward)  10.9 us
    pallas_call x2, Pallas kernels, first_merge(): pl.pallas_call(functools.partial(first_kernel, spans=spans, next_spans=ne...  10.5 us
    ppermute x4, waiting for transfers between devices, send(): lax.ppermute(forward, 'ctx', along(1))  8.36 us
  transfers between devices with their start and end apart: 27, of which 15 were waited for; matrix products, arithmetic and copies ran while one was open for 4% of the time, Pallas kernels for 17%

profile of v2, /device:TPU:1, one launch (start us, length us, event | category | flops | bytes accessed | tf_op | source)
XLA Modules:
  0.0 254.9 jit_solution(16928110439718437125)
XLA Ops:
  8.3 3.1 %copy.43.prompt_ref = bf16[2048,576]{1,0:T(8,128)(2,1)S(1)} copy(bf16[2048,576]{0,1:T(8,128)(2,1)} %param.15) | data formatting | bytes 4718592 | tf_op args[1]
  12.3 9.6 %shard_map.137 = (bf16[4,272,512]{2,1,0:T(8,128)(2,1)S(1)}, bf16[4,272,512]{2,1,0:T(8,128)(2,1)}, bf16[4,272,512]{2,1,0:T(8,128)(2,1)}, bf16[4,272,512]{2,1,0:T(8,128)(2,1)S(1)}) custom-call(s32[32]{0:T(128)S(1)} %broadcast_minimum_fusion.count_ref, s32[32,8]{1,0:T(8,128)S(1)} %select_reduce_fusion.table_ref, s32[2]{0:T(128)S(1)} %get-tuple-element.64.info_ref, ...), custom_call_target="tpu_custom_call" | custom-call | flops 2281701376 | bytes 17825792 | tf_op jit(solution)/shard_map/pallas_call | solution.py:108
  25.6 10.7 %shard_map.136 = (bf16[4,272,512]{2,1,0:T(8,128)(2,1)S(1)}, bf16[4,272,512]{2,1,0:T(8,128)(2,1)}, bf16[4,272,512]{2,1,0:T(8,128)(2,1)}, bf16[4,272,512]{2,1,0:T(8,128)(2,1)S(1)}) custom-call(s32[32]{0:T(128)S(1)} %broadcast_minimum_fusion.count_ref, s32[32,8]{1,0:T(8,128)S(1)} %select_reduce_fusion.table_ref, s32[2]{0:T(128)S(1)} %get-tuple-element.63.info_ref, ...), custom_call_target="tpu_custom_call" | custom-call | flops 2281701376 | bytes 17825792 | tf_op jit(solution)/shard_map/pallas_call | solution.py:108
  38.5 5.9 %collective-permute-start.4 = (bf16[4,272,512]{2,1,0:T(8,128)(2,1)}, bf16[4,272,512]{2,1,0:T(8,128)(2,1)S(1)}, u32[]{:S(2)}, u32[]{:S(2)}) collective-permute-start(bf16[4,272,512]{2,1,0:T(8,128)(2,1)} %get-tuple-element.37), channel_id=1, source_target_pairs={{0,96},{8,104},{16,112},{24,120},{32,0},{40,8},{48,16},{56,24},{64... | collective-permute-start | bytes 3342344 | tf_op jit(solution)/shard_map/ppermute | solution.py:406
  44.5 3.3 %collective-permute-done.1 = bf16[4,272,512]{2,1,0:T(8,128)(2,1)} collective-permute-done((bf16[4,272,512]{2,1,0:T(8,128)(2,1)}, bf16[4,272,512]{2,1,0:T(8,128)(2,1)}, u32[]{:S(2)}, u32[]{:S(2)}) %collective-permute-start.1) | collective-permute-done | bytes 1114144 | tf_op jit(solution)/shard_map/ppermute | solution.py:406
  47.8 5.6 %collective-permute-done.2 = bf16[4,272,512]{2,1,0:T(8,128)(2,1)} collective-permute-done((bf16[4,272,512]{2,1,0:T(8,128)(2,1)}, bf16[4,272,512]{2,1,0:T(8,128)(2,1)}, u32[]{:S(2)}, u32[]{:S(2)}) %collective-permute-start.2) | collective-permute-done | bytes 1114144 | tf_op jit(solution)/shard_map/ppermute | solution.py:406
  54.7 3.8 %shard_map.138 = (bf16[2,272,512]{2,1,0:T(8,128)(2,1)}, bf16[2,272,512]{2,1,0:T(8,128)(2,1)}) custom-call(s32[2]{0:T(128)S(1)} %rev.3.place_ref, bf16[2,2,272,512]{3,2,1,0:T(8,128)(2,1)S(1)} %bitcast.94, bf16[2,2,272,512]{3,2,1,0:T(8,128)(2,1)} %bitcast.5.ahead, bf16[2,2,272,512]{3,2,1,0:T(8,128)(2,1)} %bitcast.6.behind), custom_call_target="tpu_custom_call" | custom-call | flops 2228224 | bytes 3342336 | tf_op jit(solution)/shard_map/pallas_call | solution.py:199
  59.6 4.8 %all-to-all-start = ((bf16[8,512,128]{2,1,0:T(8,128)(2,1)}), bf16[8,512,128]{2,1,0:T(8,128)(2,1)}, u32[]{:S(2)}, u32[]{:S(2)}) async-start(bf16[8,512,128]{2,1,0:T(8,128)(2,1)} %broadcast_in_dim.23), calls=%async_computation | async-start | bytes 2097152 | tf_op jit(solution)/shard_map/all_to_all | solution.py:423
  70.2 2.8 %shard_map.139 = (bf16[2,272,512]{2,1,0:T(8,128)(2,1)}, bf16[2,272,512]{2,1,0:T(8,128)(2,1)}) custom-call(s32[2]{0:T(128)S(1)} %pad_add_fusion.1.place_ref, bf16[2,2,272,512]{3,2,1,0:T(8,128)(2,1)S(1)} %bitcast.93, bf16[2,2,272,512]{3,2,1,0:T(8,128)(2,1)S(1)} %bitcast.87, bf16[2,2,272,512]{3,2,1,0:T(8,128)(2,1)S(1)} %bitcast.89), custom_call_target="tpu_custom_call" | custom-call | flops 2228224 | bytes 3342336 | tf_op jit(solution)/shard_map/pallas_call | solution.py:199
  74.2 2.7 %collective-permute-start.6 = (bf16[2,272,512]{2,1,0:T(8,128)(2,1)}, bf16[2,272,512]{2,1,0:T(8,128)(2,1)}, u32[]{:S(2)}, u32[]{:S(2)}) collective-permute-start(bf16[2,272,512]{2,1,0:T(8,128)(2,1)} %get-tuple-element.40), channel_id=1, source_target_pairs={{0,96},{8,104},{16,112},{24,120},{32,0},{40,8},{48,16},{56,24},{64... | collective-permute-start | bytes 1671176 | tf_op jit(solution)/shard_map/ppermute | solution.py:406
  76.9 3.3 %collective-permute-done.10.passed_f = bf16[2,272,512]{2,1,0:T(8,128)(2,1)S(1)} collective-permute-done((bf16[2,272,512]{2,1,0:T(8,128)(2,1)}, bf16[2,272,512]{2,1,0:T(8,128)(2,1)S(1)}, u32[]{:S(2)}, u32[]{:S(2)}) %collective-permute-start.10) | collective-permute-done | bytes 557088 | tf_op jit(solution)/shard_map/ppermute | solution.py:406
  80.8 5.4 %shard_map.142 = (bf16[2,2,80,512]{3,2,1,0:T(8,128)(2,1)S(1)}, bf16[2,2,80,512]{3,2,1,0:T(8,128)(2,1)}, bf16[2,2,80,512]{3,2,1,0:T(8,128)(2,1)}, bf16[2,2,80,512]{3,2,1,0:T(8,128)(2,1)}) custom-call(s32[2]{0:T(128)S(1)} %rev.3.place_ref, bf16[2,2,272,512]{3,2,1,0:T(8,128)(2,1)S(1)} %bitcast.92, bf16[2,2,272,512]{3,2,1,0:T(8,128)(2,1)} %bitcast.5.ahead, ...), custom_call_target="tpu_custom_call" | custom-call | flops 3342336 | bytes 4456448 | tf_op jit(solution)/shard_map/pallas_call | solution.py:266
  86.1 6.1 %collective-permute-start.13 = (bf16[4,80,512]{2,1,0:T(8,128)(2,1)}, bf16[4,80,512]{2,1,0:T(8,128)(2,1)}, u32[]{:S(2)}, u32[]{:S(2)}) collective-permute-start(bf16[4,80,512]{2,1,0:T(8,128)(2,1)} %bitcast.21), channel_id=1, source_target_pairs={{0,64},{8,72},{16,80},{24,88},{32,96},{40,104},{48,112},{56,120},{... | collective-permute-start | bytes 983048 | tf_op jit(solution)/shard_map/ppermute | solution.py:439
  93.5 5.2 %shard_map.140 = (bf16[2,2,80,512]{3,2,1,0:T(8,128)(2,1)S(1)}, bf16[2,2,80,512]{3,2,1,0:T(8,128)(2,1)}, bf16[2,2,80,512]{3,2,1,0:T(8,128)(2,1)}, bf16[2,2,80,512]{3,2,1,0:T(8,128)(2,1)}) custom-call(s32[2]{0:T(128)S(1)} %pad_add_fusion.1.place_ref, bf16[2,2,272,512]{3,2,1,0:T(8,128)(2,1)S(1)} %bitcast.91, bf16[2,2,272,512]{3,2,1,0:T(8,128)(2,1)S(1)} %bitcast.88, ...), custom_call_target="tpu_custom_call" | custom-call | flops 3342336 | bytes 4456448 | tf_op jit(solution)/shard_map/pallas_call | solution.py:266
  99.5 3.5 %collective-permute-start.8 = (bf16[4,80,512]{2,1,0:T(8,128)(2,1)}, bf16[4,80,512]{2,1,0:T(8,128)(2,1)S(1)}, u32[]{:S(2)}, u32[]{:S(2)}) collective-permute-start(bf16[4,80,512]{2,1,0:T(8,128)(2,1)} %bitcast.16), channel_id=1, source_target_pairs={{0,16},{8,24},{16,0},{24,8},{32,48},{40,56},{48,32},{56,40},{64,80... | collective-permute-start | bytes 983048 | tf_op jit(solution)/shard_map/ppermute | solution.py:438
  104.1 2.3 collective-permute-done.13.refs_2_
  106.5 4.0 %shard_map.143 = bf16[4,64,512]{2,1,0:T(8,128)(2,1)S(1)} custom-call(s32[2]{0:T(128)S(1)} %pad_add_fusion.1.place_ref, bf16[4,80,512]{2,1,0:T(8,128)(2,1)S(1)} %bitcast.95, bf16[4,80,512]{2,1,0:T(8,128)(2,1)} %collective-permute-done.12.refs_1_, bf16[4,80,512]{2,1,0:T(8,128)(2,1)} %collective-permute-done.13.refs_2_, ...), custom_call_target="tpu_custom_call" | custom-call | flops 1310720 | bytes 1638400 | tf_op jit(solution)/shard_map/pallas_call | solution.py:310
  110.5 5.6 %collective-permute-done.8.refs_2_ = bf16[4,80,512]{2,1,0:T(8,128)(2,1)S(1)} collective-permute-done((bf16[4,80,512]{2,1,0:T(8,128)(2,1)}, bf16[4,80,512]{2,1,0:T(8,128)(2,1)S(1)}, u32[]{:S(2)}, u32[]{:S(2)}) %collective-permute-start.8) | collective-permute-done | bytes 327712 | tf_op jit(solution)/shard_map/ppermute | solution.py:438
  118.1 2.5 shard_map.141
  125.9 4.6 %convolution_convert_fusion.1 = bf16[64,7168]{1,0:T(8,128)(2,1)S(1)} fusion(bf16[512,7168]{1,0:T(8,128)(2,1)} %all-gather.2.cloned.1.call-done, bf16[8,8,4,128]{3,2,1,0:T(4,128)(2,1)S(1)} %bitcast.112), kind=kOutput, calls=%fused_computation.1 | convolution fusion | flops 470220800 | bytes 8323072 | tf_op jit(solution)/shard_map/dot_general | solution.py:455
  135.8 7.5 %all-to-all-start.1 = ((bf16[16,4,7168]{2,1,0:T(4,128)(2,1)}), bf16[16,4,7168]{2,1,0:T(4,128)(2,1)S(1)}, u32[]{:S(2)}, u32[]{:S(2)}) async-start(bf16[16,4,7168]{2,1,0:T(4,128)(2,1)} %reshape.169), calls=%async_computation.1 | async-start | bytes 1835008 | tf_op jit(solution)/shard_map/all_to_all | solution.py:464
  143.3 4.1 %collective-permute-start = (bf16[4,7168]{1,0:T(4,128)(2,1)S(1)}, bf16[4,7168]{1,0:T(4,128)(2,1)S(1)}, u32[]{:S(2)}, u32[]{:S(2)}) collective-permute-start(bf16[4,7168]{1,0:T(4,128)(2,1)S(1)} %copy-done.19), channel_id=1, source_target_pairs={{0,0},{1,8},{2,16},{3,24},{4,32},{5,40},{6,48},{7,56},{8,64},{9,72... | collective-permute-start | bytes 172040 | tf_op jit(solution)/shard_map/ppermute | solution.py:374
  147.4 4.9 %collective-permute-start.19 = (s32[4,8]{1,0:T(4,128)S(1)}, s32[4,8]{1,0:T(4,128)S(1)}, u32[]{:S(2)}, u32[]{:S(2)}) collective-permute-start(s32[4,8]{1,0:T(4,128)S(1)} %copy-done.20), channel_id=1, source_target_pairs={{0,0},{1,8},{2,16},{3,24},{4,32},{5,40},{6,48},{7,56},{8,64},{9,72... | collective-permute-start | bytes 392 | tf_op jit(solution)/shard_map/ppermute | solution.py:374
  154.2 5.8 %collective-permute-done.19 = s32[4,8]{1,0:T(4,128)S(1)} collective-permute-done((s32[4,8]{1,0:T(4,128)S(1)}, s32[4,8]{1,0:T(4,128)S(1)}, u32[]{:S(2)}, u32[]{:S(2)}) %collective-permute-start.19) | collective-permute-done | bytes 160 | tf_op jit(solution)/shard_map/ppermute | solution.py:374
  162.0 37.4 %all_to_all.20 = bf16[128,8,896]{2,1,0:T(8,128)(2,1)S(1)} all-to-all(bf16[128,8,896]{2,1,0:T(8,128)(2,1)S(1)} %bitcast.104), channel_id=1, replica_groups=mesh['ctx'=16,'ep'=8] {'ctx','ep'}, dimensions={0} | all-to-all | bytes 3670016 | tf_op jit(solution)/shard_map/all_to_all | solution.py:501
  200.8 3.3 %collective-permute-done.21 = bf16[128,7168]{1,0:T(8,128)(2,1)S(1)} collective-permute-done((bf16[128,7168]{1,0:T(8,128)(2,1)S(1)}, bf16[128,7168]{1,0:T(8,128)(2,1)S(1)}, u32[]{:S(2)}, u32[]{:S(2)}) %collective-permute-start.21) | collective-permute-done | bytes 1835040 | tf_op jit(solution)/shard_map/ppermute | solution.py:503
  209.4 3.4 %collective-permute-done.22 = bf16[128,7168]{1,0:T(8,128)(2,1)S(1)} collective-permute-done((bf16[128,7168]{1,0:T(8,128)(2,1)S(1)}, bf16[128,7168]{1,0:T(8,128)(2,1)S(1)}, u32[]{:S(2)}, u32[]{:S(2)}) %collective-permute-start.22) | collective-permute-done | bytes 1835040 | tf_op jit(solution)/shard_map/ppermute | solution.py:509
  215.0 3.8 %all-to-all-start.3 = ((bf16[128,8,896]{2,1,0:T(8,128)(2,1)}), bf16[128,8,896]{2,1,0:T(8,128)(2,1)S(1)}, u32[]{:S(2)}, u32[]{:S(2)}) async-start(bf16[128,8,896]{2,1,0:T(8,128)(2,1)} %bitcast.38), calls=%async_computation.3 | async-start | bytes 3670016 | tf_op jit(solution)/shard_map/all_to_all | solution.py:513
  219.0 5.2 %collective-permute-start.20 = (f32[4,32]{0,1:T(8,128)S(1)}, f32[4,32]{0,1:T(8,128)S(1)}, u32[]{:S(2)}, u32[]{:S(2)}) collective-permute-start(f32[4,32]{0,1:T(8,128)S(1)} %bitcast.119), channel_id=1, source_target_pairs={{0,0},{8,1},{16,2},{24,3},{32,4},{40,5},{48,6},{56,7},{64,8},{72,9... | collective-permute-start | bytes 1544 | tf_op jit(solution)/shard_map/ppermute | solution.py:489
  224.1 3.3 %collective-permute-start.17 = (bf16[4,7168]{1,0:T(4,128)(2,1)S(1)}, bf16[4,7168]{1,0:T(4,128)(2,1)S(1)}, u32[]{:S(2)}, u32[]{:S(2)}) collective-permute-start(bf16[4,7168]{1,0:T(4,128)(2,1)S(1)} %get-tuple-element.56), channel_id=1, source_target_pairs={{0,0},{8,1},{16,2},{24,3},{32,4},{40,5},{48,6},{56,7},{64,8},{72,9... | collective-permute-start | bytes 172040 | tf_op jit(solution)/shard_map/ppermute | solution.py:492
  227.4 8.3 %collective-permute-done.20 = f32[4,32]{0,1:T(8,128)S(1)} collective-permute-done((f32[4,32]{0,1:T(8,128)S(1)}, f32[4,32]{0,1:T(8,128)S(1)}, u32[]{:S(2)}, u32[]{:S(2)}) %collective-permute-start.20) | collective-permute-done | bytes 544 | tf_op jit(solution)/shard_map/ppermute | solution.py:489
  235.9 10.9 %all-to-all-done.3 = bf16[128,8,896]{2,1,0:T(8,128)(2,1)S(1)} async-done(((bf16[128,8,896]{2,1,0:T(8,128)(2,1)}), bf16[128,8,896]{2,1,0:T(8,128)(2,1)S(1)}, u32[]{:S(2)}, u32[]{:S(2)}) %all-to-all-start.3) | async-done | bytes 1835040 | tf_op jit(solution)/shard_map/all_to_all | solution.py:513
  (129 shorter events, 48.4 us)
Async XLA Ops:
  6.5 154.1 %copy-start = (bf16[7168,16]{0,1:T(8,128)(2,1)S(1)}, bf16[7168,16]{0,1:T(8,128)(2,1)}, u32[]{:S(2)}) copy-start(bf16[7168,16]{0,1:T(8,128)(2,1)} %param.22) | copy-start | bytes 688132
  6.5 119.3 %all-gather.2.cloned.1.call-start = ((), (), s32[]{:S(2)}) async-start(), calls=%async_computation.4 | async-start | bytes 9175040 | tf_op jit(solution)/shard_map/all_gather | solution.py:360
  22.9 24.9 %collective-permute-start.1 = (bf16[4,272,512]{2,1,0:T(8,128)(2,1)}, bf16[4,272,512]{2,1,0:T(8,128)(2,1)}, u32[]{:S(2)}, u32[]{:S(2)}) collective-permute-start(bf16[4,272,512]{2,1,0:T(8,128)(2,1)} %get-tuple-element.30), channel_id=1, source_target_pairs={{0,8},{8,16},{16,24},{24,0},{32,40},{40,48},{48,56},{56,32},{64,72... | collective-permute-start | bytes 3342344 | tf_op jit(solution)/shard_map/ppermute | solution.py:406
  23.8 29.6 %collective-permute-start.2 = (bf16[4,272,512]{2,1,0:T(8,128)(2,1)}, bf16[4,272,512]{2,1,0:T(8,128)(2,1)}, u32[]{:S(2)}, u32[]{:S(2)}) collective-permute-start(bf16[4,272,512]{2,1,0:T(8,128)(2,1)} %get-tuple-element.31), channel_id=1, source_target_pairs={{0,24},{8,0},{16,8},{24,16},{32,56},{40,32},{48,40},{56,48},{64,88... | collective-permute-start | bytes 3342344 | tf_op jit(solution)/shard_map/ppermute | solution.py:406
  25.6 32.9 %copy-start.13 = (bf16[1,512,128]{2,1,0:T(8,128)(2,1)S(1)}, bf16[1,512,128]{2,1,0:T(8,128)(2,1)}, u32[]{:S(2)}) copy-start(bf16[1,512,128]{2,1,0:T(8,128)(2,1)} %param.18) | copy-start | bytes 393220
  38.4 30.6 %collective-permute-start.3 = (bf16[4,272,512]{2,1,0:T(8,128)(2,1)}, bf16[4,272,512]{2,1,0:T(8,128)(2,1)S(1)}, u32[]{:S(2)}, u32[]{:S(2)}) collective-permute-start(bf16[4,272,512]{2,1,0:T(8,128)(2,1)} %get-tuple-element.36), channel_id=1, source_target_pairs={{0,32},{8,40},{16,48},{24,56},{32,64},{40,72},{48,80},{56,88},{64,... | collective-permute-start | bytes 3342344 | tf_op jit(solution)/shard_map/ppermute | solution.py:406
  38.5 30.4 %collective-permute-start.4 = (bf16[4,272,512]{2,1,0:T(8,128)(2,1)}, bf16[4,272,512]{2,1,0:T(8,128)(2,1)S(1)}, u32[]{:S(2)}, u32[]{:S(2)}) collective-permute-start(bf16[4,272,512]{2,1,0:T(8,128)(2,1)} %get-tuple-element.37), channel_id=1, source_target_pairs={{0,96},{8,104},{16,112},{24,120},{32,0},{40,8},{48,16},{56,24},{64... | collective-permute-start | bytes 3342344 | tf_op jit(solution)/shard_map/ppermute | solution.py:406
  59.6 32.6 %all-to-all-start = ((bf16[8,512,128]{2,1,0:T(8,128)(2,1)}), bf16[8,512,128]{2,1,0:T(8,128)(2,1)}, u32[]{:S(2)}, u32[]{:S(2)}) async-start(bf16[8,512,128]{2,1,0:T(8,128)(2,1)} %broadcast_in_dim.23), calls=%async_computation | async-start | bytes 2097152 | tf_op jit(solution)/shard_map/all_to_all | solution.py:423
  64.5 16.3 %copy-start.4 = (bf16[4,272,512]{2,1,0:T(8,128)(2,1)S(1)}, bf16[4,272,512]{2,1,0:T(8,128)(2,1)}, u32[]{:S(2)}) copy-start(bf16[4,272,512]{2,1,0:T(8,128)(2,1)} %copy-done.3) | copy-start | bytes 3342340
  64.5 15.7 %collective-permute-start.10 = (bf16[2,272,512]{2,1,0:T(8,128)(2,1)}, bf16[2,272,512]{2,1,0:T(8,128)(2,1)S(1)}, u32[]{:S(2)}, u32[]{:S(2)}) collective-permute-start(bf16[2,272,512]{2,1,0:T(8,128)(2,1)} %get-tuple-element.32), channel_id=1, source_target_pairs={{0,8},{8,16},{16,24},{24,0},{32,40},{40,48},{48,56},{56,32},{64,72... | collective-permute-start | bytes 1671176 | tf_op jit(solution)/shard_map/ppermute | solution.py:406
  66.0 14.7 %collective-permute-start.11 = (bf16[2,272,512]{2,1,0:T(8,128)(2,1)}, bf16[2,272,512]{2,1,0:T(8,128)(2,1)S(1)}, u32[]{:S(2)}, u32[]{:S(2)}) collective-permute-start(bf16[2,272,512]{2,1,0:T(8,128)(2,1)} %get-tuple-element.46), channel_id=1, source_target_pairs={{0,24},{8,0},{16,8},{24,16},{32,56},{40,32},{48,40},{56,48},{64,88... | collective-permute-start | bytes 1671176 | tf_op jit(solution)/shard_map/ppermute | solution.py:406
  73.0 19.3 %collective-permute-start.5 = (bf16[2,272,512]{2,1,0:T(8,128)(2,1)}, bf16[2,272,512]{2,1,0:T(8,128)(2,1)S(1)}, u32[]{:S(2)}, u32[]{:S(2)}) collective-permute-start(bf16[2,272,512]{2,1,0:T(8,128)(2,1)} %get-tuple-element.39), channel_id=1, source_target_pairs={{0,32},{8,40},{16,48},{24,56},{32,64},{40,72},{48,80},{56,88},{64,... | collective-permute-start | bytes 1671176 | tf_op jit(solution)/shard_map/ppermute | solution.py:406
  74.2 18.1 %collective-permute-start.6 = (bf16[2,272,512]{2,1,0:T(8,128)(2,1)}, bf16[2,272,512]{2,1,0:T(8,128)(2,1)}, u32[]{:S(2)}, u32[]{:S(2)}) collective-permute-start(bf16[2,272,512]{2,1,0:T(8,128)(2,1)} %get-tuple-element.40), channel_id=1, source_target_pairs={{0,96},{8,104},{16,112},{24,120},{32,0},{40,8},{48,16},{56,24},{64... | collective-permute-start | bytes 1671176 | tf_op jit(solution)/shard_map/ppermute | solution.py:406
  86.1 16.8 %collective-permute-start.12 = (bf16[4,80,512]{2,1,0:T(8,128)(2,1)}, bf16[4,80,512]{2,1,0:T(8,128)(2,1)}, u32[]{:S(2)}, u32[]{:S(2)}) collective-permute-start(bf16[4,80,512]{2,1,0:T(8,128)(2,1)} %bitcast.20), channel_id=1, source_target_pairs={{0,32},{8,40},{16,48},{24,56},{32,64},{40,72},{48,80},{56,88},{64,... | collective-permute-start | bytes 983048 | tf_op jit(solution)/shard_map/ppermute | solution.py:439
  86.1 20.3 %collective-permute-start.13 = (bf16[4,80,512]{2,1,0:T(8,128)(2,1)}, bf16[4,80,512]{2,1,0:T(8,128)(2,1)}, u32[]{:S(2)}, u32[]{:S(2)}) collective-permute-start(bf16[4,80,512]{2,1,0:T(8,128)(2,1)} %bitcast.21), channel_id=1, source_target_pairs={{0,64},{8,72},{16,80},{24,88},{32,96},{40,104},{48,112},{56,120},{... | collective-permute-start | bytes 983048 | tf_op jit(solution)/shard_map/ppermute | solution.py:439
  92.3 14.2 %collective-permute-start.14 = (bf16[4,80,512]{2,1,0:T(8,128)(2,1)}, bf16[4,80,512]{2,1,0:T(8,128)(2,1)}, u32[]{:S(2)}, u32[]{:S(2)}) collective-permute-start(bf16[4,80,512]{2,1,0:T(8,128)(2,1)} %bitcast.22), channel_id=1, source_target_pairs={{0,96},{8,104},{16,112},{24,120},{32,0},{40,8},{48,16},{56,24},{64... | collective-permute-start | bytes 983048 | tf_op jit(solution)/shard_map/ppermute | solution.py:439
  99.4 11.1 %collective-permute-start.7 = (bf16[4,80,512]{2,1,0:T(8,128)(2,1)}, bf16[4,80,512]{2,1,0:T(8,128)(2,1)S(1)}, u32[]{:S(2)}, u32[]{:S(2)}) collective-permute-start(bf16[4,80,512]{2,1,0:T(8,128)(2,1)} %bitcast.15), channel_id=1, source_target_pairs={{0,8},{8,16},{16,24},{24,0},{32,40},{40,48},{48,56},{56,32},{64,72... | collective-permute-start | bytes 983048 | tf_op jit(solution)/shard_map/ppermute | solution.py:438
  99.5 16.7 %collective-permute-start.8 = (bf16[4,80,512]{2,1,0:T(8,128)(2,1)}, bf16[4,80,512]{2,1,0:T(8,128)(2,1)S(1)}, u32[]{:S(2)}, u32[]{:S(2)}) collective-permute-start(bf16[4,80,512]{2,1,0:T(8,128)(2,1)} %bitcast.16), channel_id=1, source_target_pairs={{0,16},{8,24},{16,0},{24,8},{32,48},{40,56},{48,32},{56,40},{64,80... | collective-permute-start | bytes 983048 | tf_op jit(solution)/shard_map/ppermute | solution.py:438
  103.0 14.2 %collective-permute-start.9 = (bf16[4,80,512]{2,1,0:T(8,128)(2,1)}, bf16[4,80,512]{2,1,0:T(8,128)(2,1)S(1)}, u32[]{:S(2)}, u32[]{:S(2)}) collective-permute-start(bf16[4,80,512]{2,1,0:T(8,128)(2,1)} %bitcast.17), channel_id=1, source_target_pairs={{0,24},{8,0},{16,8},{24,16},{32,56},{40,32},{48,40},{56,48},{64,88... | collective-permute-start | bytes 983048 | tf_op jit(solution)/shard_map/ppermute | solution.py:438
  123.1 2.7 %collective-permute-start.15 = (bf16[64,4,128]{2,0,1:T(8,128)(2,1)S(1)}, bf16[64,4,128]{2,0,1:T(8,128)(2,1)S(1)}, u32[]{:S(2)}, u32[]{:S(2)}) collective-permute-start(bf16[64,4,128]{2,0,1:T(8,128)(2,1)S(1)} %bitcast.115), channel_id=1, source_target_pairs={{0,1},{1,0},{2,3},{3,2},{4,5},{5,4},{6,7},{7,6},{8,9},{9,8},{10,11... | collective-permute-start | bytes 196616 | tf_op jit(solution)/shard_map/ppermute | solution.py:453
  130.5 2.6 %collective-permute-start.16 = (bf16[64,7168]{1,0:T(8,128)(2,1)S(1)}, bf16[64,7168]{1,0:T(8,128)(2,1)S(1)}, u32[]{:S(2)}, u32[]{:S(2)}) collective-permute-start(bf16[64,7168]{1,0:T(8,128)(2,1)S(1)} %convolution_convert_fusion.1), channel_id=1, source_target_pairs={{0,1},{1,0},{2,3},{3,2},{4,5},{5,4},{6,7},{7,6},{8,9},{9,8},{10,11... | collective-permute-start | bytes 2752520 | tf_op jit(solution)/shard_map/ppermute | solution.py:458
  134.5 17.8 %copy-start.21 = (s32[4,8]{1,0:T(4,128)S(1)}, s32[4,8]{1,0:T(4,128)}, u32[]{:S(2)}) copy-start(s32[4,8]{1,0:T(4,128)} %param.23) | copy-start | bytes 388
  134.5 26.2 %copy-start.16 = (f32[7168]{0:T(1024)S(1)}, f32[7168]{0:T(1024)}, u32[]{:S(2)}) copy-start(f32[7168]{0:T(1024)} %param.21) | copy-start | bytes 86020
  135.8 24.3 %all-to-all-start.1 = ((bf16[16,4,7168]{2,1,0:T(4,128)(2,1)}), bf16[16,4,7168]{2,1,0:T(4,128)(2,1)S(1)}, u32[]{:S(2)}, u32[]{:S(2)}) async-start(bf16[16,4,7168]{2,1,0:T(4,128)(2,1)} %reshape.169), calls=%async_computation.1 | async-start | bytes 1835008 | tf_op jit(solution)/shard_map/all_to_all | solution.py:464
  143.3 17.2 %collective-permute-start = (bf16[4,7168]{1,0:T(4,128)(2,1)S(1)}, bf16[4,7168]{1,0:T(4,128)(2,1)S(1)}, u32[]{:S(2)}, u32[]{:S(2)}) collective-permute-start(bf16[4,7168]{1,0:T(4,128)(2,1)S(1)} %copy-done.19), channel_id=1, source_target_pairs={{0,0},{1,8},{2,16},{3,24},{4,32},{5,40},{6,48},{7,56},{8,64},{9,72... | collective-permute-start | bytes 172040 | tf_op jit(solution)/shard_map/ppermute | solution.py:374
  147.4 12.6 %collective-permute-start.19 = (s32[4,8]{1,0:T(4,128)S(1)}, s32[4,8]{1,0:T(4,128)S(1)}, u32[]{:S(2)}, u32[]{:S(2)}) collective-permute-start(s32[4,8]{1,0:T(4,128)S(1)} %copy-done.20), channel_id=1, source_target_pairs={{0,0},{1,8},{2,16},{3,24},{4,32},{5,40},{6,48},{7,56},{8,64},{9,72... | collective-permute-start | bytes 392 | tf_op jit(solution)/shard_map/ppermute | solution.py:374
  152.3 7.7 %collective-permute-start.18 = (s32[4,8]{1,0:T(4,128)S(1)}, s32[4,8]{1,0:T(4,128)S(1)}, u32[]{:S(2)}, u32[]{:S(2)}) collective-permute-start(s32[4,8]{1,0:T(4,128)S(1)} %copy-done.21), channel_id=1, source_target_pairs={{0,0},{1,8},{2,16},{3,24},{4,32},{5,40},{6,48},{7,56},{8,64},{9,72... | collective-permute-start | bytes 392 | tf_op jit(solution)/shard_map/ppermute | solution.py:374
  199.7 4.4 %collective-permute-start.21 = (bf16[128,7168]{1,0:T(8,128)(2,1)S(1)}, bf16[128,7168]{1,0:T(8,128)(2,1)S(1)}, u32[]{:S(2)}, u32[]{:S(2)}) collective-permute-start(bf16[128,7168]{1,0:T(8,128)(2,1)S(1)} %bitcast.100), channel_id=1, source_target_pairs={{0,1},{1,0},{2,3},{3,2},{4,5},{5,4},{6,7},{7,6},{8,9},{9,8},{10,11... | collective-permute-start | bytes 5505032 | tf_op jit(solution)/shard_map/ppermute | solution.py:503
  209.0 3.9 %collective-permute-start.22 = (bf16[128,7168]{1,0:T(8,128)(2,1)S(1)}, bf16[128,7168]{1,0:T(8,128)(2,1)S(1)}, u32[]{:S(2)}, u32[]{:S(2)}) collective-permute-start(bf16[128,7168]{1,0:T(8,128)(2,1)S(1)} %convolution_convert_fusion), channel_id=1, source_target_pairs={{0,1},{1,0},{2,3},{3,2},{4,5},{5,4},{6,7},{7,6},{8,9},{9,8},{10,11... | collective-permute-start | bytes 5505032 | tf_op jit(solution)/shard_map/ppermute | solution.py:509
  215.0 31.7 %all-to-all-start.3 = ((bf16[128,8,896]{2,1,0:T(8,128)(2,1)}), bf16[128,8,896]{2,1,0:T(8,128)(2,1)S(1)}, u32[]{:S(2)}, u32[]{:S(2)}) async-start(bf16[128,8,896]{2,1,0:T(8,128)(2,1)} %bitcast.38), calls=%async_computation.3 | async-start | bytes 3670016 | tf_op jit(solution)/shard_map/all_to_all | solution.py:513
  219.0 16.7 %collective-permute-start.20 = (f32[4,32]{0,1:T(8,128)S(1)}, f32[4,32]{0,1:T(8,128)S(1)}, u32[]{:S(2)}, u32[]{:S(2)}) collective-permute-start(f32[4,32]{0,1:T(8,128)S(1)} %bitcast.119), channel_id=1, source_target_pairs={{0,0},{8,1},{16,2},{24,3},{32,4},{40,5},{48,6},{56,7},{64,8},{72,9... | collective-permute-start | bytes 1544 | tf_op jit(solution)/shard_map/ppermute | solution.py:489
  224.1 23.3 %collective-permute-start.17 = (bf16[4,7168]{1,0:T(4,128)(2,1)S(1)}, bf16[4,7168]{1,0:T(4,128)(2,1)S(1)}, u32[]{:S(2)}, u32[]{:S(2)}) collective-permute-start(bf16[4,7168]{1,0:T(4,128)(2,1)S(1)} %get-tuple-element.56), channel_id=1, source_target_pairs={{0,0},{8,1},{16,2},{24,3},{32,4},{40,5},{48,6},{56,7},{64,8},{72,9... | collective-permute-start | bytes 172040 | tf_op jit(solution)/shard_map/ppermute | solution.py:492
  (17 other events, 69.4 us)
Sparse Core Ops, SparseCore 0:
  9.0 88.7 all-gather.1

commit v3 on v2

--- a/solution.py
+++ b/solution.py
@@ -14,7 +14,8 @@
 GROUP = 4
 RING = 4
 STAT_ROWS = 16
-VMEM_LIMIT = 40 * 1024 * 1024
+ATTEND_VMEM = 44 * 1024 * 1024
+MERGE_VMEM = 12 * 1024 * 1024
 OWN_ROWS = 16
 
 score_scale = 192.0 ** (-0.5)
@@ -123,8 +124,8 @@
                 pltpu.VMEM((GROUP + STAT_ROWS, 2 * rows), F32),
             ],
         ),
-        out_shape=[jax.ShapeDtypeStruct((groups, part_rows, rank), BF)] * RING,
-        compiler_params=pltpu.CompilerParams(vmem_limit_bytes=VMEM_LIMIT),
+        out_shape=[pltpu.HBM((groups, part_rows, rank), BF)] * RING,
+        compiler_params=pltpu.CompilerParams(vmem_limit_bytes=ATTEND_VMEM),
         cost_estimate=pl.CostEstimate(
             flops=4 * samples * rows * FEW * BLOCK * (latent + rank),
             bytes_accessed=4 * samples * rows * (latent + rank),
@@ -209,7 +210,7 @@
             ],
         ),
         out_shape=[jax.ShapeDtypeStruct((groups // 2, part_rows, rank), BF)] * 2,
-        compiler_params=pltpu.CompilerParams(vmem_limit_bytes=VMEM_LIMIT),
+        compiler_params=pltpu.CompilerParams(vmem_limit_bytes=MERGE_VMEM),
         cost_estimate=pl.CostEstimate(
             flops=4 * groups * part_rows * rank,
             bytes_accessed=6 * groups * part_rows * rank,
@@ -277,7 +278,7 @@
             ],
         ),
         out_shape=[jax.ShapeDtypeStruct((2, groups // 2, out_rows, rank), BF)] * RING,
-        compiler_params=pltpu.CompilerParams(vmem_limit_bytes=VMEM_LIMIT),
+        compiler_params=pltpu.CompilerParams(vmem_limit_bytes=MERGE_VMEM),
         cost_estimate=pl.CostEstimate(
             flops=6 * groups * part_rows * rank,
             bytes_accessed=8 * groups * part_rows * rank,
@@ -295,35 +296,40 @@
 
 
 def last_kernel(place_ref, *refs, spans, total_base):
-    *parts, out, columns = refs
+    *parts, kept, given, columns = refs
     parts = [part.at[0] for part in parts]
     _, total, factors = combined(parts, columns, place_ref[0], spans, total_base)
     factors = [factor / total for factor in factors]
-    rows = factors[0].shape[0]
-    for j in range(GROUP):
-        out[0, j * rows : (j + 1) * rows, :] = weighted(parts, factors, j).astype(BF)
-
-
-def last_merge(parts, place, spans, total_base):
+    value = jnp.concatenate([weighted(parts, factors, j) for j in range(GROUP)], axis=0)
+    value = value.astype(BF)
+    rows = value.shape[0]
+    row = lax.broadcasted_iota(jnp.int32, (rows // 2, rows), 0)
+    column = lax.broadcasted_iota(jnp.int32, (rows // 2, rows), 1)
+    for out, core in ((kept, place_ref[1]), (given, 1 - place_ref[1])):
+        every_second = (column == 2 * row + core).astype(BF)
+        out[0] = jnp.dot(every_second, value, preferred_element_type=F32).astype(BF)
+
+
+def last_merge(parts, place, core, spans, total_base):
     groups, part_rows, rank = parts[0].shape
-    out_rows = part_rows - STAT_ROWS
+    out_rows = (part_rows - STAT_ROWS) // 2
     return pl.pallas_call(
         functools.partial(last_kernel, spans=spans, total_base=total_base),
         grid_spec=pltpu.PrefetchScalarGridSpec(
             num_scalar_prefetch=1,
             grid=(groups,),
             in_specs=[pl.BlockSpec((1, part_rows, rank), lambda s, *_: (s, 0, 0))] * RING,
-            out_specs=pl.BlockSpec((1, out_rows, rank), lambda s, *_: (s, 0, 0)),
+            out_specs=[pl.BlockSpec((1, out_rows, rank), lambda s, *_: (s, 0, 0))] * 2,
             scratch_shapes=[pltpu.VMEM((RING, rank, 128), F32)],
         ),
-        out_shape=jax.ShapeDtypeStruct((groups, out_rows, rank), BF),
-        compiler_params=pltpu.CompilerParams(vmem_limit_bytes=VMEM_LIMIT),
+        out_shape=[jax.ShapeDtypeStruct((groups, out_rows, rank), BF)] * 2,
+        compiler_params=pltpu.CompilerParams(vmem_limit_bytes=MERGE_VMEM),
         cost_estimate=pl.CostEstimate(
             flops=8 * groups * part_rows * rank,
             bytes_accessed=10 * groups * part_rows * rank,
             transcendentals=0,
         ),
-    )(place, *parts)
+    )(jnp.stack([place, core]), *parts)
 
 
 def per_device(
@@ -357,22 +363,25 @@
     model_width = w_out.shape[1]
     part = model_width // n_ep
 
-    w_rows = lax.all_gather(
-        w_out,
-        "ep",
-        axis=0,
-        axis_index_groups=[list(range(k, n_ep, 2)) for k in range(2)],
-        tiled=True,
-    )
+    same_core = [list(range(k, n_ep, 2)) for k in range(2)]
+    w_rows = lax.all_gather(w_out, "ep", axis=0, axis_index_groups=same_core, tiled=True)
     z_place, y_place = ctx_place // RING, ctx_place % RING
     ctx_axes = jnp.stack([z_place, y_place])
 
     inward = [(e * n_ctx + c, c * n_ep + e) for e in range(n_ep) for c in range(n_ctx)]
     outward = [(there, here) for here, there in inward]
     everywhere = ("ctx", "ep")
-    residual, routes, bucket_slots = (
-        lax.ppermute(value, everywhere, inward) for value in (residual, routes, bucket_slots)
-    )
+    tok_dev, model_width = residual.shape
+
+    chips = n_ep // 2
+    up_rows = [value_up] + [
+        lax.ppermute(value_up, "ep", [(i, (i + 2 * k) % n_ep) for i in range(n_ep)])
+        for k in range(1, chips)
+    ]
+    ctx_axes, *up_rows = lax.optimization_barrier((ctx_axes, *up_rows))
+    z_place, y_place = ctx_axes[0], ctx_axes[1]
+    order = jnp.mod(ep_place // 2 - jnp.arange(chips), chips)
+    up_rows = jnp.take(jnp.concatenate(up_rows, axis=0), order, axis=0)
 
     def along_z(k):
         return [(i, (i + k * RING) % n_ctx) for i in range(n_ctx)]
@@ -416,19 +425,16 @@
     ahead_b, behind_b = send(forward_b, backward_b, along_y)
     passed_a = relay(held_a, ahead_a, behind_a, z_first, by_z)
     passed_fa, passed_ba = send(*passed_a, along_z)
+    residual, _ = lax.optimization_barrier((residual, passed_a[0]))
+    chosen_in = jnp.concatenate([residual, routes.astype(BF), bucket_slots.astype(BF)], axis=1)
+    chosen_in = lax.ppermute(chosen_in, everywhere, inward)
+    held_b, chosen_in = lax.optimization_barrier((held_b, chosen_in))
+    residual = chosen_in[:, :model_width]
+    routes, bucket_slots = jnp.split(chosen_in[:, model_width:].astype(jnp.int32), 2, axis=1)
+
     passed_b = relay(held_b, ahead_b, behind_b, y_first, by_y)
     passed_fb, passed_bb = send(*passed_b, along_y)
 
-    value_up, _ = lax.optimization_barrier((value_up, passed_b[0]))
-    own_up = lax.all_to_all(
-        jnp.broadcast_to(value_up, (n_ep,) + value_up.shape[1:]),
-        "ep",
-        split_axis=0,
-        concat_axis=0,
-        tiled=True,
-    )
-    own_a, own_up = lax.optimization_barrier((own_a, own_up))
-
     next_a = first_merge(
         own_a, ahead_a, behind_a, passed_fa, passed_ba, z_first, by_z, second
     )
@@ -437,30 +443,21 @@
     )
     got_a = [next_a[0]] + [lax.ppermute(next_a[k], "ctx", along_y(k)) for k in (1, 2, 3)]
     got_b = [next_b[0]] + [lax.ppermute(next_b[k], "ctx", along_z(k)) for k in (1, 2, 3)]
-    latent_a = last_merge(got_a, y_first, second, part_rows)
-    latent_b = last_merge(got_b, z_first, second, part_rows)
-    latent_out = jnp.concatenate([latent_a, latent_b], axis=0)
-    latent_out = latent_out.reshape(samples, step_count, own_heads, rank)
+    latent_out = []
+    for got, place in ((got_a, y_place), (got_b, z_place)):
+        kept, given = last_merge(got, place, core, second, part_rows)
+        latent_out.append(jnp.stack([kept, lax.ppermute(given, "ep", swap)]))
+    latent_out = jnp.stack(latent_out, axis=1)
+    latent_out = latent_out.reshape(2 * tokens_here, own_heads // 2, rank)
     head_values = jnp.einsum(
-        "sthr,hrv->sthv", latent_out, own_up, preferred_element_type=F32
+        "nhr,hrv->nhv", latent_out, up_rows, preferred_element_type=F32
     ).astype(BF)
-    head_values = head_values.reshape(tokens_here, own_heads // 2, 2, value_width)
-
-    def pick(value, index, axis):
-        return lax.dynamic_index_in_dim(value, index, axis, keepdims=False)
-
-    kept = pick(head_values, core, 2)
-    given = lax.ppermute(pick(head_values, 1 - core, 2), "ep", swap)
-    head_flat = jnp.where(core == 0, jnp.stack([kept, given]), jnp.stack([given, kept]))
-    theirs = jnp.dot(
-        pick(head_flat, 1 - core, 0).reshape(tokens_here, -1), w_rows, preferred_element_type=F32
-    ).astype(BF)
-    theirs = lax.ppermute(theirs, "ep", swap)
-    ours = jnp.dot(
-        pick(head_flat, core, 0).reshape(tokens_here, -1), w_rows, preferred_element_type=F32
-    )
+    head_flat = head_values.reshape(2 * tokens_here, own_heads // 2 * value_width)
+    projected = jnp.dot(head_flat, w_rows, preferred_element_type=F32).astype(BF)
+    projected = lax.optimization_barrier(projected)
+    ours = projected[:tokens_here].astype(F32)
+    theirs = lax.ppermute(projected[tokens_here:], "ep", swap)
     projected = (ours + theirs.astype(F32)).astype(BF)
-    tok_dev = residual.shape[0]
     projected = lax.all_to_all(
         projected.reshape(n_ctx, tok_dev, model_width),
         "ctx",
@@ -494,7 +491,6 @@
     outgoing = jnp.einsum(
         "te,td->ed", slot_hit.astype(BF), normed, preferred_element_type=F32
     ).astype(BF)
-    chips = n_ep // CAP
     copies = jnp.broadcast_to(
         outgoing.reshape(n_ctx, 1, CAP, n_ep, part), (n_ctx, chips, CAP, n_ep, part)
     ).reshape(devices, n_ep, part)

time: 256 us -> 258 us (level)
  waiting for transfers between devices: 58.9 us -> 72.6 us
  Pallas kernels: 44 us -> 40 us
  other arithmetic: 4.13 us -> 8 us
  blocking collectives: 37.4 us -> 33.6 us
  local copies, waits for them, and re-layouts: 19.4 us -> 15.8 us
  starting transfers between devices: 65.1 us -> 61.7 us
  matrix products: 12 us -> 8.82 us
    all_to_all x1, waiting for transfers between devices: 0.01 us -> 14.7 us  [per_device(): lax.all_to_all(projected.reshape(n_ctx, tok_dev, model_width), 'ctx', spl...]
    ppermute x4, waiting for transfers between devices: 8.36 us -> 15.7 us  [send(): lax.ppermute(forward, 'ctx', along(1))]
    ppermute x3, waiting for transfers between devices: 6.67 us -> 0.01 us  [per_device(): lax.ppermute(next_a[k], 'ctx', along_y(k))]
    ppermute x4, waiting for transfers between devices: 6.16 us -> 0.6 us  [send(): lax.ppermute(backward, 'ctx', along(3))]
    ppermute x3, starting transfers between devices: 6.14 us -> 11 us  [per_device(): lax.ppermute(next_b[k], 'ctx', along_z(k))]
    all_to_all x1 -> x0, starting transfers between devices: 4.84 us -> none  [per_device(): lax.all_to_all(jnp.broadcast_to(value_up, (n_ep,) + value_up.shape[1:]),...]
    ppermute x4 -> x7, waiting for transfers between devices: 6.66 us -> 10.7 us  [the longest x1 8.36 us: per_device(): chosen_in = lax.ppermute(chosen_in, everywhere, inward)]
    all_to_all x1, blocking collectives: 37.4 us -> 33.6 us  [per_device(): lax.all_to_all(copies, ('ctx', 'ep'), split_axis=0, concat_axis=0, tiled=...]
  transfers between devices with their start and end apart: 27 -> 28, of which waited for: 15 -> 12; matrix products, arithmetic and copies ran while one was open for 4% -> 5% of each run, Pallas kernels for 17% -> 16%
where the time goes in v3:
time: 258 us; the launch traced here: 254 us
  waiting for transfers between devices  72.6 us (28%)
  starting transfers between devices  61.7 us (24%)
  Pallas kernels  40 us (16%)
  blocking collectives  33.6 us (13%)
  local copies, waits for them, and re-layouts  15.8 us (6%)
  between operations  13.9 us (5%)
  matrix products  8.82 us (3%)
  other arithmetic  8 us (3%)
    all_to_all x1, blocking collectives, per_device(): lax.all_to_all(copies, ('ctx', 'ep'), split_axis=0, concat_axis=0, tiled=...  33.6 us
    pallas_call x2, Pallas kernels, attend(): pl.pallas_call(functools.partial(attend_kernel, spans=spans, offset=half...  17.6 us
    ppermute x4, waiting for transfers between devices, send(): lax.ppermute(forward, 'ctx', along(1))  15.7 us
    all_to_all x1, waiting for transfers between devices, per_device(): lax.all_to_all(projected.reshape(n_ctx, tok_dev, model_width), 'ctx', spl...  14.7 us
    ppermute x3, starting transfers between devices, per_device(): lax.ppermute(next_b[k], 'ctx', along_z(k))  11 us
    all_to_all x1, waiting for transfers between devices, per_device(): lax.all_to_all(pair_out, ('ctx', 'ep'), split_axis=0, concat_axis=0, tile...  10.9 us
    unnamed x57, local copies, waits for them, and re-layouts  10.5 us
    pallas_call x2, Pallas kernels, first_merge(): pl.pallas_call(functools.partial(first_kernel, spans=spans, next_spans=ne...  9.58 us
  transfers between devices with their start and end apart: 28, of which 12 were waited for; matrix products, arithmetic and copies ran while one was open for 5% of the time, Pallas kernels for 16%

profile of v3, /device:TPU:1, one launch (start us, length us, event | category | flops | bytes accessed | tf_op | source)
XLA Modules:
  0.0 254.5 jit_solution(207481699590964561)
XLA Ops:
  7.3 2.1 collective-permute-start
  9.4 2.5 collective-permute-start.1
  14.8 3.1 %copy.26.prompt_ref = bf16[2048,576]{1,0:T(8,128)(2,1)S(1)} copy(bf16[2048,576]{0,1:T(8,128)(2,1)} %param.15) | data formatting | bytes 4718592 | tf_op args[1]
  20.7 8.8 %shard_map.137 = (bf16[4,272,512]{2,1,0:T(8,128)(2,1)}, bf16[4,272,512]{2,1,0:T(8,128)(2,1)}, bf16[4,272,512]{2,1,0:T(8,128)(2,1)}, bf16[4,272,512]{2,1,0:T(8,128)(2,1)}) custom-call(s32[32]{0:T(128)S(1)} %broadcast_minimum_fusion.count_ref, s32[32,8]{1,0:T(8,128)S(1)} %select_reduce_fusion.table_ref, s32[2]{0:T(128)S(1)} %get-tuple-element.84.info_ref, ...), custom_call_target="tpu_custom_call" | custom-call | flops 2281701376 | bytes 17825792 | tf_op jit(solution)/shard_map/pallas_call | solution.py:109
  29.5 2.9 %collective-permute-start.3 = (bf16[4,272,512]{2,1,0:T(8,128)(2,1)}, bf16[4,272,512]{2,1,0:T(8,128)(2,1)S(1)}, u32[]{:S(2)}, u32[]{:S(2)}) collective-permute-start(bf16[4,272,512]{2,1,0:T(8,128)(2,1)} %get-tuple-element.40), channel_id=1, source_target_pairs={{0,32},{8,40},{16,48},{24,56},{32,64},{40,72},{48,80},{56,88},{64,... | collective-permute-start | bytes 3342344 | tf_op jit(solution)/shard_map/ppermute | solution.py:415
  32.4 2.9 %collective-permute-start.4 = (bf16[4,272,512]{2,1,0:T(8,128)(2,1)}, bf16[4,272,512]{2,1,0:T(8,128)(2,1)S(1)}, u32[]{:S(2)}, u32[]{:S(2)}) collective-permute-start(bf16[4,272,512]{2,1,0:T(8,128)(2,1)} %get-tuple-element.41), channel_id=1, source_target_pairs={{0,96},{8,104},{16,112},{24,120},{32,0},{40,8},{48,16},{56,24},{64... | collective-permute-start | bytes 3342344 | tf_op jit(solution)/shard_map/ppermute | solution.py:415
  35.3 8.8 %shard_map.136 = (bf16[4,272,512]{2,1,0:T(8,128)(2,1)}, bf16[4,272,512]{2,1,0:T(8,128)(2,1)}, bf16[4,272,512]{2,1,0:T(8,128)(2,1)}, bf16[4,272,512]{2,1,0:T(8,128)(2,1)}) custom-call(s32[32]{0:T(128)S(1)} %broadcast_minimum_fusion.count_ref, s32[32,8]{1,0:T(8,128)S(1)} %select_reduce_fusion.table_ref, s32[2]{0:T(128)S(1)} %get-tuple-element.83.info_ref, ...), custom_call_target="tpu_custom_call" | custom-call | flops 2281701376 | bytes 17825792 | tf_op jit(solution)/shard_map/pallas_call | solution.py:109
  46.9 13.8 %collective-permute-done.3 = bf16[4,272,512]{2,1,0:T(8,128)(2,1)S(1)} collective-permute-done((bf16[4,272,512]{2,1,0:T(8,128)(2,1)}, bf16[4,272,512]{2,1,0:T(8,128)(2,1)S(1)}, u32[]{:S(2)}, u32[]{:S(2)}) %collective-permute-start.3) | collective-permute-done | bytes 1114144 | tf_op jit(solution)/shard_map/ppermute | solution.py:415
  60.6 2.7 %shard_map.138 = (bf16[2,272,512]{2,1,0:T(8,128)(2,1)}, bf16[2,272,512]{2,1,0:T(8,128)(2,1)}) custom-call(s32[2]{0:T(128)S(1)} %pad_add_fusion.place_ref, bf16[2,2,272,512]{3,2,1,0:T(8,128)(2,1)S(1)} %bitcast.85, bf16[2,2,272,512]{3,2,1,0:T(8,128)(2,1)S(1)} %bitcast.78, bf16[2,2,272,512]{3,2,1,0:T(8,128)(2,1)S(1)} %bitcast.80), custom_call_target="tpu_custom_call" | custom-call | flops 2228224 | bytes 3342336 | tf_op jit(solution)/shard_map/pallas_call | solution.py:200
  67.2 2.5 collective-permute-start.5
  69.8 8.4 %collective-permute-done.5 = bf16[4,7184]{1,0:T(4,128)(2,1)S(1)} collective-permute-done((bf16[4,7184]{1,0:T(4,128)(2,1)S(1)}, bf16[4,7184]{1,0:T(4,128)(2,1)S(1)}, u32[]{:S(2)}, u32[]{:S(2)}) %collective-permute-start.5) | collective-permute-done | bytes 57504 | tf_op jit(solution)/shard_map/ppermute | solution.py:430
  79.4 2.8 %shard_map.141 = (bf16[2,272,512]{2,1,0:T(8,128)(2,1)}, bf16[2,272,512]{2,1,0:T(8,128)(2,1)}) custom-call(s32[2]{0:T(128)S(1)} %rev.3.place_ref, bf16[2,2,272,512]{3,2,1,0:T(8,128)(2,1)S(1)} %bitcast.84, bf16[2,2,272,512]{3,2,1,0:T(8,128)(2,1)S(1)} %bitcast.74, bf16[2,2,272,512]{3,2,1,0:T(8,128)(2,1)S(1)} %bitcast.76), custom_call_target="tpu_custom_call" | custom-call | flops 2228224 | bytes 3342336 | tf_op jit(solution)/shard_map/pallas_call | solution.py:200
  82.2 2.7 %collective-permute-start.15 = (bf16[2,272,512]{2,1,0:T(8,128)(2,1)}, bf16[2,272,512]{2,1,0:T(8,128)(2,1)}, u32[]{:S(2)}, u32[]{:S(2)}) collective-permute-start(bf16[2,272,512]{2,1,0:T(8,128)(2,1)} %get-tuple-element.62), channel_id=1, source_target_pairs={{0,24},{8,0},{16,8},{24,16},{32,56},{40,32},{48,40},{56,48},{64,88... | collective-permute-start | bytes 1671176 | tf_op jit(solution)/shard_map/ppermute | solution.py:415
  84.9 5.1 %shard_map.139 = (bf16[2,2,80,512]{3,2,1,0:T(8,128)(2,1)S(1)}, bf16[2,2,80,512]{3,2,1,0:T(8,128)(2,1)}, bf16[2,2,80,512]{3,2,1,0:T(8,128)(2,1)S(1)}, bf16[2,2,80,512]{3,2,1,0:T(8,128)(2,1)S(1)}) custom-call(s32[2]{0:T(128)S(1)} %pad_add_fusion.place_ref, bf16[2,2,272,512]{3,2,1,0:T(8,128)(2,1)S(1)} %bitcast.83, bf16[2,2,272,512]{3,2,1,0:T(8,128)(2,1)S(1)} %bitcast.79, ...), custom_call_target="tpu_custom_call" | custom-call | flops 3342336 | bytes 4456448 | tf_op jit(solution)/shard_map/pallas_call | solution.py:267
  98.1 4.5 %shard_map.142 = (bf16[2,2,80,512]{3,2,1,0:T(8,128)(2,1)S(1)}, bf16[2,2,80,512]{3,2,1,0:T(8,128)(2,1)S(1)}, bf16[2,2,80,512]{3,2,1,0:T(8,128)(2,1)S(1)}, bf16[2,2,80,512]{3,2,1,0:T(8,128)(2,1)S(1)}) custom-call(s32[2]{0:T(128)S(1)} %rev.3.place_ref, bf16[2,2,272,512]{3,2,1,0:T(8,128)(2,1)S(1)} %bitcast.82, bf16[2,2,272,512]{3,2,1,0:T(8,128)(2,1)S(1)} %bitcast.75, ...), custom_call_target="tpu_custom_call" | custom-call | flops 3342336 | bytes 4456448 | tf_op jit(solution)/shard_map/pallas_call | solution.py:267
  102.6 8.5 %collective-permute-start.16 = (bf16[4,80,512]{2,1,0:T(8,128)(2,1)S(1)}, bf16[4,80,512]{2,1,0:T(8,128)(2,1)S(1)}, u32[]{:S(2)}, u32[]{:S(2)}) collective-permute-start(bf16[4,80,512]{2,1,0:T(8,128)(2,1)S(1)} %bitcast.94), channel_id=1, source_target_pairs={{0,32},{8,40},{16,48},{24,56},{32,64},{40,72},{48,80},{56,88},{64,... | collective-permute-start | bytes 983048 | tf_op jit(solution)/shard_map/ppermute | solution.py:445
  111.1 2.5 collective-permute-start.18
  114.4 4.2 %shard_map.140 = (bf16[4,32,512]{2,1,0:T(8,128)(2,1)S(1)}, bf16[4,32,512]{2,1,0:T(8,128)(2,1)S(1)}) custom-call(s32[2]{0:T(128)S(1)} %pad_add_fusion.3.place_ref, bf16[4,80,512]{2,1,0:T(8,128)(2,1)S(1)} %bitcast.86, bf16[4,80,512]{2,1,0:T(8,128)(2,1)} %collective-permute-done.8.refs_1_, bf16[4,80,512]{2,1,0:T(8,128)(2,1)S(1)} %collective-permute-done.9.refs_2_, ...), custom_call_target="tpu_custom_call" | custom-call | flops 1310720 | bytes 1638400 | tf_op jit(solution)/shard_map/pallas_call | solution.py:316
  121.1 4.3 %collective-permute-done.17.refs_2_ = bf16[4,80,512]{2,1,0:T(8,128)(2,1)S(1)} collective-permute-done((bf16[4,80,512]{2,1,0:T(8,128)(2,1)S(1)}, bf16[4,80,512]{2,1,0:T(8,128)(2,1)S(1)}, u32[]{:S(2)}, u32[]{:S(2)}) %collective-permute-start.17) | collective-permute-done | bytes 327712 | tf_op jit(solution)/shard_map/ppermute | solution.py:445
  125.4 3.1 %shard_map.143 = (bf16[4,32,512]{2,1,0:T(8,128)(2,1)S(1)}, bf16[4,32,512]{2,1,0:T(8,128)(2,1)S(1)}) custom-call(s32[2]{0:T(128)S(1)} %pad_add_fusion.4.place_ref, bf16[4,80,512]{2,1,0:T(8,128)(2,1)S(1)} %bitcast.87, bf16[4,80,512]{2,1,0:T(8,128)(2,1)S(1)} %collective-permute-done.16.refs_1_, bf16[4,80,512]{2,1,0:T(8,128)(2,1)S(1)} %collective-permute-done.17.refs_2_, ...), custom_call_target="tpu_custom_call" | custom-call | flops 1310720 | bytes 1638400 | tf_op jit(solution)/shard_map/pallas_call | solution.py:316
  131.8 4.2 %convolution_convert_fusion.1 = bf16[128,7168]{1,0:T(8,128)(2,1)S(1)} fusion(bf16[128,512]{0,1:T(8,128)(2,1)S(1)} %bitcast.107, bf16[512,7168]{1,0:T(8,128)(2,1)} %all-gather.2.cloned.1.call-done), kind=kOutput, calls=%fused_computation.2 | convolution fusion | flops 940441600 | bytes 9306112 | tf_op jit(solution)/shard_map/dot_general | solution.py:456
  136.7 2.1 collective-permute-done.20
  140.3 8.2 %all-to-all-start = ((bf16[16,4,7168]{2,1,0:T(4,128)(2,1)}), bf16[16,4,7168]{2,1,0:T(4,128)(2,1)S(1)}, u32[]{:S(2)}, u32[]{:S(2)}) async-start(bf16[16,4,7168]{2,1,0:T(4,128)(2,1)} %reshape.212), calls=%async_computation | async-start | bytes 1835008 | tf_op jit(solution)/shard_map/all_to_all | solution.py:461
  148.7 14.7 %all-to-all-done = bf16[16,4,7168]{2,1,0:T(4,128)(2,1)S(1)} async-done(((bf16[16,4,7168]{2,1,0:T(4,128)(2,1)}), bf16[16,4,7168]{2,1,0:T(4,128)(2,1)S(1)}, u32[]{:S(2)}, u32[]{:S(2)}) %all-to-all-start) | async-done | bytes 917536 | tf_op jit(solution)/shard_map/all_to_all | solution.py:461
  165.3 33.6 %all_to_all.15 = bf16[128,8,896]{2,1,0:T(8,128)(2,1)S(1)} all-to-all(bf16[128,8,896]{2,1,0:T(8,128)(2,1)S(1)} %bitcast.102), channel_id=1, replica_groups=mesh['ctx'=16,'ep'=8] {'ctx','ep'}, dimensions={0} | all-to-all | bytes 3670016 | tf_op jit(solution)/shard_map/all_to_all | solution.py:497
  200.3 3.3 %collective-permute-done.23 = bf16[128,7168]{1,0:T(8,128)(2,1)S(1)} collective-permute-done((bf16[128,7168]{1,0:T(8,128)(2,1)S(1)}, bf16[128,7168]{1,0:T(8,128)(2,1)S(1)}, u32[]{:S(2)}, u32[]{:S(2)}) %collective-permute-start.23) | collective-permute-done | bytes 1835040 | tf_op jit(solution)/shard_map/ppermute | solution.py:499
  209.0 3.4 %collective-permute-done.24 = bf16[128,7168]{1,0:T(8,128)(2,1)S(1)} collective-permute-done((bf16[128,7168]{1,0:T(8,128)(2,1)S(1)}, bf16[128,7168]{1,0:T(8,128)(2,1)S(1)}, u32[]{:S(2)}, u32[]{:S(2)}) %collective-permute-start.24) | collective-permute-done | bytes 1835040 | tf_op jit(solution)/shard_map/ppermute | solution.py:505
  214.6 3.8 %all-to-all-start.2 = ((bf16[128,8,896]{2,1,0:T(8,128)(2,1)}), bf16[128,8,896]{2,1,0:T(8,128)(2,1)S(1)}, u32[]{:S(2)}, u32[]{:S(2)}) async-start(bf16[128,8,896]{2,1,0:T(8,128)(2,1)} %bitcast.39), calls=%async_computation.2 | async-start | bytes 3670016 | tf_op jit(solution)/shard_map/all_to_all | solution.py:509
  218.5 5.2 %collective-permute-start.22 = (f32[4,32]{0,1:T(8,128)S(1)}, f32[4,32]{0,1:T(8,128)S(1)}, u32[]{:S(2)}, u32[]{:S(2)}) collective-permute-start(f32[4,32]{0,1:T(8,128)S(1)} %bitcast.112), channel_id=1, source_target_pairs={{0,0},{8,1},{16,2},{24,3},{32,4},{40,5},{48,6},{56,7},{64,8},{72,9... | collective-permute-start | bytes 1544 | tf_op jit(solution)/shard_map/ppermute | solution.py:486
  223.7 3.3 %collective-permute-start.21 = (bf16[4,7168]{1,0:T(4,128)(2,1)S(1)}, bf16[4,7168]{1,0:T(4,128)(2,1)S(1)}, u32[]{:S(2)}, u32[]{:S(2)}) collective-permute-start(bf16[4,7168]{1,0:T(4,128)(2,1)S(1)} %get-tuple-element.74), channel_id=1, source_target_pairs={{0,0},{8,1},{16,2},{24,3},{32,4},{40,5},{48,6},{56,7},{64,8},{72,9... | collective-permute-start | bytes 172040 | tf_op jit(solution)/shard_map/ppermute | solution.py:489
  227.0 8.3 %collective-permute-done.22 = f32[4,32]{0,1:T(8,128)S(1)} collective-permute-done((f32[4,32]{0,1:T(8,128)S(1)}, f32[4,32]{0,1:T(8,128)S(1)}, u32[]{:S(2)}, u32[]{:S(2)}) %collective-permute-start.22) | collective-permute-done | bytes 544 | tf_op jit(solution)/shard_map/ppermute | solution.py:486
  235.4 10.9 %all-to-all-done.2 = bf16[128,8,896]{2,1,0:T(8,128)(2,1)S(1)} async-done(((bf16[128,8,896]{2,1,0:T(8,128)(2,1)}), bf16[128,8,896]{2,1,0:T(8,128)(2,1)S(1)}, u32[]{:S(2)}, u32[]{:S(2)}) %all-to-all-start.2) | async-done | bytes 1835040 | tf_op jit(solution)/shard_map/all_to_all | solution.py:509
  (148 shorter events, 43.6 us)
Async XLA Ops:
  6.5 157.5 %copy-start = (bf16[7168,16]{0,1:T(8,128)(2,1)S(1)}, bf16[7168,16]{0,1:T(8,128)(2,1)}, u32[]{:S(2)}) copy-start(bf16[7168,16]{0,1:T(8,128)(2,1)} %param.22) | copy-start | bytes 688132
  6.5 125.2 %all-gather.2.cloned.1.call-start = ((), (), s32[]{:S(2)}) async-start(), calls=%async_computation.3 | async-start | bytes 9175040 | tf_op jit(solution)/shard_map/all_gather | solution.py:367
  7.3 11.4 %collective-permute-start = (bf16[1,512,128]{2,1,0:T(8,128)(2,1)}, bf16[1,512,128]{2,1,0:T(8,128)(2,1)S(1)}, u32[]{:S(2)}, u32[]{:S(2)}) collective-permute-start(bf16[1,512,128]{2,1,0:T(8,128)(2,1)} %param.18), channel_id=1, source_target_pairs={{0,2},{1,3},{2,4},{3,5},{4,6},{5,7},{6,0},{7,1},{8,10},{9,11},{10,... | collective-permute-start | bytes 393224 | tf_op jit(solution)/shard_map/ppermute | solution.py:378
  9.4 9.3 %collective-permute-start.1 = (bf16[1,512,128]{2,1,0:T(8,128)(2,1)}, bf16[1,512,128]{2,1,0:T(8,128)(2,1)S(1)}, u32[]{:S(2)}, u32[]{:S(2)}) collective-permute-start(bf16[1,512,128]{2,1,0:T(8,128)(2,1)} %param.18), channel_id=1, source_target_pairs={{0,4},{1,5},{2,6},{3,7},{4,0},{5,1},{6,2},{7,3},{8,12},{9,13},{10,... | collective-permute-start | bytes 393224 | tf_op jit(solution)/shard_map/ppermute | solution.py:378
  11.8 6.9 %collective-permute-start.2 = (bf16[1,512,128]{2,1,0:T(8,128)(2,1)}, bf16[1,512,128]{2,1,0:T(8,128)(2,1)S(1)}, u32[]{:S(2)}, u32[]{:S(2)}) collective-permute-start(bf16[1,512,128]{2,1,0:T(8,128)(2,1)} %param.18), channel_id=1, source_target_pairs={{0,6},{1,7},{2,0},{3,1},{4,2},{5,3},{6,4},{7,5},{8,14},{9,15},{10,... | collective-permute-start | bytes 393224 | tf_op jit(solution)/shard_map/ppermute | solution.py:378
  29.5 31.1 %collective-permute-start.3 = (bf16[4,272,512]{2,1,0:T(8,128)(2,1)}, bf16[4,272,512]{2,1,0:T(8,128)(2,1)S(1)}, u32[]{:S(2)}, u32[]{:S(2)}) collective-permute-start(bf16[4,272,512]{2,1,0:T(8,128)(2,1)} %get-tuple-element.40), channel_id=1, source_target_pairs={{0,32},{8,40},{16,48},{24,56},{32,64},{40,72},{48,80},{56,88},{64,... | collective-permute-start | bytes 3342344 | tf_op jit(solution)/shard_map/ppermute | solution.py:415
  32.4 28.2 %collective-permute-start.4 = (bf16[4,272,512]{2,1,0:T(8,128)(2,1)}, bf16[4,272,512]{2,1,0:T(8,128)(2,1)S(1)}, u32[]{:S(2)}, u32[]{:S(2)}) collective-permute-start(bf16[4,272,512]{2,1,0:T(8,128)(2,1)} %get-tuple-element.41), channel_id=1, source_target_pairs={{0,96},{8,104},{16,112},{24,120},{32,0},{40,8},{48,16},{56,24},{64... | collective-permute-start | bytes 3342344 | tf_op jit(solution)/shard_map/ppermute | solution.py:415
  44.2 34.0 %collective-permute-start.12 = (bf16[4,272,512]{2,1,0:T(8,128)(2,1)}, bf16[4,272,512]{2,1,0:T(8,128)(2,1)S(1)}, u32[]{:S(2)}, u32[]{:S(2)}) collective-permute-start(bf16[4,272,512]{2,1,0:T(8,128)(2,1)} %get-tuple-element.58), channel_id=1, source_target_pairs={{0,8},{8,16},{16,24},{24,0},{32,40},{40,48},{48,56},{56,32},{64,72... | collective-permute-start | bytes 3342344 | tf_op jit(solution)/shard_map/ppermute | solution.py:415
  46.2 32.0 %collective-permute-start.13 = (bf16[4,272,512]{2,1,0:T(8,128)(2,1)}, bf16[4,272,512]{2,1,0:T(8,128)(2,1)S(1)}, u32[]{:S(2)}, u32[]{:S(2)}) collective-permute-start(bf16[4,272,512]{2,1,0:T(8,128)(2,1)} %get-tuple-element.59), channel_id=1, source_target_pairs={{0,24},{8,0},{16,8},{24,16},{32,56},{40,32},{48,40},{56,48},{64,88... | collective-permute-start | bytes 3342344 | tf_op jit(solution)/shard_map/ppermute | solution.py:415
  64.4 20.5 %collective-permute-start.6 = (bf16[2,272,512]{2,1,0:T(8,128)(2,1)}, bf16[2,272,512]{2,1,0:T(8,128)(2,1)}, u32[]{:S(2)}, u32[]{:S(2)}) collective-permute-start(bf16[2,272,512]{2,1,0:T(8,128)(2,1)} %get-tuple-element.42), channel_id=1, source_target_pairs={{0,32},{8,40},{16,48},{24,56},{32,64},{40,72},{48,80},{56,88},{64,... | collective-permute-start | bytes 1671176 | tf_op jit(solution)/shard_map/ppermute | solution.py:415
  65.6 19.2 %collective-permute-start.7 = (bf16[2,272,512]{2,1,0:T(8,128)(2,1)}, bf16[2,272,512]{2,1,0:T(8,128)(2,1)}, u32[]{:S(2)}, u32[]{:S(2)}) collective-permute-start(bf16[2,272,512]{2,1,0:T(8,128)(2,1)} %get-tuple-element.50), channel_id=1, source_target_pairs={{0,96},{8,104},{16,112},{24,120},{32,0},{40,8},{48,16},{56,24},{64... | collective-permute-start | bytes 1671176 | tf_op jit(solution)/shard_map/ppermute | solution.py:415
  67.2 10.9 %collective-permute-start.5 = (bf16[4,7184]{1,0:T(4,128)(2,1)S(1)}, bf16[4,7184]{1,0:T(4,128)(2,1)S(1)}, u32[]{:S(2)}, u32[]{:S(2)}) collective-permute-start(bf16[4,7184]{1,0:T(4,128)(2,1)S(1)} %concatenate.9), channel_id=1, source_target_pairs={{0,0},{1,8},{2,16},{3,24},{4,32},{5,40},{6,48},{7,56},{8,64},{9,72... | collective-permute-start | bytes 172424 | tf_op jit(solution)/shard_map/ppermute | solution.py:430
  82.2 14.1 %collective-permute-start.14 = (bf16[2,272,512]{2,1,0:T(8,128)(2,1)}, bf16[2,272,512]{2,1,0:T(8,128)(2,1)S(1)}, u32[]{:S(2)}, u32[]{:S(2)}) collective-permute-start(bf16[2,272,512]{2,1,0:T(8,128)(2,1)} %get-tuple-element.61), channel_id=1, source_target_pairs={{0,8},{8,16},{16,24},{24,0},{32,40},{40,48},{48,56},{56,32},{64,72... | collective-permute-start | bytes 1671176 | tf_op jit(solution)/shard_map/ppermute | solution.py:415
  82.2 14.7 %collective-permute-start.15 = (bf16[2,272,512]{2,1,0:T(8,128)(2,1)}, bf16[2,272,512]{2,1,0:T(8,128)(2,1)}, u32[]{:S(2)}, u32[]{:S(2)}) collective-permute-start(bf16[2,272,512]{2,1,0:T(8,128)(2,1)} %get-tuple-element.62), channel_id=1, source_target_pairs={{0,24},{8,0},{16,8},{24,16},{32,56},{40,32},{48,40},{56,48},{64,88... | collective-permute-start | bytes 1671176 | tf_op jit(solution)/shard_map/ppermute | solution.py:415
  84.9 45.1 %copy-start.12 = (bf16[1,512,128]{2,1,0:T(8,128)(2,1)S(1)}, bf16[1,512,128]{2,1,0:T(8,128)(2,1)}, u32[]{:S(2)}) copy-start(bf16[1,512,128]{2,1,0:T(8,128)(2,1)} %param.18) | copy-start | bytes 393220
  91.5 19.6 %collective-permute-start.8 = (bf16[4,80,512]{2,1,0:T(8,128)(2,1)}, bf16[4,80,512]{2,1,0:T(8,128)(2,1)}, u32[]{:S(2)}, u32[]{:S(2)}) collective-permute-start(bf16[4,80,512]{2,1,0:T(8,128)(2,1)} %bitcast.11), channel_id=1, source_target_pairs={{0,8},{8,16},{16,24},{24,0},{32,40},{40,48},{48,56},{56,32},{64,72... | collective-permute-start | bytes 983048 | tf_op jit(solution)/shard_map/ppermute | solution.py:444
  91.5 22.8 %collective-permute-start.9 = (bf16[4,80,512]{2,1,0:T(8,128)(2,1)}, bf16[4,80,512]{2,1,0:T(8,128)(2,1)S(1)}, u32[]{:S(2)}, u32[]{:S(2)}) collective-permute-start(bf16[4,80,512]{2,1,0:T(8,128)(2,1)} %bitcast.91), channel_id=1, source_target_pairs={{0,16},{8,24},{16,0},{24,8},{32,48},{40,56},{48,32},{56,40},{64,80... | collective-permute-start | bytes 983048 | tf_op jit(solution)/shard_map/ppermute | solution.py:444
  92.8 21.6 %collective-permute-start.10 = (bf16[4,80,512]{2,1,0:T(8,128)(2,1)}, bf16[4,80,512]{2,1,0:T(8,128)(2,1)S(1)}, u32[]{:S(2)}, u32[]{:S(2)}) collective-permute-start(bf16[4,80,512]{2,1,0:T(8,128)(2,1)} %bitcast.90), channel_id=1, source_target_pairs={{0,24},{8,0},{16,8},{24,16},{32,56},{40,32},{48,40},{56,48},{64,88... | collective-permute-start | bytes 983048 | tf_op jit(solution)/shard_map/ppermute | solution.py:444
  98.1 31.9 %copy-start.16 = (bf16[1,512,128]{2,1,0:T(8,128)(2,1)S(1)}, bf16[1,512,128]{2,1,0:T(8,128)(2,1)}, u32[]{:S(2)}) copy-start(bf16[1,512,128]{2,1,0:T(8,128)(2,1)} %copy-done.15) | copy-start | bytes 393220
  98.1 31.9 %copy-start.18 = (bf16[1,512,128]{2,1,0:T(8,128)(2,1)S(1)}, bf16[1,512,128]{2,1,0:T(8,128)(2,1)}, u32[]{:S(2)}) copy-start(bf16[1,512,128]{2,1,0:T(8,128)(2,1)} %copy-done.17) | copy-start | bytes 393220
  102.6 18.4 %collective-permute-start.16 = (bf16[4,80,512]{2,1,0:T(8,128)(2,1)S(1)}, bf16[4,80,512]{2,1,0:T(8,128)(2,1)S(1)}, u32[]{:S(2)}, u32[]{:S(2)}) collective-permute-start(bf16[4,80,512]{2,1,0:T(8,128)(2,1)S(1)} %bitcast.94), channel_id=1, source_target_pairs={{0,32},{8,40},{16,48},{24,56},{32,64},{40,72},{48,80},{56,88},{64,... | collective-permute-start | bytes 983048 | tf_op jit(solution)/shard_map/ppermute | solution.py:445
  111.1 14.2 %collective-permute-start.17 = (bf16[4,80,512]{2,1,0:T(8,128)(2,1)S(1)}, bf16[4,80,512]{2,1,0:T(8,128)(2,1)S(1)}, u32[]{:S(2)}, u32[]{:S(2)}) collective-permute-start(bf16[4,80,512]{2,1,0:T(8,128)(2,1)S(1)} %bitcast.93), channel_id=1, source_target_pairs={{0,64},{8,72},{16,80},{24,88},{32,96},{40,104},{48,112},{56,120},{... | collective-permute-start | bytes 983048 | tf_op jit(solution)/shard_map/ppermute | solution.py:445
  111.1 14.2 %collective-permute-start.18 = (bf16[4,80,512]{2,1,0:T(8,128)(2,1)S(1)}, bf16[4,80,512]{2,1,0:T(8,128)(2,1)S(1)}, u32[]{:S(2)}, u32[]{:S(2)}) collective-permute-start(bf16[4,80,512]{2,1,0:T(8,128)(2,1)S(1)} %bitcast.92), channel_id=1, source_target_pairs={{0,96},{8,104},{16,112},{24,120},{32,0},{40,8},{48,16},{56,24},{64... | collective-permute-start | bytes 983048 | tf_op jit(solution)/shard_map/ppermute | solution.py:445
  118.6 12.2 %collective-permute-start.11 = (bf16[4,32,512]{2,1,0:T(8,128)(2,1)S(1)}, bf16[4,32,512]{2,1,0:T(8,128)(2,1)S(1)}, u32[]{:S(2)}, u32[]{:S(2)}) collective-permute-start(bf16[4,32,512]{2,1,0:T(8,128)(2,1)S(1)} %get-tuple-element.56), channel_id=1, source_target_pairs={{0,1},{1,0},{2,3},{3,2},{4,5},{5,4},{6,7},{7,6},{8,9},{9,8},{10,11... | collective-permute-start | bytes 393224 | tf_op jit(solution)/shard_map/ppermute | solution.py:449
  128.4 2.6 %collective-permute-start.19 = (bf16[4,32,512]{2,1,0:T(8,128)(2,1)S(1)}, bf16[4,32,512]{2,1,0:T(8,128)(2,1)S(1)}, u32[]{:S(2)}, u32[]{:S(2)}) collective-permute-start(bf16[4,32,512]{2,1,0:T(8,128)(2,1)S(1)} %get-tuple-element.68), channel_id=1, source_target_pairs={{0,1},{1,0},{2,3},{3,2},{4,5},{5,4},{6,7},{7,6},{8,9},{9,8},{10,11... | collective-permute-start | bytes 393224 | tf_op jit(solution)/shard_map/ppermute | solution.py:449
  136.1 2.8 %collective-permute-start.20 = (bf16[64,7168]{1,0:T(8,128)(2,1)S(1)}, bf16[64,7168]{1,0:T(8,128)(2,1)S(1)}, u32[]{:S(2)}, u32[]{:S(2)}) collective-permute-start(bf16[64,7168]{1,0:T(8,128)(2,1)S(1)} %slice.35), channel_id=1, source_target_pairs={{0,1},{1,0},{2,3},{3,2},{4,5},{5,4},{6,7},{7,6},{8,9},{9,8},{10,11... | collective-permute-start | bytes 2752520 | tf_op jit(solution)/shard_map/ppermute | solution.py:459
  140.3 23.1 %all-to-all-start = ((bf16[16,4,7168]{2,1,0:T(4,128)(2,1)}), bf16[16,4,7168]{2,1,0:T(4,128)(2,1)S(1)}, u32[]{:S(2)}, u32[]{:S(2)}) async-start(bf16[16,4,7168]{2,1,0:T(4,128)(2,1)} %reshape.212), calls=%async_computation | async-start | bytes 1835008 | tf_op jit(solution)/shard_map/all_to_all | solution.py:461
  199.3 4.4 %collective-permute-start.23 = (bf16[128,7168]{1,0:T(8,128)(2,1)S(1)}, bf16[128,7168]{1,0:T(8,128)(2,1)S(1)}, u32[]{:S(2)}, u32[]{:S(2)}) collective-permute-start(bf16[128,7168]{1,0:T(8,128)(2,1)S(1)} %bitcast.98), channel_id=1, source_target_pairs={{0,1},{1,0},{2,3},{3,2},{4,5},{5,4},{6,7},{7,6},{8,9},{9,8},{10,11... | collective-permute-start | bytes 5505032 | tf_op jit(solution)/shard_map/ppermute | solution.py:499
  208.5 3.9 %collective-permute-start.24 = (bf16[128,7168]{1,0:T(8,128)(2,1)S(1)}, bf16[128,7168]{1,0:T(8,128)(2,1)S(1)}, u32[]{:S(2)}, u32[]{:S(2)}) collective-permute-start(bf16[128,7168]{1,0:T(8,128)(2,1)S(1)} %convolution_convert_fusion), channel_id=1, source_target_pairs={{0,1},{1,0},{2,3},{3,2},{4,5},{5,4},{6,7},{7,6},{8,9},{9,8},{10,11... | collective-permute-start | bytes 5505032 | tf_op jit(solution)/shard_map/ppermute | solution.py:505
  214.6 31.7 %all-to-all-start.2 = ((bf16[128,8,896]{2,1,0:T(8,128)(2,1)}), bf16[128,8,896]{2,1,0:T(8,128)(2,1)S(1)}, u32[]{:S(2)}, u32[]{:S(2)}) async-start(bf16[128,8,896]{2,1,0:T(8,128)(2,1)} %bitcast.39), calls=%async_computation.2 | async-start | bytes 3670016 | tf_op jit(solution)/shard_map/all_to_all | solution.py:509
  218.5 16.7 %collective-permute-start.22 = (f32[4,32]{0,1:T(8,128)S(1)}, f32[4,32]{0,1:T(8,128)S(1)}, u32[]{:S(2)}, u32[]{:S(2)}) collective-permute-start(f32[4,32]{0,1:T(8,128)S(1)} %bitcast.112), channel_id=1, source_target_pairs={{0,0},{8,1},{16,2},{24,3},{32,4},{40,5},{48,6},{56,7},{64,8},{72,9... | collective-permute-start | bytes 1544 | tf_op jit(solution)/shard_map/ppermute | solution.py:486
  223.7 23.3 %collective-permute-start.21 = (bf16[4,7168]{1,0:T(4,128)(2,1)S(1)}, bf16[4,7168]{1,0:T(4,128)(2,1)S(1)}, u32[]{:S(2)}, u32[]{:S(2)}) collective-permute-start(bf16[4,7168]{1,0:T(4,128)(2,1)S(1)} %get-tuple-element.74), channel_id=1, source_target_pairs={{0,0},{8,1},{16,2},{24,3},{32,4},{40,5},{48,6},{56,7},{64,8},{72,9... | collective-permute-start | bytes 172040 | tf_op jit(solution)/shard_map/ppermute | solution.py:489
  (22 other events, 285.1 us)
Sparse Core Ops, SparseCore 0:
  9.0 80.0 all-gather.1

commit v4 on v2

--- a/solution.py
+++ b/solution.py
@@ -370,9 +370,9 @@
     inward = [(e * n_ctx + c, c * n_ep + e) for e in range(n_ep) for c in range(n_ctx)]
     outward = [(there, here) for here, there in inward]
     everywhere = ("ctx", "ep")
-    residual, routes, bucket_slots = (
-        lax.ppermute(value, everywhere, inward) for value in (residual, routes, bucket_slots)
-    )
+    choices = jnp.concatenate([routes, bucket_slots], axis=1)
+    residual, choices = (lax.ppermute(value, everywhere, inward) for value in (residual, choices))
+    routes, bucket_slots = jnp.split(choices, 2, axis=1)
 
     def along_z(k):
         return [(i, (i + k * RING) % n_ctx) for i in range(n_ctx)]

time: 256 us -> 259 us (1.012)
  waiting for transfers between devices: 58.9 us -> 69.2 us
  blocking collectives: 37.4 us -> 31.2 us
    all_to_all x1, waiting for transfers between devices: 0.01 us -> 18.1 us  [per_device(): lax.all_to_all(projected.reshape(n_ctx, tok_dev, model_width), 'ctx', spl...]
    all_to_all x1, blocking collectives: 37.4 us -> 31.2 us  [per_device(): lax.all_to_all(copies, ('ctx', 'ep'), split_axis=0, concat_axis=0, tiled=...]
    ppermute x4, waiting for transfers between devices: 6.16 us -> 0.01 us  [send(): lax.ppermute(backward, 'ctx', along(3))]
    ppermute x4, waiting for transfers between devices: 8.36 us -> 14.3 us  [send(): lax.ppermute(forward, 'ctx', along(1))]
    ppermute x3 -> x2, waiting for transfers between devices: 5.78 us -> 0.01 us  [per_device(): lax.ppermute(value, everywhere, inward)]
    ppermute x4, starting transfers between devices: 11.4 us -> 7.82 us  [send(): lax.ppermute(backward, 'ctx', along(3))]
    ppermute x4, starting transfers between devices: 3.81 us -> 6.6 us  [send(): lax.ppermute(forward, 'ctx', along(1))]
    ppermute x3 -> x2, starting transfers between devices: 10.9 us -> 9.24 us  [per_device(): lax.ppermute(value, everywhere, inward)]
  transfers between devices with their start and end apart: 27 -> 26, of which waited for: 15 -> 12; matrix products, arithmetic and copies ran while one was open for 4% -> 5% of each run, Pallas kernels for 17% -> 17%
where the time goes in v4:
time: 259 us; the launch traced here: 257 us
  waiting for transfers between devices  69.2 us (27%)
  starting transfers between devices  64.2 us (25%)
  Pallas kernels  42.6 us (16%)
  blocking collectives  31.2 us (12%)
  local copies, waits for them, and re-layouts  19.5 us (8%)
  between operations  13.9 us (5%)
  matrix products  12 us (5%)
  other arithmetic  4.28 us (2%)
    all_to_all x1, blocking collectives, per_device(): lax.all_to_all(copies, ('ctx', 'ep'), split_axis=0, concat_axis=0, tiled=...  31.2 us
    pallas_call x2, Pallas kernels, attend(): pl.pallas_call(functools.partial(attend_kernel, spans=spans, offset=half...  18.9 us
    all_to_all x1, waiting for transfers between devices, per_device(): lax.all_to_all(projected.reshape(n_ctx, tok_dev, model_width), 'ctx', spl...  18.1 us
    ppermute x4, waiting for transfers between devices, send(): lax.ppermute(forward, 'ctx', along(1))  14.3 us
    unnamed x49, local copies, waits for them, and re-layouts  14.1 us
    all_to_all x1, waiting for transfers between devices, per_device(): lax.all_to_all(pair_out, ('ctx', 'ep'), split_axis=0, concat_axis=0, tile...  10.9 us
    pallas_call x2, Pallas kernels, first_merge(): pl.pallas_call(functools.partial(first_kernel, spans=spans, next_spans=ne...  10.5 us
    ppermute x2, starting transfers between devices, per_device(): lax.ppermute(value, everywhere, inward)  9.24 us
  transfers between devices with their start and end apart: 26, of which 12 were waited for; matrix products, arithmetic and copies ran while one was open for 5% of the time, Pallas kernels for 17%

profile of v4, /device:TPU:1, one launch (start us, length us, event | category | flops | bytes accessed | tf_op | source)
XLA Modules:
  0.0 256.9 jit_solution(11596205117862300586)
XLA Ops:
  8.3 3.1 %copy.43.prompt_ref = bf16[2048,576]{1,0:T(8,128)(2,1)S(1)} copy(bf16[2048,576]{0,1:T(8,128)(2,1)} %param.15) | data formatting | bytes 4718592 | tf_op args[1]
  12.3 10.8 %shard_map.137 = (bf16[4,272,512]{2,1,0:T(8,128)(2,1)S(1)}, bf16[4,272,512]{2,1,0:T(8,128)(2,1)}, bf16[4,272,512]{2,1,0:T(8,128)(2,1)}, bf16[4,272,512]{2,1,0:T(8,128)(2,1)S(1)}) custom-call(s32[32]{0:T(128)S(1)} %broadcast_minimum_fusion.count_ref, s32[32,8]{1,0:T(8,128)S(1)} %select_reduce_fusion.table_ref, s32[2]{0:T(128)S(1)} %get-tuple-element.66.info_ref, ...), custom_call_target="tpu_custom_call" | custom-call | flops 2281701376 | bytes 17825792 | tf_op jit(solution)/shard_map/pallas_call | solution.py:108
  24.1 2.7 %collective-permute-start.2 = (bf16[4,272,512]{2,1,0:T(8,128)(2,1)}, bf16[4,272,512]{2,1,0:T(8,128)(2,1)}, u32[]{:S(2)}, u32[]{:S(2)}) collective-permute-start(bf16[4,272,512]{2,1,0:T(8,128)(2,1)} %get-tuple-element.31), channel_id=1, source_target_pairs={{0,24},{8,0},{16,8},{24,16},{32,56},{40,32},{48,40},{56,48},{64,88... | collective-permute-start | bytes 3342344 | tf_op jit(solution)/shard_map/ppermute | solution.py:406
  26.8 8.1 %shard_map.136 = (bf16[4,272,512]{2,1,0:T(8,128)(2,1)S(1)}, bf16[4,272,512]{2,1,0:T(8,128)(2,1)}, bf16[4,272,512]{2,1,0:T(8,128)(2,1)}, bf16[4,272,512]{2,1,0:T(8,128)(2,1)S(1)}) custom-call(s32[32]{0:T(128)S(1)} %broadcast_minimum_fusion.count_ref, s32[32,8]{1,0:T(8,128)S(1)} %select_reduce_fusion.table_ref, s32[2]{0:T(128)S(1)} %get-tuple-element.65.info_ref, ...), custom_call_target="tpu_custom_call" | custom-call | flops 2281701376 | bytes 17825792 | tf_op jit(solution)/shard_map/pallas_call | solution.py:108
  37.0 3.8 %collective-permute-start.3 = (bf16[4,272,512]{2,1,0:T(8,128)(2,1)}, bf16[4,272,512]{2,1,0:T(8,128)(2,1)S(1)}, u32[]{:S(2)}, u32[]{:S(2)}) collective-permute-start(bf16[4,272,512]{2,1,0:T(8,128)(2,1)} %get-tuple-element.36), channel_id=1, source_target_pairs={{0,32},{8,40},{16,48},{24,56},{32,64},{40,72},{48,80},{56,88},{64,... | collective-permute-start | bytes 3342344 | tf_op jit(solution)/shard_map/ppermute | solution.py:406
  40.8 2.3 collective-permute-start.4
  43.3 8.2 %collective-permute-done.1 = bf16[4,272,512]{2,1,0:T(8,128)(2,1)} collective-permute-done((bf16[4,272,512]{2,1,0:T(8,128)(2,1)}, bf16[4,272,512]{2,1,0:T(8,128)(2,1)}, u32[]{:S(2)}, u32[]{:S(2)}) %collective-permute-start.1) | collective-permute-done | bytes 1114144 | tf_op jit(solution)/shard_map/ppermute | solution.py:406
  52.8 3.9 %shard_map.138 = (bf16[2,272,512]{2,1,0:T(8,128)(2,1)}, bf16[2,272,512]{2,1,0:T(8,128)(2,1)}) custom-call(s32[2]{0:T(128)S(1)} %rev.3.place_ref, bf16[2,2,272,512]{3,2,1,0:T(8,128)(2,1)S(1)} %bitcast.94, bf16[2,2,272,512]{3,2,1,0:T(8,128)(2,1)} %bitcast.5.ahead, bf16[2,2,272,512]{3,2,1,0:T(8,128)(2,1)} %bitcast.6.behind), custom_call_target="tpu_custom_call" | custom-call | flops 2228224 | bytes 3342336 | tf_op jit(solution)/shard_map/pallas_call | solution.py:199
  57.8 6.4 %all-to-all-start = ((bf16[8,512,128]{2,1,0:T(8,128)(2,1)}), bf16[8,512,128]{2,1,0:T(8,128)(2,1)}, u32[]{:S(2)}, u32[]{:S(2)}) async-start(bf16[8,512,128]{2,1,0:T(8,128)(2,1)} %broadcast_in_dim.23), calls=%async_computation | async-start | bytes 2097152 | tf_op jit(solution)/shard_map/all_to_all | solution.py:423
  68.9 2.8 %shard_map.139 = (bf16[2,272,512]{2,1,0:T(8,128)(2,1)}, bf16[2,272,512]{2,1,0:T(8,128)(2,1)}) custom-call(s32[2]{0:T(128)S(1)} %pad_add_fusion.2.place_ref, bf16[2,2,272,512]{3,2,1,0:T(8,128)(2,1)S(1)} %bitcast.93, bf16[2,2,272,512]{3,2,1,0:T(8,128)(2,1)S(1)} %bitcast.87, bf16[2,2,272,512]{3,2,1,0:T(8,128)(2,1)S(1)} %bitcast.89), custom_call_target="tpu_custom_call" | custom-call | flops 2228224 | bytes 3342336 | tf_op jit(solution)/shard_map/pallas_call | solution.py:199
  74.6 5.3 %collective-permute-done.10.passed_f = bf16[2,272,512]{2,1,0:T(8,128)(2,1)S(1)} collective-permute-done((bf16[2,272,512]{2,1,0:T(8,128)(2,1)}, bf16[2,272,512]{2,1,0:T(8,128)(2,1)S(1)}, u32[]{:S(2)}, u32[]{:S(2)}) %collective-permute-start.10) | collective-permute-done | bytes 557088 | tf_op jit(solution)/shard_map/ppermute | solution.py:406
  79.9 5.4 %shard_map.142 = (bf16[2,2,80,512]{3,2,1,0:T(8,128)(2,1)S(1)}, bf16[2,2,80,512]{3,2,1,0:T(8,128)(2,1)}, bf16[2,2,80,512]{3,2,1,0:T(8,128)(2,1)}, bf16[2,2,80,512]{3,2,1,0:T(8,128)(2,1)}) custom-call(s32[2]{0:T(128)S(1)} %rev.3.place_ref, bf16[2,2,272,512]{3,2,1,0:T(8,128)(2,1)S(1)} %bitcast.92, bf16[2,2,272,512]{3,2,1,0:T(8,128)(2,1)} %bitcast.5.ahead, ...), custom_call_target="tpu_custom_call" | custom-call | flops 3342336 | bytes 4456448 | tf_op jit(solution)/shard_map/pallas_call | solution.py:266
  85.3 2.0 collective-permute-start.12
  87.3 3.2 %collective-permute-start.13 = (bf16[4,80,512]{2,1,0:T(8,128)(2,1)}, bf16[4,80,512]{2,1,0:T(8,128)(2,1)}, u32[]{:S(2)}, u32[]{:S(2)}) collective-permute-start(bf16[4,80,512]{2,1,0:T(8,128)(2,1)} %bitcast.21), channel_id=1, source_target_pairs={{0,64},{8,72},{16,80},{24,88},{32,96},{40,104},{48,112},{56,120},{... | collective-permute-start | bytes 983048 | tf_op jit(solution)/shard_map/ppermute | solution.py:439
  93.8 5.2 %shard_map.140 = (bf16[2,2,80,512]{3,2,1,0:T(8,128)(2,1)S(1)}, bf16[2,2,80,512]{3,2,1,0:T(8,128)(2,1)}, bf16[2,2,80,512]{3,2,1,0:T(8,128)(2,1)}, bf16[2,2,80,512]{3,2,1,0:T(8,128)(2,1)}) custom-call(s32[2]{0:T(128)S(1)} %pad_add_fusion.2.place_ref, bf16[2,2,272,512]{3,2,1,0:T(8,128)(2,1)S(1)} %bitcast.91, bf16[2,2,272,512]{3,2,1,0:T(8,128)(2,1)S(1)} %bitcast.88, ...), custom_call_target="tpu_custom_call" | custom-call | flops 3342336 | bytes 4456448 | tf_op jit(solution)/shard_map/pallas_call | solution.py:266
  100.4 2.9 %collective-permute-start.8 = (bf16[4,80,512]{2,1,0:T(8,128)(2,1)}, bf16[4,80,512]{2,1,0:T(8,128)(2,1)S(1)}, u32[]{:S(2)}, u32[]{:S(2)}) collective-permute-start(bf16[4,80,512]{2,1,0:T(8,128)(2,1)} %bitcast.16), channel_id=1, source_target_pairs={{0,16},{8,24},{16,0},{24,8},{32,48},{40,56},{48,32},{56,40},{64,80... | collective-permute-start | bytes 983048 | tf_op jit(solution)/shard_map/ppermute | solution.py:438
  104.9 4.0 %shard_map.143 = bf16[4,64,512]{2,1,0:T(8,128)(2,1)S(1)} custom-call(s32[2]{0:T(128)S(1)} %pad_add_fusion.2.place_ref, bf16[4,80,512]{2,1,0:T(8,128)(2,1)S(1)} %bitcast.95, bf16[4,80,512]{2,1,0:T(8,128)(2,1)} %collective-permute-done.12.refs_1_, bf16[4,80,512]{2,1,0:T(8,128)(2,1)} %collective-permute-done.13.refs_2_, ...), custom_call_target="tpu_custom_call" | custom-call | flops 1310720 | bytes 1638400 | tf_op jit(solution)/shard_map/pallas_call | solution.py:310
  108.9 7.5 %collective-permute-done.8.refs_2_ = bf16[4,80,512]{2,1,0:T(8,128)(2,1)S(1)} collective-permute-done((bf16[4,80,512]{2,1,0:T(8,128)(2,1)}, bf16[4,80,512]{2,1,0:T(8,128)(2,1)S(1)}, u32[]{:S(2)}, u32[]{:S(2)}) %collective-permute-start.8) | collective-permute-done | bytes 327712 | tf_op jit(solution)/shard_map/ppermute | solution.py:438
  118.3 2.5 shard_map.141
  126.3 4.6 %convolution_convert_fusion.1 = bf16[64,7168]{1,0:T(8,128)(2,1)S(1)} fusion(bf16[512,7168]{1,0:T(8,128)(2,1)} %all-gather.2.cloned.1.call-done, bf16[8,8,4,128]{3,2,1,0:T(4,128)(2,1)S(1)} %bitcast.112), kind=kOutput, calls=%fused_computation.1 | convolution fusion | flops 470220800 | bytes 8323072 | tf_op jit(solution)/shard_map/dot_general | solution.py:455
  131.3 3.0 %collective-permute-start = (bf16[4,7168]{1,0:T(4,128)(2,1)S(1)}, bf16[4,7168]{1,0:T(4,128)(2,1)S(1)}, u32[]{:S(2)}, u32[]{:S(2)}) collective-permute-start(bf16[4,7168]{1,0:T(4,128)(2,1)S(1)} %copy-done.21), channel_id=1, source_target_pairs={{0,0},{1,8},{2,16},{3,24},{4,32},{5,40},{6,48},{7,56},{8,64},{9,72... | collective-permute-start | bytes 172040 | tf_op jit(solution)/shard_map/ppermute | solution.py:374
  134.4 6.2 %collective-permute-start.18 = (s32[4,16]{1,0:T(4,128)S(1)}, s32[4,16]{1,0:T(4,128)S(1)}, u32[]{:S(2)}, u32[]{:S(2)}) collective-permute-start(s32[4,16]{1,0:T(4,128)S(1)} %pad_add_fusion), channel_id=1, source_target_pairs={{0,0},{1,8},{2,16},{3,24},{4,32},{5,40},{6,48},{7,56},{8,64},{9,72... | collective-permute-start | bytes 776 | tf_op jit(solution)/shard_map/ppermute | solution.py:374
  143.4 6.6 %all-to-all-start.1 = ((bf16[16,4,7168]{2,1,0:T(4,128)(2,1)}), bf16[16,4,7168]{2,1,0:T(4,128)(2,1)S(1)}, u32[]{:S(2)}, u32[]{:S(2)}) async-start(bf16[16,4,7168]{2,1,0:T(4,128)(2,1)} %reshape.169), calls=%async_computation.1 | async-start | bytes 1835008 | tf_op jit(solution)/shard_map/all_to_all | solution.py:464
  150.2 18.1 %all-to-all-done.1 = bf16[16,4,7168]{2,1,0:T(4,128)(2,1)S(1)} async-done(((bf16[16,4,7168]{2,1,0:T(4,128)(2,1)}), bf16[16,4,7168]{2,1,0:T(4,128)(2,1)S(1)}, u32[]{:S(2)}, u32[]{:S(2)}) %all-to-all-start.1) | async-done | bytes 917536 | tf_op jit(solution)/shard_map/all_to_all | solution.py:464
  170.2 31.2 %all_to_all.20 = bf16[128,8,896]{2,1,0:T(8,128)(2,1)S(1)} all-to-all(bf16[128,8,896]{2,1,0:T(8,128)(2,1)S(1)} %bitcast.104), channel_id=1, replica_groups=mesh['ctx'=16,'ep'=8] {'ctx','ep'}, dimensions={0} | all-to-all | bytes 3670016 | tf_op jit(solution)/shard_map/all_to_all | solution.py:501
  202.8 3.3 %collective-permute-done.20 = bf16[128,7168]{1,0:T(8,128)(2,1)S(1)} collective-permute-done((bf16[128,7168]{1,0:T(8,128)(2,1)S(1)}, bf16[128,7168]{1,0:T(8,128)(2,1)S(1)}, u32[]{:S(2)}, u32[]{:S(2)}) %collective-permute-start.20) | collective-permute-done | bytes 1835040 | tf_op jit(solution)/shard_map/ppermute | solution.py:503
  211.4 3.4 %collective-permute-done.21 = bf16[128,7168]{1,0:T(8,128)(2,1)S(1)} collective-permute-done((bf16[128,7168]{1,0:T(8,128)(2,1)S(1)}, bf16[128,7168]{1,0:T(8,128)(2,1)S(1)}, u32[]{:S(2)}, u32[]{:S(2)}) %collective-permute-start.21) | collective-permute-done | bytes 1835040 | tf_op jit(solution)/shard_map/ppermute | solution.py:509
  217.0 3.8 %all-to-all-start.3 = ((bf16[128,8,896]{2,1,0:T(8,128)(2,1)}), bf16[128,8,896]{2,1,0:T(8,128)(2,1)S(1)}, u32[]{:S(2)}, u32[]{:S(2)}) async-start(bf16[128,8,896]{2,1,0:T(8,128)(2,1)} %bitcast.38), calls=%async_computation.3 | async-start | bytes 3670016 | tf_op jit(solution)/shard_map/all_to_all | solution.py:513
  220.9 5.2 %collective-permute-start.19 = (f32[4,32]{0,1:T(8,128)S(1)}, f32[4,32]{0,1:T(8,128)S(1)}, u32[]{:S(2)}, u32[]{:S(2)}) collective-permute-start(f32[4,32]{0,1:T(8,128)S(1)} %bitcast.119), channel_id=1, source_target_pairs={{0,0},{8,1},{16,2},{24,3},{32,4},{40,5},{48,6},{56,7},{64,8},{72,9... | collective-permute-start | bytes 1544 | tf_op jit(solution)/shard_map/ppermute | solution.py:489
  226.1 3.3 %collective-permute-start.17 = (bf16[4,7168]{1,0:T(4,128)(2,1)S(1)}, bf16[4,7168]{1,0:T(4,128)(2,1)S(1)}, u32[]{:S(2)}, u32[]{:S(2)}) collective-permute-start(bf16[4,7168]{1,0:T(4,128)(2,1)S(1)} %get-tuple-element.56), channel_id=1, source_target_pairs={{0,0},{8,1},{16,2},{24,3},{32,4},{40,5},{48,6},{56,7},{64,8},{72,9... | collective-permute-start | bytes 172040 | tf_op jit(solution)/shard_map/ppermute | solution.py:492
  229.4 8.3 %collective-permute-done.19 = f32[4,32]{0,1:T(8,128)S(1)} collective-permute-done((f32[4,32]{0,1:T(8,128)S(1)}, f32[4,32]{0,1:T(8,128)S(1)}, u32[]{:S(2)}, u32[]{:S(2)}) %collective-permute-start.19) | collective-permute-done | bytes 544 | tf_op jit(solution)/shard_map/ppermute | solution.py:489
  237.8 10.9 %all-to-all-done.3 = bf16[128,8,896]{2,1,0:T(8,128)(2,1)S(1)} async-done(((bf16[128,8,896]{2,1,0:T(8,128)(2,1)}), bf16[128,8,896]{2,1,0:T(8,128)(2,1)S(1)}, u32[]{:S(2)}, u32[]{:S(2)}) %all-to-all-start.3) | async-done | bytes 1835040 | tf_op jit(solution)/shard_map/all_to_all | solution.py:513
  (129 shorter events, 45.2 us)
Async XLA Ops:
  6.5 162.4 %copy-start = (bf16[7168,16]{0,1:T(8,128)(2,1)S(1)}, bf16[7168,16]{0,1:T(8,128)(2,1)}, u32[]{:S(2)}) copy-start(bf16[7168,16]{0,1:T(8,128)(2,1)} %param.22) | copy-start | bytes 688132
  6.5 119.7 %all-gather.2.cloned.1.call-start = ((), (), s32[]{:S(2)}) async-start(), calls=%async_computation.4 | async-start | bytes 9175040 | tf_op jit(solution)/shard_map/all_gather | solution.py:360
  24.1 10.8 %copy-start.3 = (bf16[4,272,512]{2,1,0:T(8,128)(2,1)}, bf16[4,272,512]{2,1,0:T(8,128)(2,1)S(1)}, u32[]{:S(2)}) copy-start(bf16[4,272,512]{2,1,0:T(8,128)(2,1)S(1)} %get-tuple-element.45) | copy-start | bytes 3342340
  24.1 27.4 %collective-permute-start.1 = (bf16[4,272,512]{2,1,0:T(8,128)(2,1)}, bf16[4,272,512]{2,1,0:T(8,128)(2,1)}, u32[]{:S(2)}, u32[]{:S(2)}) collective-permute-start(bf16[4,272,512]{2,1,0:T(8,128)(2,1)} %get-tuple-element.30), channel_id=1, source_target_pairs={{0,8},{8,16},{16,24},{24,0},{32,40},{40,48},{48,56},{56,32},{64,72... | collective-permute-start | bytes 3342344 | tf_op jit(solution)/shard_map/ppermute | solution.py:406
  24.1 27.4 %collective-permute-start.2 = (bf16[4,272,512]{2,1,0:T(8,128)(2,1)}, bf16[4,272,512]{2,1,0:T(8,128)(2,1)}, u32[]{:S(2)}, u32[]{:S(2)}) collective-permute-start(bf16[4,272,512]{2,1,0:T(8,128)(2,1)} %get-tuple-element.31), channel_id=1, source_target_pairs={{0,24},{8,0},{16,8},{24,16},{32,56},{40,32},{48,40},{56,48},{64,88... | collective-permute-start | bytes 3342344 | tf_op jit(solution)/shard_map/ppermute | solution.py:406
  26.8 29.9 %copy-start.13 = (bf16[1,512,128]{2,1,0:T(8,128)(2,1)S(1)}, bf16[1,512,128]{2,1,0:T(8,128)(2,1)}, u32[]{:S(2)}) copy-start(bf16[1,512,128]{2,1,0:T(8,128)(2,1)} %param.18) | copy-start | bytes 393220
  37.0 30.6 %collective-permute-start.3 = (bf16[4,272,512]{2,1,0:T(8,128)(2,1)}, bf16[4,272,512]{2,1,0:T(8,128)(2,1)S(1)}, u32[]{:S(2)}, u32[]{:S(2)}) collective-permute-start(bf16[4,272,512]{2,1,0:T(8,128)(2,1)} %get-tuple-element.36), channel_id=1, source_target_pairs={{0,32},{8,40},{16,48},{24,56},{32,64},{40,72},{48,80},{56,88},{64,... | collective-permute-start | bytes 3342344 | tf_op jit(solution)/shard_map/ppermute | solution.py:406
  40.8 26.8 %collective-permute-start.4 = (bf16[4,272,512]{2,1,0:T(8,128)(2,1)}, bf16[4,272,512]{2,1,0:T(8,128)(2,1)S(1)}, u32[]{:S(2)}, u32[]{:S(2)}) collective-permute-start(bf16[4,272,512]{2,1,0:T(8,128)(2,1)} %get-tuple-element.37), channel_id=1, source_target_pairs={{0,96},{8,104},{16,112},{24,120},{32,0},{40,8},{48,16},{56,24},{64... | collective-permute-start | bytes 3342344 | tf_op jit(solution)/shard_map/ppermute | solution.py:406
  57.8 34.7 %all-to-all-start = ((bf16[8,512,128]{2,1,0:T(8,128)(2,1)}), bf16[8,512,128]{2,1,0:T(8,128)(2,1)}, u32[]{:S(2)}, u32[]{:S(2)}) async-start(bf16[8,512,128]{2,1,0:T(8,128)(2,1)} %broadcast_in_dim.23), calls=%async_computation | async-start | bytes 2097152 | tf_op jit(solution)/shard_map/all_to_all | solution.py:423
  64.2 15.7 %copy-start.4 = (bf16[4,272,512]{2,1,0:T(8,128)(2,1)S(1)}, bf16[4,272,512]{2,1,0:T(8,128)(2,1)}, u32[]{:S(2)}) copy-start(bf16[4,272,512]{2,1,0:T(8,128)(2,1)} %copy-done.3) | copy-start | bytes 3342340
  64.2 15.7 %collective-permute-start.10 = (bf16[2,272,512]{2,1,0:T(8,128)(2,1)}, bf16[2,272,512]{2,1,0:T(8,128)(2,1)S(1)}, u32[]{:S(2)}, u32[]{:S(2)}) collective-permute-start(bf16[2,272,512]{2,1,0:T(8,128)(2,1)} %get-tuple-element.32), channel_id=1, source_target_pairs={{0,8},{8,16},{16,24},{24,0},{32,40},{40,48},{48,56},{56,32},{64,72... | collective-permute-start | bytes 1671176 | tf_op jit(solution)/shard_map/ppermute | solution.py:406
  65.7 14.3 %collective-permute-start.11 = (bf16[2,272,512]{2,1,0:T(8,128)(2,1)}, bf16[2,272,512]{2,1,0:T(8,128)(2,1)S(1)}, u32[]{:S(2)}, u32[]{:S(2)}) collective-permute-start(bf16[2,272,512]{2,1,0:T(8,128)(2,1)} %get-tuple-element.46), channel_id=1, source_target_pairs={{0,24},{8,0},{16,8},{24,16},{32,56},{40,32},{48,40},{56,48},{64,88... | collective-permute-start | bytes 1671176 | tf_op jit(solution)/shard_map/ppermute | solution.py:406
  71.7 20.8 %collective-permute-start.5 = (bf16[2,272,512]{2,1,0:T(8,128)(2,1)}, bf16[2,272,512]{2,1,0:T(8,128)(2,1)S(1)}, u32[]{:S(2)}, u32[]{:S(2)}) collective-permute-start(bf16[2,272,512]{2,1,0:T(8,128)(2,1)} %get-tuple-element.39), channel_id=1, source_target_pairs={{0,32},{8,40},{16,48},{24,56},{32,64},{40,72},{48,80},{56,88},{64,... | collective-permute-start | bytes 1671176 | tf_op jit(solution)/shard_map/ppermute | solution.py:406
  73.0 19.5 %collective-permute-start.6 = (bf16[2,272,512]{2,1,0:T(8,128)(2,1)}, bf16[2,272,512]{2,1,0:T(8,128)(2,1)}, u32[]{:S(2)}, u32[]{:S(2)}) collective-permute-start(bf16[2,272,512]{2,1,0:T(8,128)(2,1)} %get-tuple-element.40), channel_id=1, source_target_pairs={{0,96},{8,104},{16,112},{24,120},{32,0},{40,8},{48,16},{56,24},{64... | collective-permute-start | bytes 1671176 | tf_op jit(solution)/shard_map/ppermute | solution.py:406
  85.3 18.0 %collective-permute-start.12 = (bf16[4,80,512]{2,1,0:T(8,128)(2,1)}, bf16[4,80,512]{2,1,0:T(8,128)(2,1)}, u32[]{:S(2)}, u32[]{:S(2)}) collective-permute-start(bf16[4,80,512]{2,1,0:T(8,128)(2,1)} %bitcast.20), channel_id=1, source_target_pairs={{0,32},{8,40},{16,48},{24,56},{32,64},{40,72},{48,80},{56,88},{64,... | collective-permute-start | bytes 983048 | tf_op jit(solution)/shard_map/ppermute | solution.py:439
  87.3 17.5 %collective-permute-start.13 = (bf16[4,80,512]{2,1,0:T(8,128)(2,1)}, bf16[4,80,512]{2,1,0:T(8,128)(2,1)}, u32[]{:S(2)}, u32[]{:S(2)}) collective-permute-start(bf16[4,80,512]{2,1,0:T(8,128)(2,1)} %bitcast.21), channel_id=1, source_target_pairs={{0,64},{8,72},{16,80},{24,88},{32,96},{40,104},{48,112},{56,120},{... | collective-permute-start | bytes 983048 | tf_op jit(solution)/shard_map/ppermute | solution.py:439
  90.5 14.4 %collective-permute-start.14 = (bf16[4,80,512]{2,1,0:T(8,128)(2,1)}, bf16[4,80,512]{2,1,0:T(8,128)(2,1)}, u32[]{:S(2)}, u32[]{:S(2)}) collective-permute-start(bf16[4,80,512]{2,1,0:T(8,128)(2,1)} %bitcast.22), channel_id=1, source_target_pairs={{0,96},{8,104},{16,112},{24,120},{32,0},{40,8},{48,16},{56,24},{64... | collective-permute-start | bytes 983048 | tf_op jit(solution)/shard_map/ppermute | solution.py:439
  99.6 9.2 %collective-permute-start.7 = (bf16[4,80,512]{2,1,0:T(8,128)(2,1)}, bf16[4,80,512]{2,1,0:T(8,128)(2,1)S(1)}, u32[]{:S(2)}, u32[]{:S(2)}) collective-permute-start(bf16[4,80,512]{2,1,0:T(8,128)(2,1)} %bitcast.15), channel_id=1, source_target_pairs={{0,8},{8,16},{16,24},{24,0},{32,40},{40,48},{48,56},{56,32},{64,72... | collective-permute-start | bytes 983048 | tf_op jit(solution)/shard_map/ppermute | solution.py:438
  100.4 16.0 %collective-permute-start.8 = (bf16[4,80,512]{2,1,0:T(8,128)(2,1)}, bf16[4,80,512]{2,1,0:T(8,128)(2,1)S(1)}, u32[]{:S(2)}, u32[]{:S(2)}) collective-permute-start(bf16[4,80,512]{2,1,0:T(8,128)(2,1)} %bitcast.16), channel_id=1, source_target_pairs={{0,16},{8,24},{16,0},{24,8},{32,48},{40,56},{48,32},{56,40},{64,80... | collective-permute-start | bytes 983048 | tf_op jit(solution)/shard_map/ppermute | solution.py:438
  103.3 14.1 %collective-permute-start.9 = (bf16[4,80,512]{2,1,0:T(8,128)(2,1)}, bf16[4,80,512]{2,1,0:T(8,128)(2,1)S(1)}, u32[]{:S(2)}, u32[]{:S(2)}) collective-permute-start(bf16[4,80,512]{2,1,0:T(8,128)(2,1)} %bitcast.17), channel_id=1, source_target_pairs={{0,24},{8,0},{16,8},{24,16},{32,56},{40,32},{48,40},{56,48},{64,88... | collective-permute-start | bytes 983048 | tf_op jit(solution)/shard_map/ppermute | solution.py:438
  123.3 2.8 %collective-permute-start.15 = (bf16[64,4,128]{2,0,1:T(8,128)(2,1)S(1)}, bf16[64,4,128]{2,0,1:T(8,128)(2,1)S(1)}, u32[]{:S(2)}, u32[]{:S(2)}) collective-permute-start(bf16[64,4,128]{2,0,1:T(8,128)(2,1)S(1)} %bitcast.115), channel_id=1, source_target_pairs={{0,1},{1,0},{2,3},{3,2},{4,5},{5,4},{6,7},{7,6},{8,9},{9,8},{10,11... | collective-permute-start | bytes 196616 | tf_op jit(solution)/shard_map/ppermute | solution.py:453
  126.2 14.5 %copy-start.11 = (bf16[512,7168]{1,0:T(8,128)(2,1)S(1)}, bf16[512,7168]{1,0:T(8,128)(2,1)}, u32[]{:S(2)}) copy-start(bf16[512,7168]{1,0:T(8,128)(2,1)} %all-gather.2.cloned.1.call-done) | copy-start | bytes 22020100
  130.9 9.8 %collective-permute-start.16 = (bf16[64,7168]{1,0:T(8,128)(2,1)S(1)}, bf16[64,7168]{1,0:T(8,128)(2,1)S(1)}, u32[]{:S(2)}, u32[]{:S(2)}) collective-permute-start(bf16[64,7168]{1,0:T(8,128)(2,1)S(1)} %convolution_convert_fusion.1), channel_id=1, source_target_pairs={{0,1},{1,0},{2,3},{3,2},{4,5},{5,4},{6,7},{7,6},{8,9},{9,8},{10,11... | collective-permute-start | bytes 2752520 | tf_op jit(solution)/shard_map/ppermute | solution.py:458
  131.3 37.4 %collective-permute-start = (bf16[4,7168]{1,0:T(4,128)(2,1)S(1)}, bf16[4,7168]{1,0:T(4,128)(2,1)S(1)}, u32[]{:S(2)}, u32[]{:S(2)}) collective-permute-start(bf16[4,7168]{1,0:T(4,128)(2,1)S(1)} %copy-done.21), channel_id=1, source_target_pairs={{0,0},{1,8},{2,16},{3,24},{4,32},{5,40},{6,48},{7,56},{8,64},{9,72... | collective-permute-start | bytes 172040 | tf_op jit(solution)/shard_map/ppermute | solution.py:374
  134.4 15.6 %collective-permute-start.18 = (s32[4,16]{1,0:T(4,128)S(1)}, s32[4,16]{1,0:T(4,128)S(1)}, u32[]{:S(2)}, u32[]{:S(2)}) collective-permute-start(s32[4,16]{1,0:T(4,128)S(1)} %pad_add_fusion), channel_id=1, source_target_pairs={{0,0},{1,8},{2,16},{3,24},{4,32},{5,40},{6,48},{7,56},{8,64},{9,72... | collective-permute-start | bytes 776 | tf_op jit(solution)/shard_map/ppermute | solution.py:374
  142.1 26.8 %copy-start.16 = (f32[7168]{0:T(1024)S(1)}, f32[7168]{0:T(1024)}, u32[]{:S(2)}) copy-start(f32[7168]{0:T(1024)} %param.21) | copy-start | bytes 86020
  143.4 24.9 %all-to-all-start.1 = ((bf16[16,4,7168]{2,1,0:T(4,128)(2,1)}), bf16[16,4,7168]{2,1,0:T(4,128)(2,1)S(1)}, u32[]{:S(2)}, u32[]{:S(2)}) async-start(bf16[16,4,7168]{2,1,0:T(4,128)(2,1)} %reshape.169), calls=%async_computation.1 | async-start | bytes 1835008 | tf_op jit(solution)/shard_map/all_to_all | solution.py:464
  201.7 4.4 %collective-permute-start.20 = (bf16[128,7168]{1,0:T(8,128)(2,1)S(1)}, bf16[128,7168]{1,0:T(8,128)(2,1)S(1)}, u32[]{:S(2)}, u32[]{:S(2)}) collective-permute-start(bf16[128,7168]{1,0:T(8,128)(2,1)S(1)} %bitcast.100), channel_id=1, source_target_pairs={{0,1},{1,0},{2,3},{3,2},{4,5},{5,4},{6,7},{7,6},{8,9},{9,8},{10,11... | collective-permute-start | bytes 5505032 | tf_op jit(solution)/shard_map/ppermute | solution.py:503
  210.9 3.9 %collective-permute-start.21 = (bf16[128,7168]{1,0:T(8,128)(2,1)S(1)}, bf16[128,7168]{1,0:T(8,128)(2,1)S(1)}, u32[]{:S(2)}, u32[]{:S(2)}) collective-permute-start(bf16[128,7168]{1,0:T(8,128)(2,1)S(1)} %convolution_convert_fusion), channel_id=1, source_target_pairs={{0,1},{1,0},{2,3},{3,2},{4,5},{5,4},{6,7},{7,6},{8,9},{9,8},{10,11... | collective-permute-start | bytes 5505032 | tf_op jit(solution)/shard_map/ppermute | solution.py:509
  217.0 31.7 %all-to-all-start.3 = ((bf16[128,8,896]{2,1,0:T(8,128)(2,1)}), bf16[128,8,896]{2,1,0:T(8,128)(2,1)S(1)}, u32[]{:S(2)}, u32[]{:S(2)}) async-start(bf16[128,8,896]{2,1,0:T(8,128)(2,1)} %bitcast.38), calls=%async_computation.3 | async-start | bytes 3670016 | tf_op jit(solution)/shard_map/all_to_all | solution.py:513
  220.9 16.7 %collective-permute-start.19 = (f32[4,32]{0,1:T(8,128)S(1)}, f32[4,32]{0,1:T(8,128)S(1)}, u32[]{:S(2)}, u32[]{:S(2)}) collective-permute-start(f32[4,32]{0,1:T(8,128)S(1)} %bitcast.119), channel_id=1, source_target_pairs={{0,0},{8,1},{16,2},{24,3},{32,4},{40,5},{48,6},{56,7},{64,8},{72,9... | collective-permute-start | bytes 1544 | tf_op jit(solution)/shard_map/ppermute | solution.py:489
  226.1 23.3 %collective-permute-start.17 = (bf16[4,7168]{1,0:T(4,128)(2,1)S(1)}, bf16[4,7168]{1,0:T(4,128)(2,1)S(1)}, u32[]{:S(2)}, u32[]{:S(2)}) collective-permute-start(bf16[4,7168]{1,0:T(4,128)(2,1)S(1)} %get-tuple-element.56), channel_id=1, source_target_pairs={{0,0},{8,1},{16,2},{24,3},{32,4},{40,5},{48,6},{56,7},{64,8},{72,9... | collective-permute-start | bytes 172040 | tf_op jit(solution)/shard_map/ppermute | solution.py:492
  (16 other events, 48.5 us)
Sparse Core Ops, SparseCore 0:
  9.0 88.7 all-gather.1
